TPU v7x, 256 devices: a whole 4x4x8 slice. The times are simulated.
256 devices in a mesh: head: 4 (over y_hi, core), seq: 32 (over z, x), mp: 2 (over y_lo).
Axes of the slice: x: 4, y: 4 (y_hi: 2, y_lo: 2; y = y_hi * 2 + y_lo), z: 8, core: 2. Of those that a mesh axis runs over, the one named last changes fastest.
Arguments:
- hidden_states: bfloat16 [12288, 2048], P('seq', ('head', 'mp'))
- norm_gain: bfloat16 [4, 2048], P('head'), may hold values from 0.25 to 1.75
- qkv_weight: bfloat16 [4, 2048, 3, 1024], P('head', 'seq', None, 'mp')
- out_weight: bfloat16 [4, 2048, 1024], P('head', 'seq', 'mp'), may hold values from -0.1875 to 0.1875
- cotangent: bfloat16 [4, 12288, 2048], P('head', 'seq'), may hold values from -1.5 to 1.5
- segment_ids: int32 [12288], replicated, may hold values from 0 to 63, as said below
Outputs:
- trunk_grad: bfloat16 [12288, 2048], P('seq', ('head', 'mp'))
- qkv_grad: bfloat16 [4, 2048, 3, 1024], P('head', 'seq', None, 'mp')
- out_grad: bfloat16 [4, 2048, 1024], P('head', 'seq', 'mp')
Inputs may be any that keep to these rules, and one draw needn't show every extreme that they name: `segment_ids`: numbers never fall along the window; each document holds 1 to 384 positions and some document holds exactly 384.
All inputs are finite; a program needn't handle non-finite values.
Results may differ from a plain program's by a relative error of at most 0.022.
Values may be sent and summed in bfloat16 or wider, within the bound.
A program may use at most 128 MiB of HBM per device.

v0:
```python
import jax
import jax.numpy as jnp
from jax import lax
from jax.sharding import PartitionSpec as P

HD = 64


epsilon = 1e-05
masked_score = -1e30


def passed_along(value, axis, steps):
    count = lax.axis_size(axis)
    leading, last = (max(0, -steps), min(count, count - steps))
    return lax.ppermute(value, axis, [(source, source + steps) for source in range(leading, last)])


def block_mask(own_seg, earlier_seg):
    row_count = own_seg.shape[0]
    positions = jnp.arange(row_count)
    causal = positions[None, :] <= positions[:, None]
    own_ok = causal & (own_seg[None, :] == own_seg[:, None])
    prior_ok = earlier_seg[None, :] == own_seg[:, None]
    return jnp.concatenate([prior_ok, own_ok], axis=1)


def attend(queries, key_rows, value_rows, allowed, attn_grad):
    score_scale = HD ** (-0.5)
    scores = (
        jnp.einsum("qhd,khd->hqk", queries, key_rows, preferred_element_type=jnp.float32)
        * score_scale
    )
    scores = jnp.where(allowed[None], scores, masked_score)
    row_max = jnp.max(scores, axis=-1, keepdims=True)
    expo = jnp.exp(scores - row_max)
    probs = expo / jnp.sum(expo, axis=-1, keepdims=True)
    prob_rows = probs.astype(jnp.bfloat16)
    attn_out = jnp.einsum(
        "hqk,khd->qhd", prob_rows, value_rows, preferred_element_type=jnp.float32
    ).astype(jnp.bfloat16)
    prob_grad = jnp.einsum(
        "qhd,khd->hqk", attn_grad, value_rows, preferred_element_type=jnp.float32
    )
    row_delta = jnp.sum(probs * prob_grad, axis=-1, keepdims=True)
    score_grad = (probs * (prob_grad - row_delta) * score_scale).astype(jnp.bfloat16)
    query_grad = jnp.einsum(
        "hqk,khd->qhd", score_grad, key_rows, preferred_element_type=jnp.float32
    ).astype(jnp.bfloat16)
    key_grads = jnp.einsum("hqk,qhd->khd", score_grad, queries, preferred_element_type=jnp.float32)
    value_grads = jnp.einsum(
        "hqk,qhd->khd", prob_rows, attn_grad, preferred_element_type=jnp.float32
    )
    return (attn_out, query_grad, key_grads, value_grads)


def attend_groups(queries, key_rows, value_rows, allowed, attn_grad):
    local_attender_tally = queries.shape[1]
    group_count = 2
    width = local_attender_tally // group_count
    results = []
    for index in range(group_count):
        lower = index * width
        upper = lower + width
        results.append(
            attend(
                queries[:, lower:upper],
                key_rows[:, lower:upper],
                value_rows[:, lower:upper],
                allowed,
                attn_grad[:, lower:upper],
            )
        )
    return tuple(
        (jnp.concatenate([item[position] for item in results], axis=1) for position in range(4))
    )


def per_device(hidden_states, norm_gain, qkv_weight, out_weight, cotangent, segment_ids):
    gathered = lax.all_gather(hidden_states, ("head", "mp"), axis=1, tiled=True)
    row_count = gathered.shape[0]
    states = gathered.astype(jnp.float32)
    inverse = lax.rsqrt(jnp.mean(states * states, axis=-1, keepdims=True) + epsilon)
    unit_rows = states * inverse
    norm_scale = norm_gain[0].astype(jnp.float32)
    rescaled_hidden = (unit_rows * norm_scale).astype(jnp.bfloat16)
    triple_mapping_matrix, weight_out = (
        lax.all_gather(qkv_weight[0], "seq", axis=0, tiled=True),
        lax.all_gather(out_weight[0], "seq", axis=0, tiled=True),
    )
    inner_width = triple_mapping_matrix.shape[2]
    local_attender_tally = inner_width // HD
    mapped_triple = jnp.einsum(
        "gl,lru->gru", rescaled_hidden, triple_mapping_matrix, preferred_element_type=jnp.float32
    ).astype(jnp.bfloat16)
    carried = passed_along(jnp.stack([mapped_triple[:, 1], mapped_triple[:, 2]]), "seq", 1)
    device_index = lax.axis_index("seq")
    own_seg = lax.dynamic_slice_in_dim(segment_ids, device_index * row_count, row_count)
    earlier_seg = lax.dynamic_slice_in_dim(
        segment_ids, jnp.maximum(device_index - 1, 0) * row_count, row_count
    )
    earlier_seg = jnp.where(device_index > 0, earlier_seg, -1)
    allowed = block_mask(own_seg, earlier_seg)
    key_rows = jnp.concatenate([carried[0], mapped_triple[:, 1]], axis=0).reshape(
        2 * row_count, local_attender_tally, HD
    )
    value_rows = jnp.concatenate([carried[1], mapped_triple[:, 2]], axis=0).reshape(
        2 * row_count, local_attender_tally, HD
    )
    queries = mapped_triple[:, 0].reshape(row_count, local_attender_tally, HD)
    upstream = cotangent[0]
    attn_grad = jnp.einsum(
        "td,de->te", upstream, weight_out, preferred_element_type=jnp.float32
    ).astype(jnp.bfloat16)
    attn_out, query_grad, key_grads, value_grads = attend_groups(
        queries,
        key_rows,
        value_rows,
        allowed,
        attn_grad.reshape(row_count, local_attender_tally, HD),
    )
    key_grads = key_grads.reshape(2 * row_count, inner_width)
    value_grads = value_grads.reshape(2 * row_count, inner_width)
    returned = passed_along(
        jnp.stack([key_grads[:row_count], value_grads[:row_count]]).astype(jnp.bfloat16), "seq", -1
    ).astype(jnp.float32)
    key_total = (key_grads[row_count:] + returned[0]).astype(jnp.bfloat16)
    value_total = (value_grads[row_count:] + returned[1]).astype(jnp.bfloat16)
    triple_matrix_sensitivity = jnp.stack(
        [query_grad.reshape(row_count, inner_width), key_total, value_total], axis=1
    )
    attn_flat = attn_out.reshape(row_count, inner_width)
    columns = rescaled_hidden
    qkv_sum = lax.psum_scatter(
        jnp.einsum(
            "tc,tse->cse", columns, triple_matrix_sensitivity, preferred_element_type=jnp.float32
        ).astype(jnp.bfloat16),
        "seq",
        scatter_dimension=0,
        tiled=True,
    )
    columns = upstream
    out_sum = lax.psum_scatter(
        jnp.einsum("tc,te->ce", columns, attn_flat, preferred_element_type=jnp.float32).astype(
            jnp.bfloat16
        ),
        "seq",
        scatter_dimension=0,
        tiled=True,
    )
    rescaled_hidden_sensitivity = jnp.einsum(
        "byq,xyq->bx",
        triple_matrix_sensitivity,
        triple_mapping_matrix,
        preferred_element_type=jnp.float32,
    )
    scaled = rescaled_hidden_sensitivity * norm_scale
    state_grad = inverse * (
        scaled - unit_rows * jnp.mean(scaled * unit_rows, axis=-1, keepdims=True)
    )
    state_grad = state_grad + jnp.where(
        lax.axis_index("mp") == 0, upstream.astype(jnp.float32), 0.0
    )
    summed = lax.psum_scatter(
        state_grad.astype(jnp.bfloat16), ("head", "mp"), scatter_dimension=1, tiled=True
    )
    return (summed, qkv_sum[None], out_sum[None])


def solution(mesh):
    placed = (
        P("seq", ("head", "mp")),
        P("head", None),
        P("head", "seq", None, "mp"),
        P("head", "seq", "mp"),
        P("head", "seq", None),
        P(),
    )
    return jax.shard_map(
        per_device,
        mesh=mesh,
        in_specs=placed,
        out_specs=(P("seq", ("head", "mp")), P("head", "seq", None, "mp"), P("head", "seq", "mp")),
        check_vma=False,
    )
```

profile of v0, /device:TPU:4, one launch (start us, length us, event | category | flops | bytes accessed | tf_op | source)
XLA Modules:
  0.0 749.8 jit_solution(7948051286664341454)
XLA Ops:
  10.2 44.0 %all-gather.6.cloned.1.call-done = bf16[384,2048]{1,0:T(8,128)(2,1)} async-done(((bf16[384,256]{1,0:T(8,128)(2,1)}), bf16[384,2048]{1,0:T(8,128)(2,1)}) %all-gather.6.cloned.1.call-update) | async-done | bytes 1572880 | tf_op jit(solution)/shard_map/all_gather | solution.py:80
  54.1 1.8 fusion.25
  55.9 89.1 %all-gather.8.cloned.1.call-done = bf16[1,2048,3,512]{3,1,2,0:T(8,128)(2,1)} async-done(((bf16[1,64,3,512]{3,1,2,0:T(8,128)(2,1)}), bf16[1,2048,3,512]{3,1,2,0:T(8,128)(2,1)}) %all-gather.8.cloned.1.call-update) | async-done | bytes 6291472 | tf_op jit(solution)/shard_map/all_gather | solution.py:88
  145.0 5.9 fusion.52
  152.1 2.9 collective-permute-start
  156.9 65.8 %all-gather.10.cloned.1.call-done = bf16[1,2048,512]{2,1,0:T(8,128)(2,1)} async-done(((bf16[1,64,512]{2,1,0:T(8,128)(2,1)}), bf16[1,2048,512]{2,1,0:T(8,128)(2,1)}) %all-gather.10.cloned.1.call-update) | async-done | bytes 2097168 | tf_op jit(solution)/shard_map/all_gather | solution.py:89
  222.7 2.6 fusion.61
  229.1 4.1 fusion.114
  233.2 3.0 fusion.117
  236.5 6.2 fusion.143
  242.8 2.3 fusion.144
  246.4 1.6 fusion.93
  248.0 1.6 fusion.90
  253.5 2.6 fusion.28
  256.1 4.0 copy.52
  260.4 3.0 fusion.108
  263.4 12.3 %fusion.58 = f32[768,4,64]{0,2,1:T(8,128)S(1)} fusion(bf16[384,8,64]{0,2,1:T(8,128)(2,1)S(1)} %bitcast.111, f32[4,384,768]{2,1,0:T(8,128)} %fusion.108, f32[4,384,768]{2,1,0:T(8,128)} %copy-done.17, f32[4,384]{1,0:T(4,128)} %copy-done.19), kind=kOutput, calls=%fused_computation.59 | convolution fusion | flops 159254784 | bytes 10622976 | tf_op jit(solution)/shard_map/hqk,qhd->khd/dot_general | solution.py:50
  275.7 4.0 fusion.111
  279.6 15.0 %fusion.55 = f32[768,4,64]{0,2,1:T(8,128)S(1)} fusion(bf16[384,8,64]{0,2,1:T(8,128)(2,1)} %bitcast.109, f32[4,384,768]{2,1,0:T(8,128)} %fusion.111, f32[4,384,768]{2,1,0:T(8,128)} %copy-done.16, f32[4,384]{1,0:T(4,128)} %copy-done.18), kind=kOutput, calls=%fused_computation.58 | convolution fusion | flops 159254784 | bytes 10622976 | tf_op jit(solution)/shard_map/hqk,qhd->khd/dot_general | solution.py:50
  295.5 1.9 copy.43
  297.4 2.0 pad_maximum_fusion.6
  299.5 2.8 collective-permute-start.1
  302.2 15.6 %fusion.84 = bf16[384,4,64]{0,2,1:T(8,128)(2,1)} fusion(f32[4,384,768]{2,1,0:T(8,128)} %fusion.108, bf16[384,8,64]{0,2,1:T(8,128)(2,1)} %bitcast.98, bf16[384,8,64]{0,2,1:T(8,128)(2,1)} %bitcast.102, f32[4,384,768]{2,1,0:T(8,128)} %copy-done.17, f32[4,384]{1,0:T(4,128)} %copy-done.19), kind=kOutput, calls=%fused_computation.75 | convolution fusion | flops 160925952 | bytes 10426368 | tf_op jit(solution)/shard_map/hqk,khd->qhd/dot_general | solution.py:47
  317.8 15.5 %fusion.87 = bf16[384,4,64]{0,2,1:T(8,128)(2,1)} fusion(f32[4,384,768]{2,1,0:T(8,128)} %fusion.111, bf16[384,8,64]{0,2,1:T(8,128)(2,1)S(1)} %bitcast.99, bf16[384,8,64]{0,2,1:T(8,128)(2,1)} %bitcast.103, f32[4,384,768]{2,1,0:T(8,128)} %copy-done.16, f32[4,384]{1,0:T(4,128)} %copy-done.18), kind=kOutput, calls=%fused_computation.76 | convolution fusion | flops 160925952 | bytes 10426368 | tf_op jit(solution)/shard_map/hqk,khd->qhd/dot_general | solution.py:47
  337.3 1.3 convert_element_type.101
  338.6 1.4 fusion.104
  340.1 5.1 fusion.20
  345.2 2.2 fusion.24
  347.5 5.5 convolution_convert_fusion
  353.0 121.7 %reduce-scatter.10.cloned.1.call-done = bf16[64,512]{1,0:T(8,128)(2,1)} async-done(((bf16[2048,512]{1,0:T(8,128)(2,1)}), bf16[64,512]{1,0:T(8,128)(2,1)}) %reduce-scatter.10.cloned.1.call-update) | async-done | bytes 65552
  476.5 38.3 %reduce-scatter.6.cloned.1.call-done = bf16[384,256]{1,0:T(8,128)(2,1)} async-done(((bf16[384,2048]{1,0:T(8,128)(2,1)}), bf16[384,256]{1,0:T(8,128)(2,1)}) %reduce-scatter.6.cloned.1.call-update) | async-done | bytes 196624 | tf_op jit(solution)/shard_map/reduce_scatter | solution.py:164
  514.8 228.1 %reduce-scatter.8.cloned.1.call-done = bf16[64,3,512]{2,0,1:T(8,128)(2,1)} async-done(((bf16[2048,3,512]{2,0,1:T(8,128)(2,1)}), bf16[64,3,512]{2,0,1:T(8,128)(2,1)}) %reduce-scatter.8.cloned.1.call-update) | async-done | bytes 196624 | tf_op jit(solution)/shard_map/reduce_scatter | solution.py:134
  (88 shorter events, 21.9 us)
Async XLA Ops:
  7.2 46.9 %all-gather.6.cloned.1.call-start = ((), (), s32[]{:S(2)}) async-start(), calls=%async_computation.3 | async-start | bytes 1769472 | tf_op jit(solution)/shard_map/all_gather | solution.py:80
  7.9 137.1 %all-gather.8.cloned.1.call-start = ((), (), s32[]{:S(2)}) async-start(), calls=%async_computation.6 | async-start | bytes 6488064 | tf_op jit(solution)/shard_map/all_gather | solution.py:88
  8.6 214.0 %all-gather.10.cloned.1.call-start = ((), (), s32[]{:S(2)}) async-start(), calls=%async_computation.7 | async-start | bytes 2162688 | tf_op jit(solution)/shard_map/all_gather | solution.py:89
  9.4 465.4 %reduce-scatter.10.cloned.1.call-start = ((), (), s32[]{:S(2)}) async-start(), calls=%async_computation.8 | async-start | bytes 2162688
  150.9 71.8 %copy-start.2 = (bf16[1,384,2048]{2,1,0:T(8,128)(2,1)S(1)}, bf16[1,384,2048]{2,1,0:T(8,128)(2,1)}, u32[]{:S(2)}) copy-start(bf16[1,384,2048]{2,1,0:T(8,128)(2,1)} %param.10) | copy-start | bytes 4718596
  152.1 75.5 %collective-permute-start = (bf16[2,384,512]{2,1,0:T(8,128)(2,1)}, bf16[2,384,512]{2,1,0:T(8,128)(2,1)}, u32[]{:S(2)}, u32[]{:S(2)}) collective-permute-start(bf16[2,384,512]{2,1,0:T(8,128)(2,1)} %pad_maximum_fusion.5), channel_id=1, source_target_pairs={{0,2},{2,4},{4,6},{6,8},{8,10},{10,12},{12,14},{14,16},{16,18},{18... | collective-permute-start | bytes 2359304 | tf_op jit(solution)/shard_map/ppermute | solution.py:16
  225.5 24.2 %copy-start.7 = (bf16[384,512]{0,1:T(8,128)(2,1)}, bf16[384,512]{0,1:T(8,128)(2,1)S(1)}, u32[]{:S(2)}) copy-start(bf16[384,512]{0,1:T(8,128)(2,1)S(1)} %copy.40) | copy-start | bytes 1179652
  227.6 5.7 copy-start.4
  229.1 4.1 copy-start.6
  229.1 4.1 copy-start.9
  236.3 6.5 slice-start
  236.5 11.5 %copy-start.13 = (bf16[1,384,512]{1,2,0:T(8,128)(2,1)}, bf16[1,384,512]{1,2,0:T(8,128)(2,1)S(1)}, u32[]{:S(2)}) copy-start(bf16[1,384,512]{1,2,0:T(8,128)(2,1)S(1)} %copy.41) | copy-start | bytes 1179652
  236.5 6.2 copy-start.15
  236.5 6.2 slice-start.1
  242.8 3.1 copy-start.17
  242.8 3.1 copy-start.19
  245.1 4.6 copy-start.16
  245.1 4.6 copy-start.18
  245.1 1.3 copy-start.11
  256.1 4.3 copy-start.8
  256.1 4.3 copy-start.12
  256.1 4.4 copy-start.14
  260.1 3.3 copy-start.10
  260.1 254.7 %reduce-scatter.6.cloned.1.call-start = ((), (), s32[]{:S(2)}) async-start(), calls=%async_computation.4 | async-start | bytes 1769472 | tf_op jit(solution)/shard_map/reduce_scatter | solution.py:164
  294.6 23.2 %copy-start.1 = (f32[768,4,64]{0,2,1:T(8,128)}, f32[768,4,64]{0,2,1:T(8,128)S(1)}, u32[]{:S(2)}) copy-start(f32[768,4,64]{0,2,1:T(8,128)S(1)} %fusion.55) | copy-start | bytes 2359300
  299.5 18.3 %copy-start.5 = (bf16[384,1,512]{0,2,1:T(8,128)(2,1)S(1)}, bf16[384,1,512]{0,2,1:T(8,128)(2,1)}, u32[]{:S(2)}) copy-start(bf16[384,1,512]{0,2,1:T(8,128)(2,1)} %copy-done.4) | copy-start | bytes 1179652
  299.5 37.8 %collective-permute-start.1 = (bf16[2,384,512]{2,1,0:T(8,128)(2,1)}, bf16[2,384,512]{2,1,0:T(8,128)(2,1)}, u32[]{:S(2)}, u32[]{:S(2)}) collective-permute-start(bf16[2,384,512]{2,1,0:T(8,128)(2,1)} %pad_maximum_fusion.6), channel_id=1, source_target_pairs={{2,0},{4,2},{6,4},{8,6},{10,8},{12,10},{14,12},{16,14},{18,16},{20... | collective-permute-start | bytes 2359304 | tf_op jit(solution)/shard_map/ppermute | solution.py:16
  335.8 4.3 copy-start
  340.1 5.1 copy-start.3
  347.4 395.5 %reduce-scatter.8.cloned.1.call-start = ((), (), s32[]{:S(2)}) async-start(), calls=%async_computation.5 | async-start | bytes 6488064 | tf_op jit(solution)/shard_map/reduce_scatter | solution.py:134
Sparse Core Ops, SparseCore 0:
  9.7 44.3 all-gather.5
  56.7 88.2 all-gather.7
  147.6 75.0 all-gather.9
  260.2 214.4 reduce-scatter.9
  477.9 36.8 reduce-scatter.5
  519.7 223.1 reduce-scatter.7
where the time goes:
time: 751 us; the launch traced here: 750 us
  waiting for transfers between devices  589 us (78%)
  matrix products  98.9 us (13%)
  other arithmetic  25.9 us (3%)
  local copies, waits for them, and re-layouts  15.1 us (2%)
  between operations  14.6 us (2%)
    reduce_scatter x1, waiting for transfers between devices, per_device(): lax.psum_scatter(jnp.einsum('tc,tse->cse', columns, triple_matrix_sensiti...  228 us
    unnamed x7, waiting for transfers between devices  124 us
    all_gather x1, waiting for transfers between devices, per_device(): lax.all_gather(qkv_weight[0], 'seq', axis=0, tiled=True)  89.1 us
    all_gather x1, waiting for transfers between devices, per_device(): lax.all_gather(out_weight[0], 'seq', axis=0, tiled=True)  65.8 us
    all_gather x1, waiting for transfers between devices, per_device(): gathered = lax.all_gather(hidden_states, ('head', 'mp'), axis=1, tiled=True)  44 us
    reduce_scatter x1, waiting for transfers between devices, per_device(): lax.psum_scatter(state_grad.astype(jnp.bfloat16), ('head', 'mp'), scatter...  38.3 us
    dot_general x2, matrix products, attend(): jnp.einsum('hqk,khd->qhd', score_grad, key_rows, preferred_element_type=j...  31.1 us
    dot_general x2, matrix products, attend(): jnp.einsum('hqk,qhd->khd', score_grad, queries, preferred_element_type=jn...  27.3 us
  transfers between devices with their start and end apart: 8, of which 6 were waited for; matrix products, arithmetic and copies ran while one was open for 14% of the time, Pallas kernels for 0%

commit v1 on v0

v1 whole, which is shorter than its diff:
```python
import functools

import jax
import jax.numpy as jnp
from jax import lax
from jax.experimental import pallas as pl
from jax.experimental.pallas import tpu as pltpu
from jax.sharding import PartitionSpec as P

HD = 64
EPS = 1e-05
MASKED = -1e30
MESH = pl.DeviceIdType.MESH
VMEM_LIMIT = 56 * 1024 * 1024
BF = jnp.bfloat16
F32 = jnp.float32


def places():
    head, seq, mp = (lax.axis_index(name) for name in ("head", "seq", "mp"))
    z, x = seq // 4, seq % 4
    odd = x % 2
    info = {
        "head": head,
        "mp": mp,
        "z": z,
        "x": x,
        "odd": odd,
        "pair": x // 2,
        "quarter": ((x + 1) // 2) % 2,
        "core": head % 2,
        "hi": head // 2,
        "e1": (head, seq + 1 - 2 * odd, mp),
        "e2": (head, z * 4 + 3 - x, mp),
        "zp": (head, ((z + 1) % 8) * 4 + x, mp),
        "zm": (head, ((z + 7) % 8) * 4 + x, mp),
        "near": (head, seq, 1 - mp),
        "far": ((head + 2) % 4, seq, 1 - mp),
        "twin": (head + 1 - 2 * (head % 2), seq, mp),
        "halo": (head, (seq + 31 + 2 * odd) % 32, mp),
    }
    return info


def greet(info):
    barrier = pltpu.get_barrier_semaphore()
    names = ("e1", "e2", "zp", "zm", "near", "far", "twin", "halo")
    for name in names:
        pl.semaphore_signal(barrier, inc=1, device_id=info[name], device_id_type=MESH)
    pl.semaphore_wait(barrier, len(names))


class Wires:
    def __init__(self, send, recv):
        self.send, self.recv, self.count = send, recv, 0
        self.started = []

    def slot(self):
        self.count += 1
        return self.count - 1

    def put(self, slot, src, dst, device):
        copy = pltpu.make_async_remote_copy(
            src_ref=src,
            dst_ref=dst,
            send_sem=self.send.at[slot],
            recv_sem=self.recv.at[slot],
            device_id=device,
            device_id_type=MESH,
        )
        copy.start()
        self.started.append((slot, src))

    def got(self, slot, dst):
        pltpu.make_async_copy(dst, dst, self.recv.at[slot]).wait()

    def finish(self):
        for slot, src in self.started:
            pltpu.make_async_copy(src, src, self.send.at[slot]).wait()


GATHER_SLOTS = 80


def gather_kernel(hid, ws, cot, h_out, w_out, c_out, send, recv, local):
    info = places()
    z, x, odd, p, q = (info[name] for name in ("z", "x", "odd", "pair", "quarter"))
    mp, core, hi = info["mp"], info["core"], info["hi"]
    wires = Wires(send, recv)

    own_w = pltpu.make_async_copy(ws.at[q], w_out.at[:, z, x], local.at[0])
    own_w.start()
    own_c = pltpu.make_async_copy(cot, c_out.at[odd], local.at[1])
    piece = (info["head"] * 2 + mp) * 256
    b = 1 + odd
    blocks = (b, 3 - b, 0)

    def cols(block, head_hi, head_core, part):
        start = pl.multiple_of(((head_hi * 2 + head_core) * 2 + part) * 256, 256)
        return h_out.at[block, :, pl.ds(start, 256)]

    own_h = pltpu.make_async_copy(hid, cols(b, hi, core, mp), local.at[2])
    own_h.start()
    own_c.start()

    greet(info)

    w_e1 = [wires.slot() for _ in range(2)]
    for half in range(2):
        arrs = pl.ds(2 * half, 2)
        wires.put(w_e1[half], ws.at[1 - q, arrs], w_out.at[arrs, z, x], info["e1"])
    h_e1, h_halo = wires.slot(), wires.slot()
    h_near = [wires.slot() for _ in range(3)]
    h_far = [wires.slot() for _ in range(3)]
    h_opp = [wires.slot() for _ in range(3)]
    h_twin = [[wires.slot() for _ in range(4)] for _ in range(3)]
    mine = cols(b, hi, core, mp)
    wires.put(h_e1, hid, mine, info["e1"])
    halo_own = cols(0, hi, core, mp)

    @pl.when(odd == 1)
    def _():
        pltpu.make_async_remote_copy(
            src_ref=hid,
            dst_ref=halo_own,
            send_sem=send.at[h_halo],
            recv_sem=recv.at[h_halo],
            device_id=info["halo"],
            device_id_type=MESH,
        ).start()

    def spread(r, src):
        dst = cols(blocks[r], hi, core, mp)
        wires.put(h_near[r], src, dst, info["near"])
        wires.put(h_far[r], src, dst, info["far"])
        wires.put(h_twin[r][0], src, dst, info["twin"])

    def from_near(r):
        got = cols(blocks[r], hi, core, 1 - mp)
        wires.got(h_near[r], got)
        wires.put(h_opp[r], got, got, info["far"])
        wires.put(h_twin[r][1], got, got, info["twin"])

    def from_far(r):
        got = cols(blocks[r], 1 - hi, core, 1 - mp)
        wires.got(h_far[r], got)
        wires.put(h_twin[r][2], got, got, info["twin"])

    def from_opp(r):
        got = cols(blocks[r], 1 - hi, core, mp)
        wires.got(h_opp[r], got)
        wires.put(h_twin[r][3], got, got, info["twin"])

    def from_twin(r):
        other = 1 - core
        wires.got(h_twin[r][0], cols(blocks[r], hi, other, mp))
        wires.got(h_twin[r][1], cols(blocks[r], hi, other, 1 - mp))
        wires.got(h_twin[r][2], cols(blocks[r], 1 - hi, other, 1 - mp))
        wires.got(h_twin[r][3], cols(blocks[r], 1 - hi, other, mp))

    spread(0, hid)

    def own_pair(first, count, layer):
        return w_out.at[pl.ds(first, count), layer, pl.ds(2 * p, 2)]

    def other_pair(first, count, layer):
        return w_out.at[pl.ds(first, count), layer, pl.ds(2 - 2 * p, 2)]

    a_own = [[wires.slot() for _ in range(4)] for _ in range(2)]
    a_oth = [[wires.slot() for _ in range(4)] for _ in range(2)]
    b_own = [[wires.slot() for _ in range(4)] for _ in range(2)]
    a_e2 = wires.slot()
    b_e2 = [wires.slot()] + [wires.slot() for _ in range(8)]
    ways = ("zp", "zm")

    def span(way, hop, first):
        return (first, 2) if hop < 4 else (first + way, 1)

    def layer_from(way, hop):
        return (z + 8 - hop) % 8 if way == 0 else (z + hop) % 8

    def pass_on(slots, part, first, way, hop):
        lo, count = span(way, hop + 1, first)
        ref = part(lo, count, layer_from(way, hop))
        wires.put(slots[way][hop], ref, ref, info[ways[way]])

    def take(slots, part, first, way, hop):
        lo, count = span(way, hop, first)
        ref = part(lo, count, layer_from(way, hop))
        wires.got(slots[way][hop - 1], ref)
        return ref

    own_w.wait()
    wires.got(w_e1[0], w_out.at[pl.ds(0, 2), z, x + 1 - 2 * odd])
    for way in range(2):
        pass_on(a_own, own_pair, 0, way, 0)
    ref = own_pair(0, 2, z)
    wires.put(a_e2, ref, ref, info["e2"])
    wires.got(w_e1[1], w_out.at[pl.ds(2, 2), z, x + 1 - 2 * odd])
    for way in range(2):
        pass_on(b_own, own_pair, 2, way, 0)
    ref = own_pair(2, 2, z)
    wires.put(b_e2[0], ref, ref, info["e2"])

    rows = 48
    c_e1 = [wires.slot() for _ in range(4)]
    c_near = [wires.slot() for _ in range(4)]

    def c_rows(block, part, k):
        return c_out.at[block, pl.ds(pl.multiple_of(part * 192 + k * rows, rows), rows)]

    for k in range(4):
        src = cot.at[pl.ds(pl.multiple_of(mp * 192 + k * rows, rows), rows)]
        wires.put(c_e1[k], src, c_rows(odd, mp, k), info["e1"])

    def c_step(k):
        ref = c_rows(1 - odd, mp, k)
        wires.got(c_e1[k], ref)
        wires.put(c_near[k], ref, ref, info["near"])

    wires.got(h_e1, cols(3 - b, hi, core, mp))
    spread(1, cols(3 - b, hi, core, mp))

    wires.got(a_e2, other_pair(0, 2, z))
    for way in range(2):
        pass_on(a_oth, other_pair, 0, way, 0)
    from_near(0)
    wires.got(h_halo, halo_own)

    @pl.when(odd == 0)
    def _():
        pltpu.make_async_remote_copy(
            src_ref=halo_own,
            dst_ref=halo_own,
            send_sem=send.at[h_halo],
            recv_sem=recv.at[h_halo],
            device_id=info["e1"],
            device_id_type=MESH,
        ).start()

    wires.started.append((h_halo, hid))
    spread(2, halo_own)

    count = 1
    for hop in range(1, 5):
        for way in range(2):
            take(a_own, own_pair, 0, way, hop)
            if hop < 4:
                pass_on(a_own, own_pair, 0, way, hop)
        for way in range(2):
            ref = take(b_own, own_pair, 2, way, hop)
            if hop < 4:
                pass_on(b_own, own_pair, 2, way, hop)
            wires.put(b_e2[count], ref, ref, info["e2"])
            count += 1
        if hop < 4:
            from_far(hop - 1)
            from_near(hop) if hop < 3 else None
        c_step(hop - 1)
        for way in range(2):
            take(a_oth, other_pair, 0, way, hop)
            if hop < 4:
                pass_on(a_oth, other_pair, 0, way, hop)
        if hop < 4:
            from_opp(hop - 1)

    wires.got(b_e2[0], other_pair(2, 2, z))
    count = 1
    for hop in range(1, 5):
        for way in range(2):
            lo, width = span(way, hop, 2)
            wires.got(b_e2[count], other_pair(lo, width, layer_from(way, hop)))
            count += 1
    for r in range(3):
        from_twin(r)
    for k in range(4):
        wires.got(c_near[k], c_rows(1 - odd, 1 - mp, k))
    own_h.wait()
    own_c.wait()
    wires.finish()


def gather(hid, ws, cot):
    anywhere = pl.BlockSpec(memory_space=pl.ANY)
    return pl.pallas_call(
        gather_kernel,
        out_shape=(
            jax.ShapeDtypeStruct((3, 384, 2048), BF),
            jax.ShapeDtypeStruct((4, 8, 4, 64, 256), BF),
            jax.ShapeDtypeStruct((2, 384, 2048), BF),
        ),
        in_specs=[anywhere] * 3,
        out_specs=(anywhere,) * 3,
        scratch_shapes=[
            pltpu.SemaphoreType.DMA((GATHER_SLOTS,)),
            pltpu.SemaphoreType.DMA((GATHER_SLOTS,)),
            pltpu.SemaphoreType.DMA((3,)),
        ],
        compiler_params=pltpu.CompilerParams(
            collective_id=0, has_side_effects=True, vmem_limit_bytes=VMEM_LIMIT
        ),
        name="gather",
    )(hid, ws, cot)


REDUCE_SLOTS = 64


def add(*terms):
    total = terms[0].astype(F32)
    for term in terms[1:]:
        total = total + term.astype(F32)
    return total.astype(BF)


def reduce_kernel(
    grads, trunk, w_res, t_res,
    a_got, a_out, b_e2got, b_got, b_out, a_fin, a_e2got, w_pair,
    t_twin, t_sum, t_far, t_mid, t_near, t_fin, t_e1, t_halo, t_pass,
    send, recv, local,
):
    info = places()
    z, x, odd, p, q = (info[name] for name in ("z", "x", "odd", "pair", "quarter"))
    mp, core, hi = info["mp"], info["core"], info["hi"]
    wires = Wires(send, recv)
    ways = ("zp", "zm")
    a_slot = [[wires.slot() for _ in range(4)] for _ in range(2)]
    b_slot = [[wires.slot() for _ in range(4)] for _ in range(2)]
    b_e2 = [wires.slot() for _ in range(8)]
    a_e2 = wires.slot()
    w_e1 = [wires.slot() for _ in range(2)]
    s_twin = [[wires.slot() for _ in range(2)] for _ in range(3)]
    s_far = [wires.slot() for _ in range(3)]
    s_near = [wires.slot() for _ in range(3)]
    s_e1 = wires.slot()
    s_half = wires.slot()
    s_halo = wires.slot()
    blocks = (0, 2 - odd, 1 + odd)
    half = 512

    greet(info)

    def to_layer(way, left):
        return (z + left) % 8 if way == 0 else (z + 8 - left) % 8

    for way in range(2):
        wires.put(
            a_slot[way][0],
            grads.at[pl.ds(way, 1), to_layer(way, 4)],
            a_got.at[way, 0, pl.ds(way, 1)],
            info[ways[way]],
        )
    order = [(0, 4), (0, 3), (1, 3), (0, 2), (1, 2), (0, 1), (1, 1), (0, 0)]
    for k, (way, left) in enumerate(order):
        wires.put(
            b_e2[k],
            grads.at[pl.ds(2, 2), to_layer(way, left), pl.ds(2 - 2 * p, 2)],
            b_e2got.at[k],
            info["e2"],
        )

    def columns(side, head_core):
        return pl.ds(pl.multiple_of(side * 1024 + head_core * half, half), half)

    for r in range(3):
        for side in range(2):
            wires.put(
                s_twin[r][side],
                trunk.at[blocks[r], :, columns(side, 1 - core)],
                t_twin.at[r, side],
                info["twin"],
            )

    def fold_twin(r):
        for side in (0, 1):
            wires.got(s_twin[r][side], t_twin.at[r, side])
            t_sum[r, side] = add(
                trunk[blocks[r], :, columns(side, core)], t_twin[r, side]
            )
        wires.put(s_far[r], t_sum.at[r, 1 - hi], t_far.at[r], info["far"])

    def fold_far(r):
        wires.got(s_far[r], t_far.at[r])
        for part in range(2):
            lanes = pl.ds(part * 256, 256)
            t_mid[r, part] = add(t_sum[r, hi, :, lanes], t_far[r, :, lanes])
        wires.put(s_near[r], t_mid.at[r, 1 - mp], t_near.at[r], info["near"])

    def fold_near(r):
        wires.got(s_near[r], t_near.at[r])
        t_fin[r] = add(t_mid[r, mp], t_near[r])

    def b_start(way, left, k):
        layer = to_layer(way, left)
        return add(grads[pl.ds(2, 2), layer, pl.ds(2 * p, 2)], b_e2got[k])

    def a_step(way, step):
        arrived = a_got.at[way, step - 1]
        layer = to_layer(way, 4 - step)
        if step == 1:
            wires.got(a_slot[way][0], a_got.at[way, 0, pl.ds(way, 1)])
            a_out[way, step, way] = add(grads[way, layer], a_got[way, 0, way])
            a_out[way, step, 1 - way] = grads[1 - way, layer]
        else:
            wires.got(a_slot[way][step - 1], arrived)
            a_out[way, step] = add(grads[pl.ds(0, 2), layer], a_got[way, step - 1])
        wires.put(a_slot[way][step], a_out.at[way, step], a_got.at[way, step], info[ways[way]])

    def b_step(way, step):
        k = {1: 1 + way, 2: 3 + way, 3: 5 + way}[step]
        wires.got(b_e2[k], b_e2got.at[k])
        mine = b_start(way, 4 - step, k)
        if step == 1:
            wires.got(b_slot[way][0], b_got.at[way, 0, pl.ds(way, 1)])
            b_out[way, step, way] = add(mine[way], b_got[way, 0, way])
            b_out[way, step, 1 - way] = mine[1 - way]
        else:
            wires.got(b_slot[way][step - 1], b_got.at[way, step - 1])
            b_out[way, step] = add(mine, b_got[way, step - 1])
        wires.put(b_slot[way][step], b_out.at[way, step], b_got.at[way, step], info[ways[way]])

    fold_twin(0)
    wires.got(b_e2[0], b_e2got.at[0])
    b_out[0, 0] = b_start(0, 4, 0)
    for way in range(2):
        wires.put(
            b_slot[way][0],
            b_out.at[0, 0, pl.ds(way, 1)],
            b_got.at[way, 0, pl.ds(way, 1)],
            info[ways[way]],
        )
    fold_twin(1)
    fold_twin(2)
    for way in range(2):
        a_step(way, 1)
    for way in range(2):
        b_step(way, 1)
    fold_far(0)
    for way in range(2):
        a_step(way, 2)
    for way in range(2):
        b_step(way, 2)
    fold_near(0)

    @pl.when(odd == 1)
    def _():
        pltpu.make_async_remote_copy(
            src_ref=t_fin.at[0],
            dst_ref=t_halo,
            send_sem=send.at[s_half],
            recv_sem=recv.at[s_half],
            device_id=info["e1"],
            device_id_type=MESH,
        ).start()

    for way in range(2):
        a_step(way, 3)
    for way in range(2):
        b_step(way, 3)
    fold_far(1)

    @pl.when(odd == 0)
    def _():
        wires.got(s_half, t_halo)
        t_pass[...] = add(t_fin[0], t_halo[...])
        pltpu.make_async_remote_copy(
            src_ref=t_pass,
            dst_ref=t_halo,
            send_sem=send.at[s_halo],
            recv_sem=recv.at[s_halo],
            device_id=info["halo"],
            device_id_type=MESH,
        ).start()

    for way in range(2):
        wires.got(a_slot[way][3], a_got.at[way, 3])
    a_fin[...] = add(grads[pl.ds(0, 2), z], a_got[0, 3], a_got[1, 3])
    wires.put(a_e2, a_fin.at[:, pl.ds(2 - 2 * p, 2)], a_e2got, info["e2"])
    fold_near(1)
    wires.put(s_e1, t_fin.at[1], t_e1, info["e1"])
    wires.got(b_e2[7], b_e2got.at[7])
    for way in range(2):
        wires.got(b_slot[way][3], b_got.at[way, 3])
    w_pair[pl.ds(2, 2)] = add(
        grads[pl.ds(2, 2), z, pl.ds(2 * p, 2)], b_e2got[7], b_got[0, 3], b_got[1, 3]
    )
    wires.put(
        w_e1[1], w_pair.at[pl.ds(2, 2), 1 - odd], w_res.at[q, pl.ds(2, 2)], info["e1"]
    )
    wires.got(a_e2, a_e2got)
    w_pair[pl.ds(0, 2)] = add(a_fin[:, pl.ds(2 * p, 2)], a_e2got[...])
    wires.put(
        w_e1[0], w_pair.at[pl.ds(0, 2), 1 - odd], w_res.at[q, pl.ds(0, 2)], info["e1"]
    )
    w_res[q] = w_pair[:, odd]
    fold_far(2)
    fold_near(2)
    wires.got(s_e1, t_e1)

    @pl.when(odd == 0)
    def _():
        t_res[...] = add(t_fin[2], t_e1[...])
        pltpu.make_async_copy(t_pass, t_pass, send.at[s_halo]).wait()

    @pl.when(odd == 1)
    def _():
        wires.got(s_halo, t_halo)
        t_res[...] = add(t_fin[2], t_e1[...], t_halo[...])
        pltpu.make_async_copy(t_halo, t_halo, send.at[s_half]).wait()

    for part in range(2):
        wires.got(w_e1[part], w_res.at[1 - q, pl.ds(2 * part, 2)])
    wires.finish()


def reduce(grads, trunk):
    in_vmem = pl.BlockSpec(memory_space=pltpu.VMEM)
    return pl.pallas_call(
        reduce_kernel,
        out_shape=(
            jax.ShapeDtypeStruct((2, 4, 64, 256), BF),
            jax.ShapeDtypeStruct((384, 256), BF),
        ),
        in_specs=[in_vmem] * 2,
        out_specs=(in_vmem,) * 2,
        scratch_shapes=[
            pltpu.VMEM((2, 4, 2, 4, 64, 256), BF),
            pltpu.VMEM((2, 4, 2, 4, 64, 256), BF),
            pltpu.VMEM((8, 2, 2, 64, 256), BF),
            pltpu.VMEM((2, 4, 2, 2, 64, 256), BF),
            pltpu.VMEM((2, 4, 2, 2, 64, 256), BF),
            pltpu.VMEM((2, 4, 64, 256), BF),
            pltpu.VMEM((2, 2, 64, 256), BF),
            pltpu.VMEM((4, 2, 64, 256), BF),
            pltpu.VMEM((3, 2, 384, 512), BF),
            pltpu.VMEM((3, 2, 384, 512), BF),
            pltpu.VMEM((3, 384, 512), BF),
            pltpu.VMEM((3, 2, 384, 256), BF),
            pltpu.VMEM((3, 384, 256), BF),
            pltpu.VMEM((3, 384, 256), BF),
            pltpu.VMEM((384, 256), BF),
            pltpu.VMEM((384, 256), BF),
            pltpu.VMEM((384, 256), BF),
            pltpu.SemaphoreType.DMA((REDUCE_SLOTS,)),
            pltpu.SemaphoreType.DMA((REDUCE_SLOTS,)),
            pltpu.SemaphoreType.DMA((1,)),
        ],
        compiler_params=pltpu.CompilerParams(
            collective_id=1, has_side_effects=True, vmem_limit_bytes=VMEM_LIMIT
        ),
        name="reduce",
    )(grads, trunk)


NT = (((1,), (1,)), ((), ()))
TN = (((0,), (0,)), ((), ()))


def attend_kernel(q_ref, k_ref, v_ref, g_ref, segk_ref, segq_ref, o_ref, dq_ref, dk_ref, dv_ref, dk_acc, dv_acc):
    scale = HD**-0.5
    dk_acc[...] = jnp.zeros_like(dk_acc)
    dv_acc[...] = jnp.zeros_like(dv_acc)
    lane_head = lax.broadcasted_iota(jnp.int32, (128, 256), 1) // HD

    def by_head(rows):
        return jnp.concatenate(
            [jnp.where(lane_head == h, rows, jnp.zeros_like(rows)) for h in range(4)], axis=0
        )

    def fold(wide):
        return jnp.concatenate(
            [wide[h * HD : (h + 1) * HD, h * 128 : (h + 1) * 128] for h in range(4)], axis=0
        ).T

    key_at = lax.broadcasted_iota(jnp.int32, (512, 128), 0)
    query_at = lax.broadcasted_iota(jnp.int32, (512, 128), 1) + 384
    causal = key_at <= query_at

    def tile(t, carry):
        start = pl.multiple_of(t * 128, 128)
        here, window = pl.ds(start, 128), pl.ds(start, 512)
        queries, grads = by_head(q_ref[here, :]), by_head(g_ref[here, :])
        keys, values = k_ref[window, :], v_ref[window, :]
        allowed = causal & (segk_ref[window, :] == segq_ref[t])
        allowed = jnp.concatenate([allowed] * 4, axis=1)
        scores = lax.dot_general(keys, queries, NT, preferred_element_type=F32) * scale
        scores = jnp.where(allowed, scores, MASKED)
        expo = jnp.exp(scores - jnp.max(scores, axis=0, keepdims=True))
        probs = expo * (1.0 / jnp.sum(expo, axis=0, keepdims=True))
        prob_rows = probs.astype(BF)
        prob_grad = lax.dot_general(values, grads, NT, preferred_element_type=F32)
        delta = jnp.sum(probs * prob_grad, axis=0, keepdims=True)
        score_grad = (probs * (prob_grad - delta) * scale).astype(BF)
        dv_acc[window, :] += jnp.dot(prob_rows, grads, preferred_element_type=F32)
        dk_acc[window, :] += jnp.dot(score_grad, queries, preferred_element_type=F32)
        o_ref[here, :] = fold(
            lax.dot_general(values, prob_rows, TN, preferred_element_type=F32)
        ).astype(BF)
        dq_ref[here, :] = fold(
            lax.dot_general(keys, score_grad, TN, preferred_element_type=F32)
        ).astype(BF)
        return carry

    lax.fori_loop(0, 6, tile, 0)
    dk_ref[...] = dk_acc[...].astype(BF)
    dv_ref[...] = dv_acc[...].astype(BF)


def attend(queries, keys, values, attn_grad, seg_keys, seg_queries):
    shapes = [(768, 256), (768, 256), (1152, 256), (1152, 256)]
    return pl.pallas_call(
        attend_kernel,
        out_shape=tuple(jax.ShapeDtypeStruct(shape, BF) for shape in shapes),
        scratch_shapes=[pltpu.VMEM((1152, 256), F32)] * 2,
        compiler_params=pltpu.CompilerParams(vmem_limit_bytes=VMEM_LIMIT),
        name="attend",
    )(queries, keys, values, attn_grad, seg_keys, seg_queries)


def per_device(hidden_states, norm_gain, qkv_weight, out_weight, cotangent, segment_ids):
    seq, mp = lax.axis_index("seq"), lax.axis_index("mp")
    odd = seq % 2
    shard = jnp.concatenate(
        [jnp.transpose(qkv_weight[0], (1, 0, 2)), out_weight], axis=0
    )
    shard = jnp.transpose(shard.reshape(4, 64, 2, 256), (2, 0, 1, 3))
    hidden, weights, upstream = gather(hidden_states, shard, cotangent[0])
    hidden = hidden.reshape(1152, 2048)
    weights = weights.reshape(4, 2048, 256)
    upstream = upstream.reshape(768, 2048)

    states = hidden.astype(F32)
    inverse = lax.rsqrt(jnp.mean(states * states, axis=-1, keepdims=True) + EPS)
    unit_rows = states * inverse
    gain = norm_gain[0].astype(F32)
    normed = (unit_rows * gain).astype(BF)

    def project(rows, weight):
        return jnp.dot(rows, weight, preferred_element_type=F32).astype(BF)

    queries = project(normed[384:], weights[0])
    keys = project(normed, weights[1])
    values = project(normed, weights[2])
    attn_grad = project(upstream, weights[3])

    first = (seq - odd) * 384 - 384
    seg = lax.dynamic_slice_in_dim(segment_ids, first + 384, 768)
    earlier = lax.dynamic_slice_in_dim(segment_ids, jnp.maximum(first, 0), 384)
    earlier = jnp.where(first >= 0, earlier, -1)
    seg_keys = jnp.concatenate([earlier, seg])[:, None]
    attn_out, dq, dk, dv = attend(
        queries, keys, values, attn_grad, seg_keys, seg.reshape(6, 1, 128)
    )

    def weight_grad(rows, grad):
        return lax.dot_general(rows, grad, TN, preferred_element_type=F32).astype(BF)

    grads = jnp.stack(
        [
            weight_grad(normed[384:], dq),
            weight_grad(normed, dk),
            weight_grad(normed, dv),
            weight_grad(upstream, attn_out),
        ]
    )

    def back(grad, weight):
        return lax.dot_general(grad, weight, NT, preferred_element_type=F32)

    scaled = (
        back(jnp.pad(dq, ((384, 0), (0, 0))), weights[0])
        + back(dk, weights[1])
        + back(dv, weights[2])
    ) * gain
    state_grad = inverse * (
        scaled - unit_rows * jnp.mean(scaled * unit_rows, axis=-1, keepdims=True)
    )
    block = jnp.arange(1152) // 384
    keep = (block == 1 + odd) & (mp == 0)
    residual = jnp.pad(upstream, ((384, 0), (0, 0))).astype(F32)
    trunk = (state_grad + jnp.where(keep[:, None], residual, 0.0)).astype(BF)

    w_res, t_res = reduce(grads.reshape(4, 8, 4, 64, 256), trunk.reshape(3, 384, 2048))
    merged = jnp.transpose(w_res, (1, 2, 0, 3)).reshape(4, 64, 512)
    return (t_res, jnp.transpose(merged[:3], (1, 0, 2))[None], merged[3][None])


def solution(mesh):
    placed = (
        P("seq", ("head", "mp")),
        P("head", None),
        P("head", "seq", None, "mp"),
        P("head", "seq", "mp"),
        P("head", "seq", None),
        P(),
    )
    return jax.shard_map(
        per_device,
        mesh=mesh,
        in_specs=placed,
        out_specs=(P("seq", ("head", "mp")), P("head", "seq", None, "mp"), P("head", "seq", "mp")),
        check_vma=False,
    )
```

time: 751 us -> 181 us (0.24)
  waiting for transfers between devices: 589 us -> 0 us
  Pallas kernels: 0 us -> 128 us
  matrix products: 98.9 us -> 20.7 us
  between operations: 14.6 us -> 0.84 us
  other arithmetic: 25.9 us -> 15.9 us
    reduce_scatter x2 -> x0, waiting for transfers between devices: 266 us -> none  [the longest x1 228 us: per_device(): lax.psum_scatter(jnp.einsum('tc,tse->cse', columns, triple_matrix_sensiti...]
    all_gather x3 -> x0, waiting for transfers between devices: 199 us -> none  [the longest x1 89.1 us: per_device(): lax.all_gather(qkv_weight[0], 'seq', axis=0, tiled=True)]
    pallas_call x0 -> x3, Pallas kernels: none -> 128 us  [the longest x1 64.3 us: gather(): pl.pallas_call(gather_kernel, out_shape=(jax.ShapeDtypeStruct((3, 384, 20...]
    unnamed x7 -> x0, waiting for transfers between devices: 124 us -> none
    dot_general x17 -> x11, matrix products: 98.9 us -> 20.7 us  [the longest x4 8 us: project(): return jnp.dot(rows, weight, preferred_element_type=F32).astype(BF)]
    sub x2 -> x0, other arithmetic: 8.51 us -> none  [attend(): expo = jnp.exp(scores - row_max)]
  transfers between devices with their start and end apart: 8 -> 0, of which waited for: 6 -> 0; matrix products, arithmetic and copies ran while one was open for 14% -> 0% of each run, Pallas kernels for 0% -> 0%
where the time goes in v1:
time: 181 us; the launch traced here: 179 us
  Pallas kernels  128 us (71%)
  matrix products  20.7 us (11%)
  other arithmetic  15.9 us (9%)
  local copies, waits for them, and re-layouts  13.5 us (7%)
    pallas_call x1, Pallas kernels, gather(): pl.pallas_call(gather_kernel, out_shape=(jax.ShapeDtypeStruct((3, 384, 20...  64.3 us
    pallas_call x1, Pallas kernels, reduce(): pl.pallas_call(reduce_kernel, out_shape=(jax.ShapeDtypeStruct((2, 4, 64,...  51.2 us
    pallas_call x1, Pallas kernels, attend(): pl.pallas_call(attend_kernel, out_shape=tuple((jax.ShapeDtypeStruct(shape...  12.5 us
    dot_general x4, matrix products, project(): return jnp.dot(rows, weight, preferred_element_type=F32).astype(BF)  8 us
    dot_general x4, matrix products, weight_grad(): lax.dot_general(rows, grad, TN, preferred_element_type=F32).astype(BF)  7.46 us
    unnamed x25, local copies, waits for them, and re-layouts  6.2 us
    convert_element_type x1, other arithmetic, per_device(): trunk = (state_grad + jnp.where(keep[:, None], residual, 0.0)).astype(BF)  5.51 us
    dot_general x3, matrix products, back(): return lax.dot_general(grad, weight, NT, preferred_element_type=F32)  5.22 us

profile of v1, /device:TPU:4, one launch (start us, length us, event | category | flops | bytes accessed | tf_op | source)
XLA Modules:
  0.0 178.9 jit_solution(11128367716915145997)
XLA Ops:
  0.7 0.8 dynamic-slice_select_fusion
  1.4 0.8 dynamic_slice.7
  2.8 0.7 mul.80
  3.5 1.0 pad_maximum_fusion.1
  4.5 0.7 copy.17
  5.3 1.0 broadcast_in_dim.32.segk_ref
  6.3 64.3 %gather.1 = (bf16[3,384,2048]{2,1,0:T(8,128)(2,1)}, bf16[4,8,4,64,256]{4,3,2,1,0:T(8,128)(2,1)}, bf16[2,384,2048]{2,1,0:T(8,128)(2,1)}) custom-call(bf16[384,256]{1,0:T(8,128)(2,1)} %hid.1, bf16[2,4,64,256]{3,2,1,0:T(8,128)(2,1)} %bitcast.79, bf16[384,2048]{1,0:T(8,128)(2,1)} %bitcast.77), custom_call_target="tpu_custom_call" | custom-call | tf_op jit(solution)/shard_map/gather/pallas_call | solution.py:285
  70.6 2.8 %fusion.19 = (bf16[1,8,4,64,256]{4,3,2,1,0:T(8,128)(2,1)S(1)}, bf16[1,8,4,64,256]{4,3,2,1,0:T(8,128)(2,1)S(1)}, bf16[1,8,4,64,256]{4,3,2,1,0:T(8,128)(2,1)S(1)}, bf16[1,8,4,64,256]{4,3,2,1,0:T(8,128)(2,1)S(1)}) fusion(bf16[4,8,4,64,256]{4,3,2,1,0:T(8,128)(2,1)} %get-tuple-element.13), kind=kLoop, calls=%fused_computation.42 | loop fusion | bytes 8388608 | tf_op jit(solution)/shard_map/slice | solution.py:644
  73.7 1.8 convolution_convert_fusion.5.g_ref
  75.5 1.0 multiply_reduce_fusion.1
  76.5 3.5 %multiply_convert_fusion = bf16[3,384,2048]{2,1,0:T(8,128)(2,1)S(1)} fusion(bf16[3,384,2048]{2,1,0:T(8,128)(2,1)} %get-tuple-element.12, f32[2048]{0:T(1024)S(1)} %bitcast.89, f32[3,384]{1,0:T(4,128)S(1)} %add_rsqrt_fusion), kind=kLoop, calls=%fused_computation.6 | loop fusion | flops 9437184 | bytes 9449984 | tf_op jit(solution)/shard_map/convert_element_type | solution.py:636
  80.0 2.2 %convolution_convert_fusion.3.v_ref = bf16[1152,256]{1,0:T(8,128)(2,1)} fusion(bf16[1152,2048]{1,0:T(8,128)(2,1)S(1)} %bitcast.66, bf16[2048,256]{1,0:T(8,128)(2,1)S(1)} %bitcast.68), kind=kOutput, calls=%fused_computation.18 | convolution fusion | flops 1208254464 | bytes 6356992 | tf_op jit(solution)/shard_map/dot_general | solution.py:639
  82.2 2.3 %convolution_convert_fusion.4.k_ref = bf16[1152,256]{1,0:T(8,128)(2,1)} fusion(bf16[1152,2048]{1,0:T(8,128)(2,1)S(1)} %bitcast.67, bf16[2048,256]{1,0:T(8,128)(2,1)S(1)} %bitcast.70), kind=kOutput, calls=%fused_computation.19 | convolution fusion | flops 1208254464 | bytes 6356992 | tf_op jit(solution)/shard_map/dot_general | solution.py:639
  84.5 1.1 multiply_convert_fusion.1
  85.7 2.1 %copy-done = bf16[1152,2048]{1,0:T(8,128)(2,1)} copy-done((bf16[1152,2048]{1,0:T(8,128)(2,1)}, bf16[1152,2048]{1,0:T(8,128)(2,1)S(1)}, u32[]{:S(2)}) %copy-start) | copy-done | bytes 4718616
  87.8 1.7 fusion.8.q_ref
  89.6 12.5 %attend.1 = (bf16[768,256]{1,0:T(8,128)(2,1)}, bf16[768,256]{1,0:T(8,128)(2,1)}, bf16[1152,256]{1,0:T(8,128)(2,1)}, bf16[1152,256]{1,0:T(8,128)(2,1)}) custom-call(bf16[768,256]{1,0:T(8,128)(2,1)} %fusion.8.q_ref, bf16[1152,256]{1,0:T(8,128)(2,1)} %convolution_convert_fusion.4.k_ref, bf16[1152,256]{1,0:T(8,128)(2,1)} %convolution_convert_fusion.3.v_ref, ...), custom_call_target="tpu_custom_call" | custom-call | tf_op jit(solution)/shard_map/attend/pallas_call | solution.py:611
  102.1 3.1 %convolution_convert_fusion.2 = bf16[2048,256]{1,0:T(8,128)(2,1)S(1)} fusion(bf16[768,2048]{1,0:T(8,128)(2,1)} %bitcast.74, bf16[768,256]{1,0:T(8,128)(2,1)} %get-tuple-element.18), kind=kOutput, calls=%fused_computation.17 | convolution fusion | flops 805830656 | bytes 4587520 | tf_op jit(solution)/shard_map/dot_general | solution.py:656
  105.6 1.1 fusion.5
  106.7 1.6 convolution_convert_fusion.1
  108.3 1.6 convolution_convert_fusion
  110.0 2.3 %pad_maximum_fusion.grads = bf16[4,8,4,64,256]{4,3,2,1,0:T(8,128)(2,1)} fusion(bf16[1,8,4,64,256]{4,3,2,1,0:T(8,128)(2,1)S(1)} %bitcast.81, bf16[1,8,4,64,256]{4,3,2,1,0:T(8,128)(2,1)S(1)} %bitcast.84, bf16[1,8,4,64,256]{4,3,2,1,0:T(8,128)(2,1)S(1)} %bitcast.83, bf16[1,8,4,64,256]{4,3,2,1,0:T(8,128)(2,1)S(1)} %bitcast.82), kind=kLoop, calls=%fused_computation.9 | loop fusion | flops 6291456 | bytes 8388608 | tf_op jit(solution)/shard_map/stack | solution.py:658
  112.2 1.4 fusion.11
  113.7 1.4 convolution_add_fusion.1
  115.1 2.4 %multiply_reduce_fusion = (f32[1152]{0:T(1024)S(1)}, f32[1152,2048]{1,0:T(8,128)S(1)}) fusion(bf16[3,384,2048]{2,1,0:T(8,128)(2,1)S(1)} %bitcast.64, f32[1152]{0:T(1024)S(1)} %rsqrt.13, f32[2048]{0:T(1024)S(1)} %bitcast.91, f32[1152,2048]{1,0:T(8,128)S(1)} %convolution_add_fusion.1, bf16[1152,256]{1,0:T(8,128)(2,1)S(1)} %copy-done.4, ...), kind=kOutput, calls=%fused_computation.5 | convolution fusion | flops 1222114176 | bytes 25248768 | tf_op jit(solution)/shard_map/dot_general | solution.py:668
  117.5 5.5 %add_convert_fusion = bf16[1152,2048]{1,0:T(8,128)(2,1)} fusion(f32[1152,2048]{1,0:T(8,128)S(1)} %get-tuple-element.26, bf16[3,384,2048]{2,1,0:T(8,128)(2,1)S(1)} %bitcast.64, bf16[768,2048]{1,0:T(8,128)(2,1)} %bitcast.75, f32[1152]{0:T(1024)S(1)} %broadcast_multiply_fusion, f32[1152]{0:T(1024)S(1)} %rsqrt.13, pred[1152]{0:T(1024)(128)(4,1)S(1)} %fusion.17), kind=kLoop, calls=%fused_computation.4 | loop fusion | flops 21233664 | bytes 22030464 | tf_op jit(solution)/shard_map/convert_element_type | solution.py:681
  123.0 51.2 %reduce.2 = (bf16[2,4,64,256]{3,2,1,0:T(8,128)(2,1)}, bf16[384,256]{1,0:T(8,128)(2,1)}) custom-call(bf16[4,8,4,64,256]{4,3,2,1,0:T(8,128)(2,1)} %pad_maximum_fusion.grads, bf16[3,384,2048]{2,1,0:T(8,128)(2,1)} %bitcast.65), custom_call_target="tpu_custom_call" | custom-call | tf_op jit(solution)/shard_map/reduce/pallas_call | solution.py:518
  174.2 0.8 slice_bitcast_fusion.1
  175.0 0.9 slice_bitcast_fusion
  175.9 0.7 copy.14
  176.6 0.6 copy.15
  177.3 1.6 copy.19
  (29 shorter events, 1.3 us)
Async XLA Ops:
  70.6 3.2 %copy-start.2 = (bf16[2,384,2048]{2,1,0:T(8,128)(2,1)S(1)}, bf16[2,384,2048]{2,1,0:T(8,128)(2,1)}, u32[]{:S(2)}) copy-start(bf16[2,384,2048]{2,1,0:T(8,128)(2,1)} %get-tuple-element.14) | copy-start | bytes 9437188
  70.6 4.9 %slice-start = ((s8[4718592]{0:T(1024)(128)(4,1)}), s8[4194304]{0:T(1024)(128)(4,1)S(1)}, s32[]{:S(2)}) async-start(s8[4718592]{0:T(1024)(128)(4,1)} %bitcast.61), calls=%async_computation | async-start | bytes 8388608
  70.6 4.9 %slice-start.1 = ((s8[4718592]{0:T(1024)(128)(4,1)}), s8[524288]{0:T(1024)(128)(4,1)S(1)}, s32[]{:S(2)}) async-start(s8[4718592]{0:T(1024)(128)(4,1)} %bitcast.61), calls=%async_computation.1 | async-start | bytes 1048576
  80.0 4.5 %slice-start.2 = ((s8[4718592]{0:T(1024)(128)(4,1)}), s8[4194304]{0:T(1024)(128)(4,1)S(1)}, s32[]{:S(2)}) async-start(s8[4718592]{0:T(1024)(128)(4,1)} %bitcast.63), calls=%async_computation.2 | async-start | bytes 8388608
  82.2 2.3 %slice-start.3 = ((s8[4718592]{0:T(1024)(128)(4,1)}), s8[524288]{0:T(1024)(128)(4,1)S(1)}, s32[]{:S(2)}) async-start(s8[4718592]{0:T(1024)(128)(4,1)} %bitcast.63), calls=%async_computation.3 | async-start | bytes 1048576
  85.7 2.1 %copy-start = (bf16[1152,2048]{1,0:T(8,128)(2,1)}, bf16[1152,2048]{1,0:T(8,128)(2,1)S(1)}, u32[]{:S(2)}) copy-start(bf16[1152,2048]{1,0:T(8,128)(2,1)S(1)} %multiply_convert_fusion.1) | copy-start | bytes 14155780
  102.1 3.4 %copy-start.1 = (bf16[1152,2048]{1,0:T(8,128)(2,1)S(1)}, bf16[1152,2048]{1,0:T(8,128)(2,1)}, u32[]{:S(2)}) copy-start(bf16[1152,2048]{1,0:T(8,128)(2,1)} %copy-done) | copy-start | bytes 14155780
  102.1 3.5 %copy-start.6 = (bf16[768,256]{1,0:T(8,128)(2,1)S(1)}, bf16[768,256]{1,0:T(8,128)(2,1)}, u32[]{:S(2)}) copy-start(bf16[768,256]{1,0:T(8,128)(2,1)} %get-tuple-element.15) | copy-start | bytes 1179652
  105.6 1.1 copy-start.5
  106.7 1.7 copy-start.3
  113.6 1.5 copy-start.4

commit v2 on v1

v2 whole, which is shorter than its diff:
```python
import functools

import jax
import jax.numpy as jnp
from jax import lax
from jax.experimental import pallas as pl
from jax.experimental.pallas import tpu as pltpu
from jax.sharding import PartitionSpec as P

HD = 64
EPS = 1e-05
MASKED = -1e30
MESH = pl.DeviceIdType.MESH
VMEM_LIMIT = 56 * 1024 * 1024
BF = jnp.bfloat16
F32 = jnp.float32


def places():
    head, seq, mp = (lax.axis_index(name) for name in ("head", "seq", "mp"))
    z, x = seq // 4, seq % 4
    odd = x % 2
    info = {
        "head": head,
        "mp": mp,
        "z": z,
        "x": x,
        "odd": odd,
        "pair": x // 2,
        "quarter": ((x + 1) // 2) % 2,
        "core": head % 2,
        "hi": head // 2,
        "e1": (head, seq + 1 - 2 * odd, mp),
        "e2": (head, z * 4 + 3 - x, mp),
        "zp": (head, ((z + 1) % 8) * 4 + x, mp),
        "zm": (head, ((z + 7) % 8) * 4 + x, mp),
        "near": (head, seq, 1 - mp),
        "far": ((head + 2) % 4, seq, 1 - mp),
        "twin": (head + 1 - 2 * (head % 2), seq, mp),
        "halo": (head, (seq + 31 + 2 * odd) % 32, mp),
    }
    return info


def greet(info):
    barrier = pltpu.get_barrier_semaphore()
    names = ("e1", "e2", "zp", "zm", "near", "far", "twin", "halo")
    for name in names:
        pl.semaphore_signal(barrier, inc=1, device_id=info[name], device_id_type=MESH)
    pl.semaphore_wait(barrier, len(names))


class Wires:
    def __init__(self, send, recv):
        self.send, self.recv, self.count = send, recv, 0
        self.started = []

    def slot(self):
        self.count += 1
        return self.count - 1

    def put(self, slot, src, dst, device):
        copy = pltpu.make_async_remote_copy(
            src_ref=src,
            dst_ref=dst,
            send_sem=self.send.at[slot],
            recv_sem=self.recv.at[slot],
            device_id=device,
            device_id_type=MESH,
        )
        copy.start()
        self.started.append((slot, src))

    def got(self, slot, dst):
        pltpu.make_async_copy(dst, dst, self.recv.at[slot]).wait()

    def finish(self):
        for slot, src in self.started:
            pltpu.make_async_copy(src, src, self.send.at[slot]).wait()


NT = (((1,), (1,)), ((), ()))
TN = (((0,), (0,)), ((), ()))


LAYERS = 8
COT_PARTS = 6
COT_ROWS = 192 // COT_PARTS
GATHER_SLOTS = 100


def front_kernel(
    hid, ws, cot, gain,
    q_out, k_out, v_out, g_out, inv_out, h_out, n_out, w_out, c_out,
    hv, nv, wv, cv, acc, send, recv, local,
):
    info = places()
    z, x, odd, p, q = (info[name] for name in ("z", "x", "odd", "pair", "quarter"))
    mp, core, hi = info["mp"], info["core"], info["hi"]
    wires = Wires(send, recv)
    ways = ("zp", "zm")
    mate = x + 1 - 2 * odd
    b = 1 + odd
    blocks = (b, 3 - b, 0)
    kept = []

    def keep(src, dst):
        copy = pltpu.make_async_copy(src, dst, local.at[3 + len(kept)])
        copy.start()
        kept.append(copy)

    def cols(block, head_hi, head_core, part):
        start = pl.multiple_of(((head_hi * 2 + head_core) * 2 + part) * 256, 256)
        return hv.at[block, :, pl.ds(start, 256)]

    own_w = pltpu.make_async_copy(ws.at[q], wv.at[:, z, x], local.at[0])
    own_w.start()
    own_h = pltpu.make_async_copy(hid, cols(b, hi, core, mp), local.at[1])
    own_h.start()
    own_c = pltpu.make_async_copy(cot, cv.at[odd], local.at[2])
    own_c.start()

    greet(info)

    w_e1 = [wires.slot() for _ in range(2)]
    h_e1, h_halo = wires.slot(), wires.slot()
    h_near = [wires.slot() for _ in range(3)]
    h_far = [wires.slot() for _ in range(3)]
    h_opp = [wires.slot() for _ in range(3)]
    h_twin = [[wires.slot() for _ in range(4)] for _ in range(3)]
    a_first = [[wires.slot() for _ in range(2)] for _ in range(2)]
    b_first = [[wires.slot() for _ in range(2)] for _ in range(2)]
    a_own = [[None] + [wires.slot() for _ in range(3)] for _ in range(2)]
    b_own = [[None] + [wires.slot() for _ in range(3)] for _ in range(2)]
    a_oth = [[wires.slot() for _ in range(4)] for _ in range(2)]
    a_e2 = [wires.slot() for _ in range(2)]
    b_e2 = [[wires.slot(), wires.slot()]] + [wires.slot() for _ in range(8)]
    c_e1 = [wires.slot() for _ in range(COT_PARTS)]
    c_near = [wires.slot() for _ in range(COT_PARTS)]

    def one(first, count, layer, place):
        return wv.at[pl.ds(first, count), layer, pl.ds(place, 1)]

    def own_pair(first, count, layer):
        return wv.at[pl.ds(first, count), layer, pl.ds(2 * p, 2)]

    def other_pair(first, count, layer):
        return wv.at[pl.ds(first, count), layer, pl.ds(2 - 2 * p, 2)]

    def span(way, hop, first):
        return (first, 2) if hop < 4 else (first + way, 1)

    def layer_from(way, hop):
        return (z + 8 - hop) % 8 if way == 0 else (z + hop) % 8

    def pass_on(slots, part, first, way, hop):
        lo, count = span(way, hop + 1, first)
        ref = part(lo, count, layer_from(way, hop))
        wires.put(slots[way][hop], ref, ref, info[ways[way]])

    def take(slots, part, first, way, hop):
        lo, count = span(way, hop, first)
        ref = part(lo, count, layer_from(way, hop))
        wires.got(slots[way][hop - 1], ref)
        return ref

    for half in (1, 0):
        arrs = pl.ds(2 * half, 2)
        wires.put(w_e1[half], ws.at[1 - q, arrs], wv.at[arrs, z, x], info["e1"])
    mine = cols(b, hi, core, mp)
    halo_own = cols(0, hi, core, mp)
    for first, slots in ((2, b_first), (0, a_first)):
        src = ws.at[q, pl.ds(first, 2)]
        for way in range(2):
            wires.put(slots[way][0], src, wv.at[pl.ds(first, 2), z, x], info[ways[way]])
    for first, slots in ((2, b_e2[0]), (0, a_e2)):
        src = ws.at[q, pl.ds(first, 2)]
        wires.put(slots[0], src, wv.at[pl.ds(first, 2), z, x], info["e2"])

    def spread(r, src):
        dst = cols(blocks[r], hi, core, mp)
        wires.put(h_near[r], src, dst, info["near"])
        wires.put(h_far[r], src, dst, info["far"])
        wires.put(h_twin[r][0], src, dst, info["twin"])

    wires.put(h_e1, hid, mine, info["e1"])

    @pl.when(odd == 1)
    def _():
        pltpu.make_async_remote_copy(
            src_ref=hid,
            dst_ref=halo_own,
            send_sem=send.at[h_halo],
            recv_sem=recv.at[h_halo],
            device_id=info["halo"],
            device_id_type=MESH,
        ).start()

    spread(0, hid)

    def second(half, slots, x_slots):
        first = 2 * half
        ref = one(first, 2, z, mate)
        wires.got(w_e1[half], ref)
        for way in range(2):
            wires.put(slots[way][1], ref, ref, info[ways[way]])
        wires.put(x_slots[1], ref, ref, info["e2"])

    def from_near(r):
        got = cols(blocks[r], hi, core, 1 - mp)
        wires.got(h_near[r], got)
        wires.put(h_opp[r], got, got, info["far"])
        wires.put(h_twin[r][1], got, got, info["twin"])

    def from_far(r):
        got = cols(blocks[r], 1 - hi, core, 1 - mp)
        wires.got(h_far[r], got)
        wires.put(h_twin[r][2], got, got, info["twin"])

    def from_opp(r):
        got = cols(blocks[r], 1 - hi, core, mp)
        wires.got(h_opp[r], got)
        wires.put(h_twin[r][3], got, got, info["twin"])

    def from_twin(r):
        other = 1 - core
        wires.got(h_twin[r][0], cols(blocks[r], hi, other, mp))
        wires.got(h_twin[r][1], cols(blocks[r], hi, other, 1 - mp))
        wires.got(h_twin[r][2], cols(blocks[r], 1 - hi, other, 1 - mp))
        wires.got(h_twin[r][3], cols(blocks[r], 1 - hi, other, mp))
        if r == 0:
            own_h.wait()
        block = blocks[r]

        def rows_step(i, carry):
            rows = pl.ds(pl.multiple_of(i * 32, 32), 32)
            states = hv[block, rows, :].astype(F32)
            inverse = lax.rsqrt(jnp.mean(states * states, axis=1, keepdims=True) + EPS)
            nv[block, rows, :] = (states * inverse * gain[...]).astype(BF)
            inv_out[block, rows, :] = jnp.broadcast_to(inverse, (32, 128))
            return carry

        lax.fori_loop(0, 12, rows_step, 0)
        keep(hv.at[block], h_out.at[block])
        keep(nv.at[block], n_out.at[block])

    def halo_on():
        wires.got(h_halo, halo_own)

        @pl.when(odd == 0)
        def _():
            pltpu.make_async_remote_copy(
                src_ref=halo_own,
                dst_ref=halo_own,
                send_sem=send.at[h_halo],
                recv_sem=recv.at[h_halo],
                device_id=info["e1"],
                device_id_type=MESH,
            ).start()

        wires.started.append((h_halo, hid))

    def c_rows(block, part, k):
        start = pl.multiple_of(part * 192 + k * COT_ROWS, COT_ROWS)
        return cv.at[block, pl.ds(start, COT_ROWS)]

    def c_send():
        for k in range(COT_PARTS):
            start = pl.multiple_of(mp * 192 + k * COT_ROWS, COT_ROWS)
            wires.put(c_e1[k], cot.at[pl.ds(start, COT_ROWS)], c_rows(odd, mp, k), info["e1"])

    def c_on(k):
        ref = c_rows(1 - odd, mp, k)
        wires.got(c_e1[k], ref)
        wires.put(c_near[k], ref, ref, info["near"])

    def c_got(k):
        wires.got(c_near[k], c_rows(1 - odd, 1 - mp, k))

    def first_hop(slots, first, way):
        layer = layer_from(way, 1)
        wires.got(slots[way][0], one(first, 2, layer, x))
        wires.got(slots[way][1], one(first, 2, layer, mate))

    def a_hop(hop, way):
        if hop == 1:
            first_hop(a_first, 0, way)
        else:
            take(a_own, own_pair, 0, way, hop)
        if hop < 4:
            pass_on(a_own, own_pair, 0, way, hop)

    def b_hop(hop, way):
        if hop == 1:
            first_hop(b_first, 2, way)
        else:
            take(b_own, own_pair, 2, way, hop)
        if hop < 4:
            pass_on(b_own, own_pair, 2, way, hop)
        lo, count = span(way, hop, 2)
        ref = own_pair(lo, count, layer_from(way, hop))
        wires.put(b_e2[2 * hop - 1 + way], ref, ref, info["e2"])

    def x_hop(hop, way):
        if hop == 0:
            wires.got(a_e2[0], one(0, 2, z, 3 - x))
            wires.got(a_e2[1], one(0, 2, z, 3 - mate))
            for way in range(2):
                pass_on(a_oth, other_pair, 0, way, 0)
        else:
            take(a_oth, other_pair, 0, way, hop)
            if hop < 4:
                pass_on(a_oth, other_pair, 0, way, hop)

    def e2_got(hop, way):
        if hop == 0:
            wires.got(b_e2[0][0], one(2, 2, z, 3 - x))
            wires.got(b_e2[0][1], one(2, 2, z, 3 - mate))
        else:
            lo, count = span(way, hop, 2)
            wires.got(b_e2[2 * hop - 1 + way], other_pair(lo, count, layer_from(way, hop)))

    def project(hop, count):
        def step(i, carry):
            way, block = i // 3, i % 3
            layer = (z + hop + way * (8 - 2 * hop)) % 8
            lanes = pl.ds(pl.multiple_of(layer * 256, 256), 256)
            rows = nv[block, :, lanes]
            for s in range(3):
                weight = wv[s, layer].reshape(256, 256)
                term = jnp.dot(rows, weight, preferred_element_type=F32)
                if hop == 0:
                    acc[s, block] = term
                else:
                    acc[s, block] += term
            return carry

        lax.fori_loop(0, 3 * count, step, 0)
        for layer in {0: (z,), 4: (layer_from(0, 4),)}.get(
            hop, (layer_from(0, hop), layer_from(1, hop))
        ):
            keep(wv.at[:, layer], w_out.at[:, layer])

    second(1, b_first, b_e2[0])
    from_near(0)
    from_far(0)
    b_hop(1, 0)
    second(0, a_first, a_e2)
    b_hop(1, 1)
    halo_on()
    c_send()
    e2_got(0, 0)
    a_hop(1, 1)
    b_hop(2, 0)
    spread(2, halo_own)
    wires.got(h_e1, cols(3 - b, hi, core, mp))
    spread(1, cols(3 - b, hi, core, mp))
    from_opp(0)
    a_hop(1, 0)
    e2_got(1, 0)
    b_hop(2, 1)
    x_hop(0, 0)
    from_twin(0)
    b_hop(3, 0)
    a_hop(2, 1)
    c_on(0)
    e2_got(1, 1)
    a_hop(2, 0)
    from_near(2)
    from_far(2)
    from_near(1)
    c_on(1)
    from_far(1)
    e2_got(2, 0)
    x_hop(1, 0)
    x_hop(1, 1)
    b_hop(3, 1)
    b_hop(4, 0)
    e2_got(2, 1)
    c_on(2)
    a_hop(3, 1)
    a_hop(3, 0)
    c_got(0)
    e2_got(3, 0)
    from_opp(2)
    x_hop(2, 0)
    c_on(3)
    b_hop(4, 1)
    x_hop(2, 1)
    from_opp(1)
    e2_got(3, 1)
    own_w.wait()
    from_twin(2)
    a_hop(4, 0)
    c_on(4)
    c_got(1)
    from_twin(1)
    a_hop(4, 1)
    c_on(5)
    x_hop(3, 0)
    x_hop(3, 1)
    project(0, 1)
    project(1, 2)
    e2_got(4, 0)
    e2_got(4, 1)
    c_got(2)
    project(2, 2)
    x_hop(4, 0)
    x_hop(4, 1)
    project(3, 2)
    project(4, 1)
    c_got(3)
    c_got(4)
    c_got(5)
    own_c.wait()
    keep(cv, c_out)

    def finish_block(block, carry):
        for s, out in ((0, q_out), (1, k_out), (2, v_out)):
            out[block] = acc[s, block].astype(BF)
        return carry

    lax.fori_loop(0, 3, finish_block, 0)

    def grad_block(block, carry):
        g_out[block] = jnp.dot(
            cv[block], wv[3].reshape(2048, 256), preferred_element_type=F32
        ).astype(BF)
        return carry

    lax.fori_loop(0, 2, grad_block, 0)
    wires.finish()
    for copy in kept:
        copy.wait()


def front(hid, ws, cot, gain):
    anywhere = pl.BlockSpec(memory_space=pl.ANY)
    in_vmem = pl.BlockSpec(memory_space=pltpu.VMEM)
    return pl.pallas_call(
        front_kernel,
        out_shape=(
            jax.ShapeDtypeStruct((3, 384, 256), BF),
            jax.ShapeDtypeStruct((3, 384, 256), BF),
            jax.ShapeDtypeStruct((3, 384, 256), BF),
            jax.ShapeDtypeStruct((2, 384, 256), BF),
            jax.ShapeDtypeStruct((3, 384, 128), F32),
            jax.ShapeDtypeStruct((3, 384, 2048), BF),
            jax.ShapeDtypeStruct((3, 384, 2048), BF),
            jax.ShapeDtypeStruct((4, 8, 4, 64, 256), BF),
            jax.ShapeDtypeStruct((2, 384, 2048), BF),
        ),
        in_specs=[anywhere] * 3 + [in_vmem],
        out_specs=(in_vmem,) * 5 + (anywhere,) * 4,
        scratch_shapes=[
            pltpu.VMEM((3, 384, 2048), BF),
            pltpu.VMEM((3, 384, 2048), BF),
            pltpu.VMEM((4, 8, 4, 64, 256), BF),
            pltpu.VMEM((2, 384, 2048), BF),
            pltpu.VMEM((3, 3, 384, 256), F32),
            pltpu.SemaphoreType.DMA((GATHER_SLOTS,)),
            pltpu.SemaphoreType.DMA((GATHER_SLOTS,)),
            pltpu.SemaphoreType.DMA((24,)),
        ],
        compiler_params=pltpu.CompilerParams(
            collective_id=0, has_side_effects=True, vmem_limit_bytes=VMEM_LIMIT
        ),
        name="front",
    )(hid, ws, cot, gain)


REDUCE_SLOTS = 70


def add(*terms):
    total = terms[0].astype(F32)
    for term in terms[1:]:
        total = total + term.astype(F32)
    return total.astype(BF)


def back_kernel(
    dqkv, attn, inv, gain, h_in, n_in, w_in, c_in,
    w_res, t_res,
    hv, nv, wv, cv, grads, trunk, scaled,
    a_got, a_out, b_e2got, b_got, b_out, a_fin, a_e2got, w_pair,
    t_twin, t_sum, t_far1, t_far2, t_near1, t_near2, t_mid1, t_mid2, t_fin, t_e1, t_halo, t_pass,
    send, recv, local,
):
    info = places()
    z, x, odd, p, q = (info[name] for name in ("z", "x", "odd", "pair", "quarter"))
    mp, core, hi = info["mp"], info["core"], info["hi"]
    wires = Wires(send, recv)
    ways = ("zp", "zm")
    loads = [
        pltpu.make_async_copy(src, dst, local.at[i])
        for i, (src, dst) in enumerate(((n_in, nv), (c_in, cv), (w_in, wv), (h_in, hv)))
    ]
    for load in loads:
        load.start()
    a_slot = [[wires.slot() for _ in range(4)] for _ in range(2)]
    b_slot = [[wires.slot() for _ in range(4)] for _ in range(2)]
    b_e2 = [wires.slot() for _ in range(8)]
    a_e2 = wires.slot()
    w_e1 = [wires.slot() for _ in range(2)]
    s_twin = [[wires.slot() for _ in range(2)] for _ in range(3)]
    s_far1, s_far2, s_near1, s_near2, s_near3 = (
        [wires.slot() for _ in range(3)] for _ in range(5)
    )
    s_e1 = wires.slot()
    s_half = wires.slot()
    s_halo = wires.slot()
    blocks = (0, 2 - odd, 1 + odd)
    top, low = pl.ds(0, 192), pl.ds(192, 192)

    greet(info)

    def to_layer(way, left):
        return (z + left) % 8 if way == 0 else (z + 8 - left) % 8

    def weight_grads(left, count):
        def step(way, carry):
            layer = (z + left + way * (8 - 2 * left)) % 8
            lanes = pl.ds(pl.multiple_of(layer * 256, 256), 256)
            rows = nv[:, lanes]
            triple = lax.dot_general(rows, dqkv[...], TN, preferred_element_type=F32)
            for s in range(3):
                grads[s, layer] = triple[:, s * 256 : (s + 1) * 256].astype(BF).reshape(4, 64, 256)
            last = lax.dot_general(cv[:, lanes], attn[...], TN, preferred_element_type=F32)
            grads[3, layer] = last.astype(BF).reshape(4, 64, 256)
            return carry

        lax.fori_loop(0, count, step, 0)

    def cross(k, way, left):
        wires.put(
            b_e2[k],
            grads.at[pl.ds(2, 2), to_layer(way, left), pl.ds(2 - 2 * p, 2)],
            b_e2got.at[k],
            info["e2"],
        )

    def state_grads(r):
        block = blocks[r]
        start = pl.multiple_of(block * 384, 384)
        factor = inv[block, :, 0:1]

        def first(c, carry):
            lanes = pl.ds(pl.multiple_of(c * 256, 256), 256)
            total = None
            for s in range(3):
                if r == 0 and s == 0:
                    continue
                term = lax.dot_general(
                    dqkv[pl.ds(start, 384), s * 256 : (s + 1) * 256],
                    wv[s, c].reshape(256, 256),
                    NT,
                    preferred_element_type=F32,
                )
                total = term if total is None else total + term
            total = total * gain[:, lanes]
            scaled[c] = total
            units = hv[block, :, lanes].astype(F32) * factor
            return carry + jnp.sum(total * units, axis=1, keepdims=True)

        mean = lax.fori_loop(0, 8, first, jnp.zeros((384, 1), F32)) * (1.0 / 2048)
        once = jnp.where(mp == 0, 1.0, 0.0)

        def second(c, carry):
            lanes = pl.ds(pl.multiple_of(c * 256, 256), 256)
            units = hv[block, :, lanes].astype(F32) * factor
            result = factor * (scaled[c] - units * mean)
            if r == 2:
                own = cv[pl.ds(pl.multiple_of(odd * 384, 384), 384), lanes]
                result = result + own.astype(F32) * once
            trunk[r, c] = result.astype(BF)
            return carry

        lax.fori_loop(0, 8, second, 0)
        for side in range(2):
            there = pl.ds((side * 2 + 1 - core) * 2, 2)
            wires.put(s_twin[r][side], trunk.at[r, there], t_twin.at[r, side], info["twin"])

    def fold_twin(r):
        for side in (0, 1):
            wires.got(s_twin[r][side], t_twin.at[r, side])
            t_sum[r, side] = add(trunk[r, pl.ds((side * 2 + core) * 2, 2)], t_twin[r, side])
        wires.put(s_far1[r], t_sum.at[r, 1 - hi, :, top], t_far1.at[r], info["far"])
        wires.put(s_near1[r], t_sum.at[r, hi, 1 - mp, low], t_near1.at[r, 0], info["near"])
        wires.put(s_near3[r], t_sum.at[r, 1 - hi, mp, low], t_near1.at[r, 1], info["near"])

    def fold_first(r):
        wires.got(s_far1[r], t_far1.at[r])
        t_mid1[r] = add(t_sum[r, hi, :, 0:192], t_far1[r])
        wires.put(s_near2[r], t_mid1.at[r, 1 - mp], t_near2.at[r], info["near"])
        wires.got(s_near3[r], t_near1.at[r, 1])
        t_mid2[r, 1] = add(t_sum[r, 1 - hi, 1 - mp, 192:384], t_near1[r, 1])
        wires.put(s_far2[r], t_mid2.at[r, 1], t_far2.at[r], info["far"])
        wires.got(s_near1[r], t_near1.at[r, 0])
        t_mid2[r, 0] = add(t_sum[r, hi, mp, 192:384], t_near1[r, 0])

    def fold_second(r):
        wires.got(s_near2[r], t_near2.at[r])
        t_fin[r, 0:192] = add(t_mid1[r, mp], t_near2[r])
        wires.got(s_far2[r], t_far2.at[r])
        t_fin[r, 192:384] = add(t_mid2[r, 0], t_far2[r])

    def a_step(way, step):
        layer = to_layer(way, 4 - step)
        if step == 1:
            wires.got(a_slot[way][0], a_got.at[way, 0, pl.ds(way, 1)])
            a_out[way, step, way] = add(grads[way, layer], a_got[way, 0, way])
            a_out[way, step, 1 - way] = grads[1 - way, layer]
        else:
            wires.got(a_slot[way][step - 1], a_got.at[way, step - 1])
            a_out[way, step] = add(grads[pl.ds(0, 2), layer], a_got[way, step - 1])
        wires.put(a_slot[way][step], a_out.at[way, step], a_got.at[way, step], info[ways[way]])

    def b_start(way, left, k):
        wires.got(b_e2[k], b_e2got.at[k])
        layer = to_layer(way, left)
        return add(grads[pl.ds(2, 2), layer, pl.ds(2 * p, 2)], b_e2got[k])

    def b_step(way, step):
        mine = b_start(way, 4 - step, 2 * step - 1 + way)
        if step == 1:
            wires.got(b_slot[way][0], b_got.at[way, 0, pl.ds(way, 1)])
            b_out[way, step, way] = add(mine[way], b_got[way, 0, way])
            b_out[way, step, 1 - way] = mine[1 - way]
        else:
            wires.got(b_slot[way][step - 1], b_got.at[way, step - 1])
            b_out[way, step] = add(mine, b_got[way, step - 1])
        wires.put(b_slot[way][step], b_out.at[way, step], b_got.at[way, step], info[ways[way]])

    loads[0].wait()
    loads[1].wait()
    weight_grads(4, 1)
    for way in range(2):
        wires.put(
            a_slot[way][0],
            grads.at[pl.ds(way, 1), to_layer(way, 4)],
            a_got.at[way, 0, pl.ds(way, 1)],
            info[ways[way]],
        )
    cross(0, 0, 4)
    weight_grads(3, 2)
    cross(1, 0, 3)
    cross(2, 1, 3)
    for way in range(2):
        a_step(way, 1)
    b_out[0, 0] = b_start(0, 4, 0)
    for way in range(2):
        wires.put(
            b_slot[way][0],
            b_out.at[0, 0, pl.ds(way, 1)],
            b_got.at[way, 0, pl.ds(way, 1)],
            info[ways[way]],
        )
    loads[2].wait()
    loads[3].wait()
    state_grads(0)
    weight_grads(2, 2)
    cross(3, 0, 2)
    cross(4, 1, 2)
    fold_twin(0)
    for way in range(2):
        b_step(way, 1)
    state_grads(1)
    for way in range(2):
        a_step(way, 2)
    weight_grads(1, 2)
    cross(5, 0, 1)
    cross(6, 1, 1)
    fold_twin(1)
    fold_first(0)
    state_grads(2)
    for way in range(2):
        b_step(way, 2)
    weight_grads(0, 1)
    cross(7, 0, 0)
    fold_twin(2)
    for way in range(2):
        a_step(way, 3)
    fold_second(0)

    @pl.when(odd == 1)
    def _():
        pltpu.make_async_remote_copy(
            src_ref=t_fin.at[0],
            dst_ref=t_halo,
            send_sem=send.at[s_half],
            recv_sem=recv.at[s_half],
            device_id=info["e1"],
            device_id_type=MESH,
        ).start()

    fold_first(1)
    for way in range(2):
        b_step(way, 3)

    @pl.when(odd == 0)
    def _():
        wires.got(s_half, t_halo)
        t_pass[...] = add(t_fin[0], t_halo[...])
        pltpu.make_async_remote_copy(
            src_ref=t_pass,
            dst_ref=t_halo,
            send_sem=send.at[s_halo],
            recv_sem=recv.at[s_halo],
            device_id=info["halo"],
            device_id_type=MESH,
        ).start()

    fold_second(1)
    wires.put(s_e1, t_fin.at[1], t_e1, info["e1"])
    fold_first(2)
    for way in range(2):
        wires.got(a_slot[way][3], a_got.at[way, 3])
    a_fin[...] = add(grads[pl.ds(0, 2), z], a_got[0, 3], a_got[1, 3])
    wires.put(a_e2, a_fin.at[:, pl.ds(2 - 2 * p, 2)], a_e2got, info["e2"])
    fold_second(2)
    last = b_start(0, 0, 7)
    for way in range(2):
        wires.got(b_slot[way][3], b_got.at[way, 3])
    w_pair[pl.ds(2, 2)] = add(last, b_got[0, 3], b_got[1, 3])
    wires.put(
        w_e1[1], w_pair.at[pl.ds(2, 2), 1 - odd], w_res.at[q, pl.ds(2, 2)], info["e1"]
    )
    wires.got(a_e2, a_e2got)
    w_pair[pl.ds(0, 2)] = add(a_fin[:, pl.ds(2 * p, 2)], a_e2got[...])
    wires.put(
        w_e1[0], w_pair.at[pl.ds(0, 2), 1 - odd], w_res.at[q, pl.ds(0, 2)], info["e1"]
    )
    w_res[q] = w_pair[:, odd]
    wires.got(s_e1, t_e1)

    @pl.when(odd == 0)
    def _():
        t_res[...] = add(t_fin[2], t_e1[...])
        pltpu.make_async_copy(t_pass, t_pass, send.at[s_halo]).wait()

    @pl.when(odd == 1)
    def _():
        wires.got(s_halo, t_halo)
        t_res[...] = add(t_fin[2], t_e1[...], t_halo[...])
        pltpu.make_async_copy(t_halo, t_halo, send.at[s_half]).wait()

    for part in range(2):
        wires.got(w_e1[part], w_res.at[1 - q, pl.ds(2 * part, 2)])
    wires.finish()


def back(dqkv, attn, inv, gain, hidden, normed, weights, upstream):
    anywhere = pl.BlockSpec(memory_space=pl.ANY)
    in_vmem = pl.BlockSpec(memory_space=pltpu.VMEM)
    shapes = [
        (3, 384, 2048), (1152, 2048), (4, 8, 4, 64, 256), (768, 2048), (4, 8, 4, 64, 256),
        (3, 8, 384, 256),
    ]
    more = [
        (2, 4, 2, 4, 64, 256), (2, 4, 2, 4, 64, 256), (8, 2, 2, 64, 256), (2, 4, 2, 2, 64, 256),
        (2, 4, 2, 2, 64, 256), (2, 4, 64, 256), (2, 2, 64, 256), (4, 2, 64, 256),
        (3, 2, 2, 384, 256), (3, 2, 2, 384, 256),
        (3, 2, 192, 256), (3, 192, 256), (3, 2, 192, 256), (3, 192, 256),
        (3, 2, 192, 256), (3, 2, 192, 256),
        (3, 384, 256), (384, 256), (384, 256), (384, 256),
    ]
    return pl.pallas_call(
        back_kernel,
        out_shape=(
            jax.ShapeDtypeStruct((2, 4, 64, 256), BF),
            jax.ShapeDtypeStruct((384, 256), BF),
        ),
        in_specs=[in_vmem] * 4 + [anywhere] * 4,
        out_specs=(in_vmem,) * 2,
        scratch_shapes=[pltpu.VMEM(shape, BF) for shape in shapes]
        + [pltpu.VMEM((8, 384, 256), F32)]
        + [pltpu.VMEM(shape, BF) for shape in more]
        + [
            pltpu.SemaphoreType.DMA((REDUCE_SLOTS,)),
            pltpu.SemaphoreType.DMA((REDUCE_SLOTS,)),
            pltpu.SemaphoreType.DMA((4,)),
        ],
        compiler_params=pltpu.CompilerParams(
            collective_id=1, has_side_effects=True, vmem_limit_bytes=VMEM_LIMIT
        ),
        name="back",
    )(dqkv, attn, inv, gain, hidden, normed, weights, upstream)


def attend_kernel(q_ref, k_ref, v_ref, g_ref, segk_ref, segq_ref, dqkv_ref, o_ref, dk_acc, dv_acc):
    scale = HD**-0.5
    dk_acc[...] = jnp.zeros_like(dk_acc)
    dv_acc[...] = jnp.zeros_like(dv_acc)
    dqkv_ref[0:384, 0:256] = jnp.zeros((384, 256), BF)
    lane_head = lax.broadcasted_iota(jnp.int32, (128, 256), 1) // HD

    def by_head(rows):
        return jnp.concatenate(
            [jnp.where(lane_head == h, rows, jnp.zeros_like(rows)) for h in range(4)], axis=0
        )

    def fold(wide):
        return jnp.concatenate(
            [wide[h * HD : (h + 1) * HD, h * 128 : (h + 1) * 128] for h in range(4)], axis=0
        ).T

    key_at = lax.broadcasted_iota(jnp.int32, (512, 128), 0)
    query_at = lax.broadcasted_iota(jnp.int32, (512, 128), 1) + 384
    causal = key_at <= query_at

    def tile(t, carry):
        start = pl.multiple_of(t * 128, 128)
        here, window = pl.ds(start, 128), pl.ds(start, 512)
        there = pl.ds(pl.multiple_of(start + 384, 128), 128)
        queries, grads = by_head(q_ref[there, :]), by_head(g_ref[here, :])
        keys, values = k_ref[window, :], v_ref[window, :]
        allowed = causal & (segk_ref[window, :] == segq_ref[t])
        allowed = jnp.concatenate([allowed] * 4, axis=1)
        scores = lax.dot_general(keys, queries, NT, preferred_element_type=F32) * scale
        scores = jnp.where(allowed, scores, MASKED)
        expo = jnp.exp(scores - jnp.max(scores, axis=0, keepdims=True))
        probs = expo * (1.0 / jnp.sum(expo, axis=0, keepdims=True))
        prob_rows = probs.astype(BF)
        prob_grad = lax.dot_general(values, grads, NT, preferred_element_type=F32)
        delta = jnp.sum(probs * prob_grad, axis=0, keepdims=True)
        score_grad = (probs * (prob_grad - delta) * scale).astype(BF)
        dv_acc[window, :] += jnp.dot(prob_rows, grads, preferred_element_type=F32)
        dk_acc[window, :] += jnp.dot(score_grad, queries, preferred_element_type=F32)
        o_ref[here, :] = fold(
            lax.dot_general(values, prob_rows, TN, preferred_element_type=F32)
        ).astype(BF)
        dqkv_ref[there, 0:256] = fold(
            lax.dot_general(keys, score_grad, TN, preferred_element_type=F32)
        ).astype(BF)
        return carry

    lax.fori_loop(0, 6, tile, 0)
    dqkv_ref[:, 256:512] = dk_acc[...].astype(BF)
    dqkv_ref[:, 512:768] = dv_acc[...].astype(BF)


def attend(queries, keys, values, attn_grad, seg_keys, seg_queries):
    return pl.pallas_call(
        attend_kernel,
        out_shape=(
            jax.ShapeDtypeStruct((1152, 768), BF),
            jax.ShapeDtypeStruct((768, 256), BF),
        ),
        scratch_shapes=[pltpu.VMEM((1152, 256), F32)] * 2,
        compiler_params=pltpu.CompilerParams(vmem_limit_bytes=VMEM_LIMIT),
        name="attend",
    )(queries, keys, values, attn_grad, seg_keys, seg_queries)


def per_device(hidden_states, norm_gain, qkv_weight, out_weight, cotangent, segment_ids):
    seq = lax.axis_index("seq")
    odd = seq % 2
    shard = jnp.concatenate(
        [jnp.transpose(qkv_weight[0], (1, 0, 2)), out_weight], axis=0
    )
    shard = jnp.transpose(shard.reshape(4, 64, 2, 256), (2, 0, 1, 3))
    gain = norm_gain.astype(F32)
    queries, keys, values, attn_grad, inverse, hidden, normed, weights, upstream = front(
        hidden_states, shard, cotangent[0], gain
    )

    first = (seq - odd) * 384 - 384
    seg = lax.dynamic_slice_in_dim(segment_ids, first + 384, 768)
    earlier = lax.dynamic_slice_in_dim(segment_ids, jnp.maximum(first, 0), 384)
    earlier = jnp.where(first >= 0, earlier, -1)
    seg_keys = jnp.concatenate([earlier, seg])[:, None]
    dqkv, attn_out = attend(
        queries.reshape(1152, 256),
        keys.reshape(1152, 256),
        values.reshape(1152, 256),
        attn_grad.reshape(768, 256),
        seg_keys,
        seg.reshape(6, 1, 128),
    )
    w_res, t_res = back(
        dqkv,
        attn_out,
        inverse,
        gain,
        hidden,
        normed.reshape(1152, 2048),
        weights,
        upstream.reshape(768, 2048),
    )
    merged = jnp.transpose(w_res, (1, 2, 0, 3)).reshape(4, 64, 512)
    return (t_res, jnp.transpose(merged[:3], (1, 0, 2))[None], merged[3][None])


def solution(mesh):
    placed = (
        P("seq", ("head", "mp")),
        P("head", None),
        P("head", "seq", None, "mp"),
        P("head", "seq", "mp"),
        P("head", "seq", None),
        P(),
    )
    return jax.shard_map(
        per_device,
        mesh=mesh,
        in_specs=placed,
        out_specs=(P("seq", ("head", "mp")), P("head", "seq", None, "mp"), P("head", "seq", "mp")),
        check_vma=False,
    )
```

time: 181 us -> 139 us (0.77)
  matrix products: 20.7 us -> 0 us
  other arithmetic: 15.9 us -> 3.08 us
  local copies, waits for them, and re-layouts: 13.5 us -> 7.83 us
    dot_general x11 -> x0, matrix products: 20.7 us -> none  [the longest x4 8 us: project(): return jnp.dot(rows, weight, preferred_element_type=F32).astype(BF)]
    convert_element_type x3 -> x1, other arithmetic: 10.1 us -> 1.3 us  [per_device(): gain = norm_gain.astype(F32)]
    slice x1 -> x0, local copies, waits for them, and re-layouts: 2.84 us -> none  [per_device(): attn_grad = project(upstream, weights[3])]
    unnamed x25 -> x3, local copies, waits for them, and re-layouts: 6.2 us -> 3.4 us
    another operation x1 -> x0, other arithmetic: 2.27 us -> none  [per_device(): jnp.stack([weight_grad(normed[384:], dq), weight_grad(normed, dk), weight...]
where the time goes in v2:
time: 139 us
  Pallas kernels  127 us (91%)
  local copies, waits for them, and re-layouts  7.83 us (6%)
  other arithmetic  3.08 us (2%)
    pallas_call x1, Pallas kernels, back(): pl.pallas_call(back_kernel, out_shape=(jax.ShapeDtypeStruct((2, 4, 64, 25...  58.9 us
    pallas_call x1, Pallas kernels, front(): pl.pallas_call(front_kernel, out_shape=(jax.ShapeDtypeStruct((3, 384, 256...  55.5 us
    pallas_call x1, Pallas kernels, attend(): pl.pallas_call(attend_kernel, out_shape=(jax.ShapeDtypeStruct((1152, 768)...  12.6 us
    unnamed x3, local copies, waits for them, and re-layouts  3.4 us

profile of v2, /device:TPU:4, one launch (start us, length us, event | category | flops | bytes accessed | tf_op | source)
XLA Modules:
  0.0 138.6 jit_solution(13061229391215074307)
XLA Ops:
  0.7 0.8 dynamic-slice_select_fusion
  1.4 0.8 dynamic_slice.7
  2.2 0.6 reshape.38.segq_ref
  2.8 1.3 convert_element_type.3.gain
  4.1 1.0 pad_maximum_fusion
  5.1 0.7 copy.17
  5.8 1.0 broadcast_in_dim.13.segk_ref
  6.8 55.5 %front.1 = (bf16[3,384,256]{2,1,0:T(8,128)(2,1)}, bf16[3,384,256]{2,1,0:T(8,128)(2,1)}, bf16[3,384,256]{2,1,0:T(8,128)(2,1)}, bf16[2,384,256]{2,1,0:T(8,128)(2,1...) custom-call(bf16[384,256]{1,0:T(8,128)(2,1)} %hid.1, ...), custom_call_target="tpu_custom_call" | custom-call | tf_op jit(solution)/shard_map/front/pallas_call | solution.py:440
  62.4 12.6 %attend.1 = (bf16[1152,768]{1,0:T(8,128)(2,1)}, bf16[768,256]{1,0:T(8,128)(2,1)}) custom-call(bf16[1152,256]{1,0:T(8,128)(2,1)} %bitcast.33, bf16[1152,256]{1,0:T(8,128)(2,1)} %bitcast.34, bf16[1152,256]{1,0:T(8,128)(2,1)} %bitcast.35, bf16[768,256]{1,0:T(8,128)(2,1)} %bitcast.36, s32[1152,1]{1,0:T(8,128)} %broadcast_in_dim.13.segk_ref, ...), custom_call_target="tpu_custom_call" | custom-call | tf_op jit(solution)/shard_map/attend/pallas_call | solution.py:844
  74.9 58.9 %back.1 = (bf16[2,4,64,256]{3,2,1,0:T(8,128)(2,1)}, bf16[384,256]{1,0:T(8,128)(2,1)}) custom-call(bf16[1152,768]{1,0:T(8,128)(2,1)} %get-tuple-element.20.dqkv, bf16[768,256]{1,0:T(8,128)(2,1)} %get-tuple-element.21.attn, f32[3,384,128]{2,1,0:T(8,128)} %get-tuple-element.22.inv, f32[1,2048]{1,0:T(1,128)} %convert_element_type.3.gain, ...), custom_call_target="tpu_custom_call" | custom-call | tf_op jit(solution)/shard_map/back/pallas_call | solution.py:768
  133.8 0.8 slice_bitcast_fusion.1
  134.7 0.9 slice_bitcast_fusion
  135.6 0.7 copy.14
  136.3 0.6 copy.15
  137.0 1.6 %copy.19 = bf16[384,256]{1,0:T(8,128)(2,1)} copy(bf16[384,256]{1,0:T(8,128)(2,1)} %get-tuple-element.32) | data formatting | bytes 393216
  (1 shorter events, 0.0 us)

commit v3 on v0

v3 whole, which is shorter than its diff:
```python
import functools

import jax
import jax.numpy as jnp
from jax import lax
from jax.experimental import pallas as pl
from jax.experimental.pallas import tpu as pltpu
from jax.sharding import PartitionSpec as P

HD = 64
EPS = 1e-05
MASKED = -1e30
MESH = pl.DeviceIdType.MESH
VMEM_LIMIT = 60 * 1024 * 1024
BF = jnp.bfloat16
F32 = jnp.float32


def places():
    head, seq, mp = (lax.axis_index(name) for name in ("head", "seq", "mp"))
    z, x = seq // 4, seq % 4
    odd = x % 2
    info = {
        "head": head,
        "mp": mp,
        "z": z,
        "x": x,
        "odd": odd,
        "pair": x // 2,
        "quarter": ((x + 1) // 2) % 2,
        "core": head % 2,
        "hi": head // 2,
        "e1": (head, seq + 1 - 2 * odd, mp),
        "e2": (head, z * 4 + 3 - x, mp),
        "zp": (head, ((z + 1) % 8) * 4 + x, mp),
        "zm": (head, ((z + 7) % 8) * 4 + x, mp),
        "near": (head, seq, 1 - mp),
        "far": ((head + 2) % 4, seq, 1 - mp),
        "twin": (head + 1 - 2 * (head % 2), seq, mp),
        "halo": (head, (seq + 31 + 2 * odd) % 32, mp),
    }
    return info


def greet(info):
    barrier = pltpu.get_barrier_semaphore()
    names = ("e1", "e2", "zp", "zm", "near", "far", "twin", "halo")
    for name in names:
        pl.semaphore_signal(barrier, inc=1, device_id=info[name], device_id_type=MESH)
    pl.semaphore_wait(barrier, len(names))


class Wires:
    def __init__(self, send, recv):
        self.send, self.recv, self.count = send, recv, 0
        self.started = []

    def slot(self):
        self.count += 1
        return self.count - 1

    def put(self, slot, src, dst, device):
        copy = pltpu.make_async_remote_copy(
            src_ref=src,
            dst_ref=dst,
            send_sem=self.send.at[slot],
            recv_sem=self.recv.at[slot],
            device_id=device,
            device_id_type=MESH,
        )
        copy.start()
        self.started.append((slot, src))

    def got(self, slot, dst):
        pltpu.make_async_copy(dst, dst, self.recv.at[slot]).wait()

    def finish(self):
        for slot, src in self.started:
            pltpu.make_async_copy(src, src, self.send.at[slot]).wait()


NT = (((1,), (1,)), ((), ()))
TN = (((0,), (0,)), ((), ()))
COT_PARTS = 6
COT_ROWS = 192 // COT_PARTS
SLOTS = 216


def add(*terms):
    total = terms[0].astype(F32)
    for term in terms[1:]:
        total = total + term.astype(F32)
    return total.astype(BF)


def kernel(
    hid, qkv, wo, cot, gain, seg,
    t_res, qkv_res, wo_res,
    ws, hv, nv, wv, cv, inv, acc, q_s, k_s, v_s, g_s, segk, dqkv, attn, grads,
    a_got, b_e2got, b_got, a_fin, a_e2got, w_pair, w_res,
    t_twin, t_far1, t_far2, t_near1, t_near2, t_mid1, t_mid2, t_fin, t_e1, t_halo, t_pass,
    send, recv, local,
):
    info = places()
    z, x, odd, p, q = (info[name] for name in ("z", "x", "odd", "pair", "quarter"))
    mp, core, hi = info["mp"], info["core"], info["hi"]
    seq = z * 4 + x
    wires = Wires(send, recv)
    ways = ("zp", "zm")
    mate = x + 1 - 2 * odd
    b = 1 + odd
    order = (b, 3 - b, 0)

    def cols(block, head_hi, head_core, part):
        start = pl.multiple_of(((head_hi * 2 + head_core) * 2 + part) * 256, 256)
        return hv.at[block, :, pl.ds(start, 256)]

    own_h = pltpu.make_async_copy(hid, cols(b, hi, core, mp), local.at[0])
    own_h.start()
    own_rows = pl.ds(pl.multiple_of(odd * 384, 384), 384)
    own_c = pltpu.make_async_copy(cot.at[0], cv.at[own_rows], local.at[1])
    own_c.start()
    for half in range(2):
        lanes = slice(half * 256, half * 256 + 256)
        for s in range(3):
            ws[half, s] = qkv[0, s, :, lanes]
        ws[half, 3] = wo[0, :, lanes]
    wv[:, z, x] = ws[q]

    greet(info)

    def slots(count):
        return [wires.slot() for _ in range(count)]

    w_e1 = slots(2)
    h_e1, h_halo = slots(2)
    h_near, h_far, h_opp = slots(3), slots(3), slots(3)
    h_twin = [slots(4) for _ in range(3)]
    w_z = {kind: [[slots(4) for _ in range(2)] for _ in range(2)] for kind in "ab"}
    x_z = [slots(4) for _ in range(2)]
    a_e2in = slots(2)
    b_e2in = [[slots(2)] + [None] * 4, [slots(2)] + [None] * 4]
    for way in range(2):
        for hop in range(1, 5):
            b_e2in[way][hop] = slots(2)
    c_e1, c_near = slots(COT_PARTS), slots(COT_PARTS)
    base = {"a": 0, "b": 2}

    def one(first, count, layer, place):
        return wv.at[pl.ds(first, count), layer, pl.ds(place, 1)]

    def other_pair(first, count, layer):
        return wv.at[pl.ds(first, count), layer, pl.ds(2 - 2 * p, 2)]

    def span(way, hop, first):
        return (first, 2) if hop < 4 else (first + way, 1)

    def layer_from(way, hop):
        return (z + 8 - hop) % 8 if way == 0 else (z + hop) % 8

    mine = cols(b, hi, core, mp)
    halo_own = cols(0, hi, core, mp)
    wires.put(h_e1, hid, mine, info["e1"])
    for half in (1, 0):
        arrs = pl.ds(2 * half, 2)
        wires.put(
            w_e1[half], ws.at[1 - q, arrs], wv.at[arrs, z, x], info["e1"]
        )
    for kind in "ba":
        arrs = pl.ds(base[kind], 2)
        for way in range(2):
            wires.put(w_z[kind][0][way][0], ws.at[q, arrs], wv.at[arrs, z, x], info[ways[way]])
    wires.put(a_e2in[0], ws.at[q, pl.ds(0, 2)], wv.at[pl.ds(0, 2), z, x], info["e2"])
    wires.put(b_e2in[0][0][0], ws.at[q, pl.ds(2, 2)], wv.at[pl.ds(2, 2), z, x], info["e2"])

    @pl.when(odd == 1)
    def _():
        pltpu.make_async_remote_copy(
            src_ref=hid,
            dst_ref=halo_own,
            send_sem=send.at[h_halo],
            recv_sem=recv.at[h_halo],
            device_id=info["halo"],
            device_id_type=MESH,
        ).start()

    def spread(r):
        dst = cols(order[r], hi, core, mp)
        if r == 1:
            wires.got(h_e1, dst)
        src = hid if r == 0 else dst
        wires.put(h_near[r], src, dst, info["near"])
        wires.put(h_far[r], src, dst, info["far"])
        wires.put(h_twin[r][0], src, dst, info["twin"])

    spread(0)

    def halo_on():
        wires.got(h_halo, halo_own)

        @pl.when(odd == 0)
        def _():
            pltpu.make_async_remote_copy(
                src_ref=halo_own,
                dst_ref=halo_own,
                send_sem=send.at[h_halo],
                recv_sem=recv.at[h_halo],
                device_id=info["e1"],
                device_id_type=MESH,
            ).start()

        wires.started.append((h_halo, hid))

    def from_near(r):
        got = cols(order[r], hi, core, 1 - mp)
        wires.got(h_near[r], got)
        wires.put(h_opp[r], got, got, info["far"])
        wires.put(h_twin[r][1], got, got, info["twin"])

    def from_far(r):
        got = cols(order[r], 1 - hi, core, 1 - mp)
        wires.got(h_far[r], got)
        wires.put(h_twin[r][2], got, got, info["twin"])

    def from_opp(r):
        got = cols(order[r], 1 - hi, core, mp)
        wires.got(h_opp[r], got)
        wires.put(h_twin[r][3], got, got, info["twin"])

    def from_twin(r):
        other = 1 - core
        wires.got(h_twin[r][0], cols(order[r], hi, other, mp))
        wires.got(h_twin[r][1], cols(order[r], hi, other, 1 - mp))
        wires.got(h_twin[r][2], cols(order[r], 1 - hi, other, 1 - mp))
        wires.got(h_twin[r][3], cols(order[r], 1 - hi, other, mp))
        if r == 0:
            own_h.wait()
        block = order[r]

        def rows_step(i, carry):
            rows = pl.ds(pl.multiple_of(i * 32, 32), 32)
            states = hv[block, rows, :].astype(F32)
            inverse = lax.rsqrt(jnp.mean(states * states, axis=1, keepdims=True) + EPS)
            there = pl.ds(pl.multiple_of(block * 384 + i * 32, 32), 32)
            nv[there, :] = (states * inverse * gain[...].astype(F32)).astype(BF)
            inv[block, rows, :] = jnp.broadcast_to(inverse, (32, 128))
            return carry

        lax.fori_loop(0, 12, rows_step, 0)

    def c_rows(block, part, k):
        start = pl.multiple_of(block * 384 + part * 192 + k * COT_ROWS, COT_ROWS)
        return cv.at[pl.ds(start, COT_ROWS)]

    def c_send(k):
        start = pl.multiple_of(mp * 192 + k * COT_ROWS, COT_ROWS)
        wires.put(c_e1[k], cot.at[0, pl.ds(start, COT_ROWS)], c_rows(odd, mp, k), info["e1"])

    def c_on(k):
        ref = c_rows(1 - odd, mp, k)
        wires.got(c_e1[k], ref)
        wires.put(c_near[k], ref, ref, info["near"])

    def c_got(k):
        wires.got(c_near[k], c_rows(1 - odd, 1 - mp, k))

    def second(half):
        kind, first = "ab"[half], 2 * half
        ref = one(first, 2, z, mate)
        wires.got(w_e1[half], wv.at[pl.ds(first, 2), z, mate])
        for way in range(2):
            wires.put(w_z[kind][1][way][0], ref, ref, info[ways[way]])
        wires.put(a_e2in[1] if half == 0 else b_e2in[0][0][1], ref, ref, info["e2"])

    def w_hop(kind, hop, way, member):
        place = (x, mate)[member]
        lo, count = span(way, hop, base[kind])
        layer = layer_from(way, hop)
        ref = one(lo, count, layer, place)
        wires.got(w_z[kind][member][way][hop - 1], ref)
        if hop < 4:
            lo, count = span(way, hop + 1, base[kind])
            on = one(lo, count, layer, place)
            wires.put(w_z[kind][member][way][hop], on, on, info[ways[way]])
        if kind == "b":
            wires.put(b_e2in[way][hop][member], ref, ref, info["e2"])

    def a_hop(hop, way, member):
        w_hop("a", hop, way, member)

    def b_hop(hop, way, member):
        w_hop("b", hop, way, member)

    def x_hop(hop, way):
        if hop == 0:
            wires.got(a_e2in[0], one(0, 2, z, 3 - x))
            wires.got(a_e2in[1], one(0, 2, z, 3 - mate))
            ref = other_pair(0, 2, z)
            for each in range(2):
                wires.put(x_z[each][0], ref, ref, info[ways[each]])
            return
        lo, count = span(way, hop, 0)
        layer = layer_from(way, hop)
        wires.got(x_z[way][hop - 1], other_pair(lo, count, layer))
        if hop < 4:
            lo, count = span(way, hop + 1, 0)
            on = other_pair(lo, count, layer)
            wires.put(x_z[way][hop], on, on, info[ways[way]])

    def e2_got(hop, way):
        lo, count = span(way, hop, 2)
        layer = layer_from(way, hop)
        wires.got(b_e2in[way][hop][0], one(lo, count, layer, 3 - x))
        wires.got(b_e2in[way][hop][1], one(lo, count, layer, 3 - mate))

    def project(hop, r):
        here = pl.ds(pl.multiple_of(order[r] * 384, 384), 384)

        def step(way, carry):
            layer = (z + hop + way * (8 - 2 * hop)) % 8
            lanes = pl.ds(pl.multiple_of(layer * 256, 256), 256)
            rows = nv[here, lanes]
            for s in range(1 if r == 2 else 0, 3):
                weight = wv[s, layer].reshape(256, 256)
                term = jnp.dot(rows, weight, preferred_element_type=F32)
                if hop == 0:
                    acc[s, here] = term
                else:
                    acc[s, here] += term
            return carry

        lax.fori_loop(0, 1 if hop in (0, 4) else 2, step, 0)

    def grad_block(block):
        rows = pl.ds(pl.multiple_of(block * 384, 384), 384)
        g_s[rows] = jnp.dot(
            cv[rows], wv[3].reshape(2048, 256), preferred_element_type=F32
        ).astype(BF)

    first_row = (seq - odd) * 3 - 3

    def seg_step(i, carry):
        row = first_row + i
        values = seg[pl.ds(jnp.maximum(row, 0), 1), :].astype(F32)
        values = jnp.where(row < 0, -1.0, values)
        segk[pl.ds(pl.multiple_of(i * 128, 128), 128), :] = jnp.broadcast_to(values, (128, 128)).T
        return carry

    lax.fori_loop(0, 9, seg_step, 0)

    b_hop(1, 0, 0)
    b_hop(1, 1, 0)
    a_hop(1, 0, 0)
    a_hop(1, 1, 0)
    from_near(0)
    b_hop(2, 0, 0)
    b_hop(2, 1, 0)
    from_far(0)
    spread(1)
    a_hop(2, 0, 0)
    a_hop(2, 1, 0)
    second(1)
    b_hop(3, 0, 0)
    b_hop(3, 1, 0)
    a_hop(3, 0, 0)
    a_hop(3, 1, 0)
    from_opp(0)
    second(0)
    b_hop(1, 0, 1)
    b_hop(1, 1, 1)
    from_near(1)
    halo_on()
    spread(2)
    c_send(0)
    c_send(1)
    c_send(2)
    c_send(3)
    a_hop(4, 0, 0)
    a_hop(4, 1, 0)
    a_hop(1, 0, 1)
    a_hop(1, 1, 1)
    b_hop(4, 0, 0)
    b_hop(4, 1, 0)
    c_send(4)
    c_send(5)
    from_far(1)
    e2_got(0, 0)
    b_hop(2, 0, 1)
    b_hop(2, 1, 1)
    from_twin(0)
    a_hop(2, 0, 1)
    a_hop(2, 1, 1)
    from_opp(1)
    x_hop(0, 0)
    project(0, 0)
    e2_got(1, 0)
    c_on(0)
    b_hop(3, 1, 1)
    from_near(2)
    a_hop(3, 0, 1)
    a_hop(3, 1, 1)
    b_hop(3, 0, 1)
    e2_got(1, 1)
    from_far(2)
    c_on(1)
    from_twin(1)
    e2_got(2, 0)
    c_got(0)
    project(0, 1)
    x_hop(1, 0)
    x_hop(1, 1)
    project(1, 1)
    e2_got(2, 1)
    a_hop(4, 0, 1)
    b_hop(4, 1, 1)
    c_on(2)
    project(1, 0)
    b_hop(4, 0, 1)
    a_hop(4, 1, 1)
    e2_got(3, 1)
    from_opp(2)
    c_got(1)
    e2_got(3, 0)
    c_on(3)
    e2_got(4, 1)
    x_hop(2, 0)
    x_hop(2, 1)
    project(2, 0)
    e2_got(4, 0)
    project(2, 1)
    c_got(2)
    c_on(4)
    from_twin(2)
    project(0, 2)
    project(1, 2)
    c_got(3)
    x_hop(3, 0)
    x_hop(3, 1)
    c_on(5)
    project(3, 2)
    project(2, 2)
    project(3, 1)
    project(3, 0)
    c_got(4)
    x_hop(4, 0)
    x_hop(4, 1)
    project(4, 1)
    project(4, 2)
    project(4, 0)
    c_got(5)
    own_c.wait()
    grad_block(odd)
    grad_block(1 - odd)
    wires.finish()
    wires.started = []

    def extract(i, carry):
        rows = pl.ds(pl.multiple_of(i * 128, 128), 128)
        q_s[rows] = (acc[0, rows] * HD**-0.5).astype(BF)
        k_s[rows] = acc[1, rows].astype(BF)
        v_s[rows] = acc[2, rows].astype(BF)
        acc[1, rows] = jnp.zeros((128, 256), F32)
        acc[2, rows] = jnp.zeros((128, 256), F32)
        return carry

    lax.fori_loop(0, 9, extract, 0)
    dqkv[0:384, 0:256] = jnp.zeros((384, 256), BF)
    lane_head = lax.broadcasted_iota(jnp.int32, (128, 256), 1) // HD

    def by_head(rows):
        return jnp.concatenate(
            [jnp.where(lane_head == h, rows, jnp.zeros_like(rows)) for h in range(4)], axis=0
        )

    def fold(wide):
        return jnp.concatenate(
            [wide[h * HD : (h + 1) * HD, h * 128 : (h + 1) * 128] for h in range(4)], axis=0
        ).T

    key_at = lax.broadcasted_iota(jnp.int32, (512, 128), 0)
    query_at = lax.broadcasted_iota(jnp.int32, (512, 128), 1) + 384
    causal = key_at <= query_at

    def tile(t, carry):
        start = pl.multiple_of(t * 128, 128)
        here, window = pl.ds(start, 128), pl.ds(start, 512)
        there = pl.ds(pl.multiple_of(start + 384, 128), 128)
        queries, out_grads = by_head(q_s[there, :]), by_head(g_s[here, :])
        keys, values = k_s[window, :], v_s[window, :]
        own_seg = seg[pl.ds(first_row + 3 + t, 1), :].astype(F32)
        allowed = causal & (segk[window, :] == own_seg)
        allowed = jnp.concatenate([allowed] * 4, axis=1)
        scores = lax.dot_general(keys, queries, NT, preferred_element_type=F32)
        scores = jnp.where(allowed, scores, MASKED)
        expo = jnp.exp(scores - jnp.max(scores, axis=0, keepdims=True))
        probs = expo * (1.0 / jnp.sum(expo, axis=0, keepdims=True))
        prob_rows = probs.astype(BF)
        prob_grad = lax.dot_general(values, out_grads, NT, preferred_element_type=F32)
        delta = jnp.sum(probs * prob_grad, axis=0, keepdims=True)
        score_grad = (probs * (prob_grad - delta)).astype(BF)
        acc[2, window] += jnp.dot(prob_rows, out_grads, preferred_element_type=F32)
        acc[1, window] += jnp.dot(score_grad, queries, preferred_element_type=F32)
        attn[here, :] = fold(
            lax.dot_general(values, prob_rows, TN, preferred_element_type=F32)
        ).astype(BF)
        dqkv[there, 0:256] = (
            fold(lax.dot_general(keys, score_grad, TN, preferred_element_type=F32)) * HD**-0.5
        ).astype(BF)
        return carry

    lax.fori_loop(0, 6, tile, 0)

    def pack(i, carry):
        rows = pl.ds(pl.multiple_of(i * 128, 128), 128)
        dqkv[rows, 256:512] = acc[1, rows].astype(BF)
        dqkv[rows, 512:768] = acc[2, rows].astype(BF)
        return carry

    lax.fori_loop(0, 9, pack, 0)

    a_slot, b_slot = ([slots(4) for _ in range(2)] for _ in range(2))
    b_e2 = slots(8)
    (a_e2,) = slots(1)
    r_e1 = slots(2)
    s_twin = [slots(2) for _ in range(3)]
    s_far1, s_far2, s_near1, s_near2, s_near3 = (slots(3) for _ in range(5))
    s_e1, s_half, s_halo = slots(3)
    blocks = (0, 2 - odd, 1 + odd)
    top, low = pl.ds(0, 192), pl.ds(192, 192)

    def to_layer(way, left):
        return (z + left) % 8 if way == 0 else (z + 8 - left) % 8

    def weight_grads(left, count):
        def step(way, carry):
            layer = (z + left + way * (8 - 2 * left)) % 8
            lanes = pl.ds(pl.multiple_of(layer * 256, 256), 256)
            triple = lax.dot_general(nv[:, lanes], dqkv[...], TN, preferred_element_type=F32)
            for s in range(3):
                grads[s, layer] = triple[:, s * 256 : (s + 1) * 256].astype(BF).reshape(4, 64, 256)
            last = lax.dot_general(cv[:, lanes], attn[...], TN, preferred_element_type=F32)
            grads[3, layer] = last.astype(BF).reshape(4, 64, 256)
            return carry

        lax.fori_loop(0, count, step, 0)

    def cross(k, way, left):
        wires.put(
            b_e2[k],
            grads.at[pl.ds(2, 2), to_layer(way, left), pl.ds(2 - 2 * p, 2)],
            b_e2got.at[k],
            info["e2"],
        )

    def w4():
        weight_grads(4, 1)
        for way in range(2):
            wires.put(
                a_slot[way][0],
                grads.at[pl.ds(way, 1), to_layer(way, 4)],
                a_got.at[way, 0, pl.ds(way, 1)],
                info[ways[way]],
            )
        cross(0, 0, 4)

    def w_part(left):
        weight_grads(left, 2 if left else 1)
        for way in range(2 if left else 1):
            cross(7 - 2 * left + way, way, left)

    def state_grads(r):
        block = blocks[r]
        start = pl.multiple_of(block * 384, 384)
        factor = inv[block, :, 0:1]

        def first(c, carry):
            lanes = pl.ds(pl.multiple_of(c * 256, 256), 256)
            total = None
            for s in range(1 if r == 0 else 0, 3):
                term = lax.dot_general(
                    dqkv[pl.ds(start, 384), s * 256 : (s + 1) * 256],
                    wv[s, c].reshape(256, 256),
                    NT,
                    preferred_element_type=F32,
                )
                total = term if total is None else total + term
            total = total * gain[:, lanes].astype(F32)
            acc[c // 3, pl.ds(pl.multiple_of((c % 3) * 384, 384), 384)] = total
            units = hv[block, :, lanes].astype(F32) * factor
            return carry + jnp.sum(total * units, axis=1, keepdims=True)

        mean = lax.fori_loop(0, 8, first, jnp.zeros((384, 1), F32)) * (1.0 / 2048)
        once = jnp.where(mp == 0, 1.0, 0.0)

        def final(c, carry):
            lanes = pl.ds(pl.multiple_of(c * 256, 256), 256)
            units = hv[block, :, lanes].astype(F32) * factor
            scaled = acc[c // 3, pl.ds(pl.multiple_of((c % 3) * 384, 384), 384)]
            result = factor * (scaled - units * mean)
            if r == 2:
                result = result + cv[own_rows, lanes].astype(F32) * once
            hv[block, :, lanes] = result.astype(BF)
            return carry

        lax.fori_loop(0, 8, final, 0)
        for side in range(2):
            lanes = pl.ds(pl.multiple_of(side * 1024 + (1 - core) * 512, 512), 512)
            wires.put(s_twin[r][side], hv.at[block, :, lanes], t_twin.at[r, side], info["twin"])

    def fold_twin(r):
        for side in (0, 1):
            lanes = pl.ds(pl.multiple_of(side * 1024 + core * 512, 512), 512)
            wires.got(s_twin[r][side], t_twin.at[r, side])
            t_twin[r, side] = add(t_twin[r, side], hv[blocks[r], :, lanes])
        wires.put(s_far1[r], t_twin.at[r, 1 - hi, top], t_far1.at[r], info["far"])
        there = pl.ds(pl.multiple_of((1 - mp) * 256, 256), 256)
        wires.put(s_near1[r], t_twin.at[r, hi, low, there], t_near1.at[r, 0], info["near"])
        there = pl.ds(pl.multiple_of(mp * 256, 256), 256)
        wires.put(s_near3[r], t_twin.at[r, 1 - hi, low, there], t_near1.at[r, 1], info["near"])

    def fold_far(r):
        wires.got(s_far1[r], t_far1.at[r])
        for part in range(2):
            lanes = slice(part * 256, part * 256 + 256)
            t_mid1[r, part] = add(t_twin[r, hi, 0:192, lanes], t_far1[r, :, lanes])
        wires.put(s_near2[r], t_mid1.at[r, 1 - mp], t_near2.at[r], info["near"])

    def fold_near(r):
        wires.got(s_near3[r], t_near1.at[r, 1])
        there = pl.ds(pl.multiple_of((1 - mp) * 256, 256), 256)
        t_mid2[r, 1] = add(t_twin[r, 1 - hi, 192:384, there], t_near1[r, 1])
        wires.put(s_far2[r], t_mid2.at[r, 1], t_far2.at[r], info["far"])
        wires.got(s_near1[r], t_near1.at[r, 0])
        there = pl.ds(pl.multiple_of(mp * 256, 256), 256)
        t_mid2[r, 0] = add(t_twin[r, hi, 192:384, there], t_near1[r, 0])

    def fold_second(r):
        wires.got(s_near2[r], t_near2.at[r])
        t_fin[r, 0:192] = add(t_mid1[r, mp], t_near2[r])
        wires.got(s_far2[r], t_far2.at[r])
        t_fin[r, 192:384] = add(t_mid2[r, 0], t_far2[r])
        if r == 0:
            @pl.when(odd == 1)
            def _():
                pltpu.make_async_remote_copy(
                    src_ref=t_fin.at[0],
                    dst_ref=t_halo,
                    send_sem=send.at[s_half],
                    recv_sem=recv.at[s_half],
                    device_id=info["e1"],
                    device_id_type=MESH,
                ).start()

        if r == 1:
            wires.put(s_e1, t_fin.at[1], t_e1, info["e1"])

    def halo_pass():
        @pl.when(odd == 0)
        def _():
            wires.got(s_half, t_halo)
            t_pass[...] = add(t_fin[0], t_halo[...])
            pltpu.make_async_remote_copy(
                src_ref=t_pass,
                dst_ref=t_halo,
                send_sem=send.at[s_halo],
                recv_sem=recv.at[s_halo],
                device_id=info["halo"],
                device_id_type=MESH,
            ).start()

    def a_step(way, step):
        layer = to_layer(way, 4 - step)
        if step == 1:
            wires.got(a_slot[way][0], a_got.at[way, 0, pl.ds(way, 1)])
            a_got[way, 0, way] = add(grads[way, layer], a_got[way, 0, way])
            a_got[way, 0, 1 - way] = grads[1 - way, layer]
        else:
            wires.got(a_slot[way][step - 1], a_got.at[way, step - 1])
            a_got[way, step - 1] = add(grads[pl.ds(0, 2), layer], a_got[way, step - 1])
        wires.put(a_slot[way][step], a_got.at[way, step - 1], a_got.at[way, step], info[ways[way]])

    def b_start(way, left, k):
        wires.got(b_e2[k], b_e2got.at[k])
        layer = to_layer(way, left)
        return add(grads[pl.ds(2, 2), layer, pl.ds(2 * p, 2)], b_e2got[k])

    def b_begin():
        b_e2got[0] = b_start(0, 4, 0)
        for way in range(2):
            wires.put(
                b_slot[way][0],
                b_e2got.at[0, pl.ds(way, 1)],
                b_got.at[way, 0, pl.ds(way, 1)],
                info[ways[way]],
            )

    def b_step(way, step):
        added = b_start(way, 4 - step, 2 * step - 1 + way)
        if step == 1:
            wires.got(b_slot[way][0], b_got.at[way, 0, pl.ds(way, 1)])
            b_got[way, 0, way] = add(added[way], b_got[way, 0, way])
            b_got[way, 0, 1 - way] = added[1 - way]
        else:
            wires.got(b_slot[way][step - 1], b_got.at[way, step - 1])
            b_got[way, step - 1] = add(added, b_got[way, step - 1])
        wires.put(b_slot[way][step], b_got.at[way, step - 1], b_got.at[way, step], info[ways[way]])

    def a_finish():
        for way in range(2):
            wires.got(a_slot[way][3], a_got.at[way, 3])
        a_fin[...] = add(grads[pl.ds(0, 2), z], a_got[0, 3], a_got[1, 3])
        wires.put(a_e2, a_fin.at[:, pl.ds(2 - 2 * p, 2)], a_e2got, info["e2"])

    def b_finish():
        last = b_start(0, 0, 7)
        for way in range(2):
            wires.got(b_slot[way][3], b_got.at[way, 3])
        w_pair[pl.ds(2, 2)] = add(last, b_got[0, 3], b_got[1, 3])
        wires.put(
            r_e1[1], w_pair.at[pl.ds(2, 2), 1 - odd], w_res.at[q, pl.ds(2, 2)], info["e1"]
        )
        w_res[q, pl.ds(2, 2)] = w_pair[pl.ds(2, 2), odd]

    def a_end():
        wires.got(a_e2, a_e2got)
        w_pair[pl.ds(0, 2)] = add(a_fin[:, pl.ds(2 * p, 2)], a_e2got[...])
        wires.put(
            r_e1[0], w_pair.at[pl.ds(0, 2), 1 - odd], w_res.at[q, pl.ds(0, 2)], info["e1"]
        )
        w_res[q, pl.ds(0, 2)] = w_pair[pl.ds(0, 2), odd]

    def w_end():
        for part in range(2):
            wires.got(r_e1[part], w_res.at[1 - q, pl.ds(2 * part, 2)])
        for half in range(2):
            lanes = slice(half * 256, half * 256 + 256)
            for s in range(3):
                qkv_res[0, s, :, lanes] = w_res[half, s]
            wo_res[0, :, lanes] = w_res[half, 3]

    def t_end():
        wires.got(s_e1, t_e1)

        @pl.when(odd == 0)
        def _():
            t_res[...] = add(t_fin[2], t_e1[...])
            pltpu.make_async_copy(t_pass, t_pass, send.at[s_halo]).wait()

        @pl.when(odd == 1)
        def _():
            wires.got(s_halo, t_halo)
            t_res[...] = add(t_fin[2], t_e1[...], t_halo[...])
            pltpu.make_async_copy(t_halo, t_halo, send.at[s_half]).wait()

    w4()
    w_part(3)
    state_grads(0)
    a_step(1, 1)
    a_step(0, 1)
    b_begin()
    w_part(2)
    fold_twin(0)
    w_part(1)
    state_grads(1)
    a_step(0, 2)
    a_step(1, 2)
    b_step(1, 1)
    b_step(0, 1)
    fold_near(0)
    fold_far(0)
    state_grads(2)
    fold_twin(1)
    fold_second(0)
    w_part(0)
    a_step(0, 3)
    a_step(1, 3)
    fold_twin(2)
    b_step(0, 2)
    b_step(1, 2)
    fold_near(1)
    halo_pass()
    fold_far(1)
    fold_near(2)
    fold_far(2)
    a_finish()
    fold_second(1)
    b_step(0, 3)
    b_step(1, 3)
    fold_second(2)
    a_end()
    b_finish()
    t_end()
    w_end()
    wires.finish()


def hand_over(a_ref, b_ref, c_ref, a_out, b_out, c_out):
    a_out[...] = a_ref[...]
    b_out[...] = b_ref[...]
    c_out[...] = c_ref[...]


def per_device(hidden_states, norm_gain, qkv_weight, out_weight, cotangent, segment_ids):
    anywhere = pl.BlockSpec(memory_space=pl.ANY)
    in_vmem = pl.BlockSpec(memory_space=pltpu.VMEM)
    first = [
        (2, 4, 64, 256), (3, 384, 2048), (1152, 2048), (4, 8, 4, 64, 256), (768, 2048),
    ]
    wide = [(3, 384, 128), (3, 1152, 256)]
    heads = [(1152, 256), (1152, 256), (1152, 256), (768, 256)]
    later = [
        (1152, 768), (768, 256), (4, 8, 4, 64, 256),
        (2, 4, 2, 4, 64, 256), (8, 2, 2, 64, 256), (2, 4, 2, 2, 64, 256),
        (2, 4, 64, 256), (2, 2, 64, 256), (4, 2, 64, 256), (2, 4, 64, 256),
        (3, 2, 384, 512), (3, 192, 512), (3, 192, 256), (3, 2, 192, 256), (3, 192, 256),
        (3, 2, 192, 256), (3, 2, 192, 256),
        (3, 384, 256), (384, 256), (384, 256), (384, 256),
    ]

    def vmem(shapes, dtype):
        return [pltpu.VMEM(shape, dtype) for shape in shapes]

    results = pl.pallas_call(
        kernel,
        out_shape=(
            jax.ShapeDtypeStruct((384, 256), BF),
            jax.ShapeDtypeStruct((1, 3, 64, 512), BF),
            jax.ShapeDtypeStruct((1, 64, 512), BF),
        ),
        in_specs=[anywhere, in_vmem, in_vmem, anywhere, in_vmem, in_vmem],
        out_specs=(in_vmem,) * 3,
        scratch_shapes=vmem(first, BF)
        + vmem(wide, F32)
        + vmem(heads, BF)
        + vmem([(1152, 128)], F32)
        + vmem(later, BF)
        + [
            pltpu.SemaphoreType.DMA((SLOTS,)),
            pltpu.SemaphoreType.DMA((SLOTS,)),
            pltpu.SemaphoreType.DMA((2,)),
        ],
        compiler_params=pltpu.CompilerParams(
            collective_id=0, has_side_effects=True, vmem_limit_bytes=VMEM_LIMIT
        ),
        name="whole",
    )(
        hidden_states,
        jnp.transpose(qkv_weight, (0, 2, 1, 3)),
        out_weight,
        cotangent,
        norm_gain,
        segment_ids.reshape(96, 128),
    )
    trunk_grad, qkv_grad, out_grad = pl.pallas_call(
        hand_over,
        out_shape=tuple(jax.ShapeDtypeStruct(result.shape, BF) for result in results),
        in_specs=[in_vmem] * 3,
        out_specs=(in_vmem,) * 3,
        name="hand_over",
    )(*results)
    return (trunk_grad, jnp.transpose(qkv_grad, (0, 2, 1, 3)), out_grad)


def solution(mesh):
    placed = (
        P("seq", ("head", "mp")),
        P("head", None),
        P("head", "seq", None, "mp"),
        P("head", "seq", "mp"),
        P("head", "seq", None),
        P(),
    )
    return jax.shard_map(
        per_device,
        mesh=mesh,
        in_specs=placed,
        out_specs=(P("seq", ("head", "mp")), P("head", "seq", None, "mp"), P("head", "seq", "mp")),
        check_vma=False,
    )
```

time: 751 us -> 119 us (0.16)
  waiting for transfers between devices: 589 us -> 0 us
  Pallas kernels: 0 us -> 118 us
  matrix products: 98.9 us -> 0 us
  other arithmetic: 25.9 us -> 0 us
  local copies, waits for them, and re-layouts: 15.1 us -> 0 us
  between operations: 14.6 us -> 0.64 us
    reduce_scatter x2 -> x0, waiting for transfers between devices: 266 us -> none  [the longest x1 228 us: per_device(): lax.psum_scatter(jnp.einsum('tc,tse->cse', columns, triple_matrix_sensiti...]
    all_gather x3 -> x0, waiting for transfers between devices: 199 us -> none  [the longest x1 89.1 us: per_device(): lax.all_gather(qkv_weight[0], 'seq', axis=0, tiled=True)]
    unnamed x7 -> x0, waiting for transfers between devices: 124 us -> none
    pallas_call x0 -> x2, Pallas kernels: none -> 118 us  [the longest x1 117 us: per_device(): pl.pallas_call(kernel, out_shape=(jax.ShapeDtypeStruct((384, 256), BF), j...]
    dot_general x17 -> x0, matrix products: 98.9 us -> none  [the longest x2 31.1 us: attend(): jnp.einsum('hqk,khd->qhd', score_grad, key_rows, preferred_element_type=j...]
    sub x2 -> x0, other arithmetic: 8.51 us -> none  [attend(): expo = jnp.exp(scores - row_max)]
  transfers between devices with their start and end apart: 8 -> 0, of which waited for: 6 -> 0; matrix products, arithmetic and copies ran while one was open for 14% -> 0% of each run, Pallas kernels for 0% -> 0%
where the time goes in v3:
time: 119 us
  Pallas kernels  118 us (99%)
    pallas_call x1, Pallas kernels, per_device(): pl.pallas_call(kernel, out_shape=(jax.ShapeDtypeStruct((384, 256), BF), j...  117 us

profile of v3, /device:TPU:4, one launch (start us, length us, event | category | flops | bytes accessed | tf_op | source)
XLA Modules:
  0.0 119.1 jit_solution(13808242930356585660)
XLA Ops:
  0.6 116.6 %whole.1 = (bf16[384,256]{1,0:T(8,128)(2,1)}, bf16[1,3,64,512]{3,2,1,0:T(8,128)(2,1)}, bf16[1,64,512]{2,1,0:T(8,128)(2,1)}) custom-call(bf16[384,256]{1,0:T(8,128)(2,1)} %hid.1, bf16[1,3,64,512]{3,2,1,0:T(8,128)(2,1)} %bitcast.3, bf16[1,64,512]{2,1,0:T(8,128)(2,1)} %wo.1, bf16[1,384,2048]{2,1,0:T(8,128)(2,1)} %cot.1, bf16[1,2048]{1,0:T(2,128)(2,1)} %gain.1, ...), custom_call_target="tpu_custom_call" | custom-call | tf_op jit(solution)/shard_map/whole/pallas_call | solution.py:823
  117.3 1.8 %hand_over.1 = (bf16[384,256]{1,0:T(8,128)(2,1)}, bf16[1,3,64,512]{3,2,1,0:T(8,128)(2,1)}, bf16[1,64,512]{2,1,0:T(8,128)(2,1)}) custom-call(bf16[384,256]{1,0:T(8,128)(2,1)} %get-tuple-element.9.a_ref, bf16[1,3,64,512]{3,2,1,0:T(8,128)(2,1)} %get-tuple-element.10.b_ref, bf16[1,64,512]{2,1,0:T(8,128)(2,1)} %get-tuple-element.11.c_ref), custom_call_target="tpu_custom_call" | custom-call | tf_op jit(solution)/shard_map/hand_over/pallas_call | solution.py:854

commit v4 on v3

--- a/solution.py
+++ b/solution.py
@@ -81,9 +81,10 @@
 
 NT = (((1,), (1,)), ((), ()))
 TN = (((0,), (0,)), ((), ()))
-COT_PARTS = 6
+COT_PARTS = 4
 COT_ROWS = 192 // COT_PARTS
-SLOTS = 216
+SLOTS = 160
+Q, K, V, O = 2, 3, 0, 1
 
 
 def add(*terms):
@@ -96,7 +97,7 @@
 def kernel(
     hid, qkv, wo, cot, gain, seg,
     t_res, qkv_res, wo_res,
-    ws, hv, nv, wv, cv, inv, acc, q_s, k_s, v_s, g_s, segk, dqkv, attn, grads,
+    ws, hv, nv, wv, cv, inv, acc, q_s, k_s, v_s, g_s, segk, means, probs, dqkv, attn, grads,
     a_got, b_e2got, b_got, a_fin, a_e2got, w_pair, w_res,
     t_twin, t_far1, t_far2, t_near1, t_near2, t_mid1, t_mid2, t_fin, t_e1, t_halo, t_pass,
     send, recv, local,
@@ -123,8 +124,8 @@
     for half in range(2):
         lanes = slice(half * 256, half * 256 + 256)
         for s in range(3):
-            ws[half, s] = qkv[0, s, :, lanes]
-        ws[half, 3] = wo[0, :, lanes]
+            ws[half, (Q, K, V)[s]] = qkv[0, s, :, lanes]
+        ws[half, O] = wo[0, :, lanes]
     wv[:, z, x] = ws[q]
 
     greet(info)
@@ -132,19 +133,15 @@
     def slots(count):
         return [wires.slot() for _ in range(count)]
 
-    w_e1 = slots(2)
+    (w_e1,) = slots(1)
     h_e1, h_halo = slots(2)
     h_near, h_far, h_opp = slots(3), slots(3), slots(3)
-    h_twin = [slots(4) for _ in range(3)]
-    w_z = {kind: [[slots(4) for _ in range(2)] for _ in range(2)] for kind in "ab"}
+    h_twin = [slots(2) for _ in range(3)]
+    w_z = [[slots(4) for _ in range(2)] for _ in range(2)]
     x_z = [slots(4) for _ in range(2)]
-    a_e2in = slots(2)
-    b_e2in = [[slots(2)] + [None] * 4, [slots(2)] + [None] * 4]
-    for way in range(2):
-        for hop in range(1, 5):
-            b_e2in[way][hop] = slots(2)
+    first_e2 = slots(2)
+    b_e2in = [slots(5) for _ in range(2)]
     c_e1, c_near = slots(COT_PARTS), slots(COT_PARTS)
-    base = {"a": 0, "b": 2}
 
     def one(first, count, layer, place):
         return wv.at[pl.ds(first, count), layer, pl.ds(place, 1)]
@@ -152,26 +149,24 @@
     def other_pair(first, count, layer):
         return wv.at[pl.ds(first, count), layer, pl.ds(2 - 2 * p, 2)]
 
-    def span(way, hop, first):
-        return (first, 2) if hop < 4 else (first + way, 1)
+    def own_pair(first, count, layer):
+        return wv.at[pl.ds(first, count), layer, pl.ds(2 * p, 2)]
+
+    def span(way, hop, count):
+        return (0, count) if hop < 4 else (way * count // 2, count // 2)
 
     def layer_from(way, hop):
         return (z + 8 - hop) % 8 if way == 0 else (z + hop) % 8
 
     mine = cols(b, hi, core, mp)
     halo_own = cols(0, hi, core, mp)
+    wires.put(w_e1, ws.at[1 - q], wv.at[:, z, x], info["e1"])
     wires.put(h_e1, hid, mine, info["e1"])
-    for half in (1, 0):
-        arrs = pl.ds(2 * half, 2)
-        wires.put(
-            w_e1[half], ws.at[1 - q, arrs], wv.at[arrs, z, x], info["e1"]
-        )
-    for kind in "ba":
-        arrs = pl.ds(base[kind], 2)
-        for way in range(2):
-            wires.put(w_z[kind][0][way][0], ws.at[q, arrs], wv.at[arrs, z, x], info[ways[way]])
-    wires.put(a_e2in[0], ws.at[q, pl.ds(0, 2)], wv.at[pl.ds(0, 2), z, x], info["e2"])
-    wires.put(b_e2in[0][0][0], ws.at[q, pl.ds(2, 2)], wv.at[pl.ds(2, 2), z, x], info["e2"])
+    own_rows_w = ws.at[q]
+    own_place = wv.at[:, z, x]
+    for way in range(2):
+        wires.put(w_z[0][way][0], own_rows_w, own_place, info[ways[way]])
+    wires.put(first_e2[0], own_rows_w, own_place, info["e2"])
 
     @pl.when(odd == 1)
     def _():
@@ -191,9 +186,12 @@
         src = hid if r == 0 else dst
         wires.put(h_near[r], src, dst, info["near"])
         wires.put(h_far[r], src, dst, info["far"])
-        wires.put(h_twin[r][0], src, dst, info["twin"])
 
     spread(0)
+
+    def half_cols(block, head_hi, head_core):
+        start = pl.multiple_of((head_hi * 2 + head_core) * 512, 512)
+        return hv.at[block, :, pl.ds(start, 512)]
 
     def halo_on():
         wires.got(h_halo, halo_own)
@@ -215,26 +213,20 @@
         got = cols(order[r], hi, core, 1 - mp)
         wires.got(h_near[r], got)
         wires.put(h_opp[r], got, got, info["far"])
-        wires.put(h_twin[r][1], got, got, info["twin"])
-
-    def from_far(r):
-        got = cols(order[r], 1 - hi, core, 1 - mp)
-        wires.got(h_far[r], got)
-        wires.put(h_twin[r][2], got, got, info["twin"])
-
-    def from_opp(r):
-        got = cols(order[r], 1 - hi, core, mp)
-        wires.got(h_opp[r], got)
-        wires.put(h_twin[r][3], got, got, info["twin"])
-
-    def from_twin(r):
-        other = 1 - core
-        wires.got(h_twin[r][0], cols(order[r], hi, other, mp))
-        wires.got(h_twin[r][1], cols(order[r], hi, other, 1 - mp))
-        wires.got(h_twin[r][2], cols(order[r], 1 - hi, other, 1 - mp))
-        wires.got(h_twin[r][3], cols(order[r], 1 - hi, other, mp))
         if r == 0:
             own_h.wait()
+        both = half_cols(order[r], hi, core)
+        wires.put(h_twin[r][0], both, both, info["twin"])
+
+    def from_far(r):
+        wires.got(h_far[r], cols(order[r], 1 - hi, core, 1 - mp))
+        wires.got(h_opp[r], cols(order[r], 1 - hi, core, mp))
+        both = half_cols(order[r], 1 - hi, core)
+        wires.put(h_twin[r][1], both, both, info["twin"])
+
+    def from_twin(r):
+        wires.got(h_twin[r][0], half_cols(order[r], hi, 1 - core))
+        wires.got(h_twin[r][1], half_cols(order[r], 1 - hi, 1 - core))
         block = order[r]
 
         def rows_step(i, carry):
@@ -264,54 +256,44 @@
     def c_got(k):
         wires.got(c_near[k], c_rows(1 - odd, 1 - mp, k))
 
-    def second(half):
-        kind, first = "ab"[half], 2 * half
-        ref = one(first, 2, z, mate)
-        wires.got(w_e1[half], wv.at[pl.ds(first, 2), z, mate])
+    def second():
+        ref = wv.at[:, z, mate]
+        wires.got(w_e1, ref)
+        wires.put(first_e2[1], ref, ref, info["e2"])
         for way in range(2):
-            wires.put(w_z[kind][1][way][0], ref, ref, info[ways[way]])
-        wires.put(a_e2in[1] if half == 0 else b_e2in[0][0][1], ref, ref, info["e2"])
-
-    def w_hop(kind, hop, way, member):
+            wires.put(w_z[1][way][0], ref, ref, info[ways[way]])
+
+    def w_hop(hop, way, member):
         place = (x, mate)[member]
-        lo, count = span(way, hop, base[kind])
         layer = layer_from(way, hop)
-        ref = one(lo, count, layer, place)
-        wires.got(w_z[kind][member][way][hop - 1], ref)
+        lo, count = span(way, hop, 4)
+        wires.got(w_z[member][way][hop - 1], one(lo, count, layer, place))
         if hop < 4:
-            lo, count = span(way, hop + 1, base[kind])
+            lo, count = span(way, hop + 1, 4)
             on = one(lo, count, layer, place)
-            wires.put(w_z[kind][member][way][hop], on, on, info[ways[way]])
-        if kind == "b":
-            wires.put(b_e2in[way][hop][member], ref, ref, info["e2"])
-
-    def a_hop(hop, way, member):
-        w_hop("a", hop, way, member)
-
-    def b_hop(hop, way, member):
-        w_hop("b", hop, way, member)
+            wires.put(w_z[member][way][hop], on, on, info[ways[way]])
+        if member == 1 and (hop < 4 or way == 1):
+            ref = own_pair(2, 2, layer)
+            wires.put(b_e2in[way][hop], ref, ref, info["e2"])
 
     def x_hop(hop, way):
         if hop == 0:
-            wires.got(a_e2in[0], one(0, 2, z, 3 - x))
-            wires.got(a_e2in[1], one(0, 2, z, 3 - mate))
+            wires.got(first_e2[0], wv.at[:, z, 3 - x])
+            wires.got(first_e2[1], wv.at[:, z, 3 - mate])
             ref = other_pair(0, 2, z)
             for each in range(2):
                 wires.put(x_z[each][0], ref, ref, info[ways[each]])
             return
-        lo, count = span(way, hop, 0)
+        lo, count = span(way, hop, 2)
         layer = layer_from(way, hop)
         wires.got(x_z[way][hop - 1], other_pair(lo, count, layer))
         if hop < 4:
-            lo, count = span(way, hop + 1, 0)
+            lo, count = span(way, hop + 1, 2)
             on = other_pair(lo, count, layer)
             wires.put(x_z[way][hop], on, on, info[ways[way]])
 
     def e2_got(hop, way):
-        lo, count = span(way, hop, 2)
-        layer = layer_from(way, hop)
-        wires.got(b_e2in[way][hop][0], one(lo, count, layer, 3 - x))
-        wires.got(b_e2in[way][hop][1], one(lo, count, layer, 3 - mate))
+        wires.got(b_e2in[way][hop], other_pair(2, 2, layer_from(way, hop)))
 
     def project(hop, r):
         here = pl.ds(pl.multiple_of(order[r] * 384, 384), 384)
@@ -321,7 +303,7 @@
             lanes = pl.ds(pl.multiple_of(layer * 256, 256), 256)
             rows = nv[here, lanes]
             for s in range(1 if r == 2 else 0, 3):
-                weight = wv[s, layer].reshape(256, 256)
+                weight = wv[(Q, K, V)[s], layer].reshape(256, 256)
                 term = jnp.dot(rows, weight, preferred_element_type=F32)
                 if hop == 0:
                     acc[s, here] = term
@@ -334,7 +316,7 @@
     def grad_block(block):
         rows = pl.ds(pl.multiple_of(block * 384, 384), 384)
         g_s[rows] = jnp.dot(
-            cv[rows], wv[3].reshape(2048, 256), preferred_element_type=F32
+            cv[rows], wv[O].reshape(2048, 256), preferred_element_type=F32
         ).astype(BF)
 
     first_row = (seq - odd) * 3 - 3
@@ -348,113 +330,12 @@
 
     lax.fori_loop(0, 9, seg_step, 0)
 
-    b_hop(1, 0, 0)
-    b_hop(1, 1, 0)
-    a_hop(1, 0, 0)
-    a_hop(1, 1, 0)
-    from_near(0)
-    b_hop(2, 0, 0)
-    b_hop(2, 1, 0)
-    from_far(0)
-    spread(1)
-    a_hop(2, 0, 0)
-    a_hop(2, 1, 0)
-    second(1)
-    b_hop(3, 0, 0)
-    b_hop(3, 1, 0)
-    a_hop(3, 0, 0)
-    a_hop(3, 1, 0)
-    from_opp(0)
-    second(0)
-    b_hop(1, 0, 1)
-    b_hop(1, 1, 1)
-    from_near(1)
-    halo_on()
-    spread(2)
-    c_send(0)
-    c_send(1)
-    c_send(2)
-    c_send(3)
-    a_hop(4, 0, 0)
-    a_hop(4, 1, 0)
-    a_hop(1, 0, 1)
-    a_hop(1, 1, 1)
-    b_hop(4, 0, 0)
-    b_hop(4, 1, 0)
-    c_send(4)
-    c_send(5)
-    from_far(1)
-    e2_got(0, 0)
-    b_hop(2, 0, 1)
-    b_hop(2, 1, 1)
-    from_twin(0)
-    a_hop(2, 0, 1)
-    a_hop(2, 1, 1)
-    from_opp(1)
-    x_hop(0, 0)
-    project(0, 0)
-    e2_got(1, 0)
-    c_on(0)
-    b_hop(3, 1, 1)
-    from_near(2)
-    a_hop(3, 0, 1)
-    a_hop(3, 1, 1)
-    b_hop(3, 0, 1)
-    e2_got(1, 1)
-    from_far(2)
-    c_on(1)
-    from_twin(1)
-    e2_got(2, 0)
-    c_got(0)
-    project(0, 1)
-    x_hop(1, 0)
-    x_hop(1, 1)
-    project(1, 1)
-    e2_got(2, 1)
-    a_hop(4, 0, 1)
-    b_hop(4, 1, 1)
-    c_on(2)
-    project(1, 0)
-    b_hop(4, 0, 1)
-    a_hop(4, 1, 1)
-    e2_got(3, 1)
-    from_opp(2)
-    c_got(1)
-    e2_got(3, 0)
-    c_on(3)
-    e2_got(4, 1)
-    x_hop(2, 0)
-    x_hop(2, 1)
-    project(2, 0)
-    e2_got(4, 0)
-    project(2, 1)
-    c_got(2)
-    c_on(4)
-    from_twin(2)
-    project(0, 2)
-    project(1, 2)
-    c_got(3)
-    x_hop(3, 0)
-    x_hop(3, 1)
-    c_on(5)
-    project(3, 2)
-    project(2, 2)
-    project(3, 1)
-    project(3, 0)
-    c_got(4)
-    x_hop(4, 0)
-    x_hop(4, 1)
-    project(4, 1)
-    project(4, 2)
-    project(4, 0)
-    c_got(5)
-    own_c.wait()
-    grad_block(odd)
-    grad_block(1 - odd)
-    wires.finish()
-    wires.started = []
-
-    def extract(i, carry):
+    def extract():
+        lax.fori_loop(0, 9, extract_step, 0)
+        dqkv[0:384, 0:256] = jnp.zeros((384, 256), BF)
+        q_s[0:384] = jnp.zeros((384, 256), BF)
+
+    def extract_step(i, carry):
         rows = pl.ds(pl.multiple_of(i * 128, 128), 128)
         q_s[rows] = (acc[0, rows] * HD**-0.5).astype(BF)
         k_s[rows] = acc[1, rows].astype(BF)
@@ -463,8 +344,6 @@
         acc[2, rows] = jnp.zeros((128, 256), F32)
         return carry
 
-    lax.fori_loop(0, 9, extract, 0)
-    dqkv[0:384, 0:256] = jnp.zeros((384, 256), BF)
     lane_head = lax.broadcasted_iota(jnp.int32, (128, 256), 1) // HD
 
     def by_head(rows):
@@ -481,11 +360,15 @@
     query_at = lax.broadcasted_iota(jnp.int32, (512, 128), 1) + 384
     causal = key_at <= query_at
 
-    def tile(t, carry):
+    def tile_rows(t):
         start = pl.multiple_of(t * 128, 128)
-        here, window = pl.ds(start, 128), pl.ds(start, 512)
-        there = pl.ds(pl.multiple_of(start + 384, 128), 128)
-        queries, out_grads = by_head(q_s[there, :]), by_head(g_s[here, :])
+        return (
+            pl.ds(start, 128), pl.ds(start, 512), pl.ds(pl.multiple_of(start + 384, 128), 128)
+        )
+
+    def tile_front(t, carry):
+        here, window, there = tile_rows(t)
+        queries = by_head(q_s[there, :])
         keys, values = k_s[window, :], v_s[window, :]
         own_seg = seg[pl.ds(first_row + 3 + t, 1), :].astype(F32)
         allowed = causal & (segk[window, :] == own_seg)
@@ -493,30 +376,161 @@
         scores = lax.dot_general(keys, queries, NT, preferred_element_type=F32)
         scores = jnp.where(allowed, scores, MASKED)
         expo = jnp.exp(scores - jnp.max(scores, axis=0, keepdims=True))
-        probs = expo * (1.0 / jnp.sum(expo, axis=0, keepdims=True))
-        prob_rows = probs.astype(BF)
-        prob_grad = lax.dot_general(values, out_grads, NT, preferred_element_type=F32)
-        delta = jnp.sum(probs * prob_grad, axis=0, keepdims=True)
-        score_grad = (probs * (prob_grad - delta)).astype(BF)
-        acc[2, window] += jnp.dot(prob_rows, out_grads, preferred_element_type=F32)
-        acc[1, window] += jnp.dot(score_grad, queries, preferred_element_type=F32)
+        rows = expo * (1.0 / jnp.sum(expo, axis=0, keepdims=True))
+        probs[t] = rows
+        prob_rows = rows.astype(BF)
         attn[here, :] = fold(
             lax.dot_general(values, prob_rows, TN, preferred_element_type=F32)
         ).astype(BF)
+        return carry
+
+    def tiles_front(low_tile, high_tile):
+        def pair(i, carry):
+            tile_front(low_tile + 2 * i, 0)
+            tile_front(low_tile + 2 * i + 1, 0)
+            return carry
+
+        lax.fori_loop(0, (high_tile - low_tile) // 2, pair, 0)
+
+    def tiles_value():
+        def value_step(t, carry):
+            here, window, there = tile_rows(t)
+            acc[2, window] += jnp.dot(
+                probs[t].astype(BF), by_head(g_s[here, :]), preferred_element_type=F32
+            )
+            return carry
+
+        lax.fori_loop(0, 6, value_step, 0)
+
+        def pack_values(i, carry):
+            rows = pl.ds(pl.multiple_of(i * 128, 128), 128)
+            dqkv[rows, 512:768] = acc[2, rows].astype(BF)
+            return carry
+
+        lax.fori_loop(0, 9, pack_values, 0)
+
+    def tile_step(t, carry):
+        here, window, there = tile_rows(t)
+        queries, out_grads = by_head(q_s[there, :]), by_head(g_s[here, :])
+        keys, values = k_s[window, :], v_s[window, :]
+        rows = probs[t]
+        prob_grad = lax.dot_general(values, out_grads, NT, preferred_element_type=F32)
+        delta = jnp.sum(rows * prob_grad, axis=0, keepdims=True)
+        score_grad = (rows * (prob_grad - delta)).astype(BF)
+        acc[1, window] += jnp.dot(score_grad, queries, preferred_element_type=F32)
         dqkv[there, 0:256] = (
             fold(lax.dot_general(keys, score_grad, TN, preferred_element_type=F32)) * HD**-0.5
         ).astype(BF)
         return carry
 
-    lax.fori_loop(0, 6, tile, 0)
-
-    def pack(i, carry):
-        rows = pl.ds(pl.multiple_of(i * 128, 128), 128)
-        dqkv[rows, 256:512] = acc[1, rows].astype(BF)
-        dqkv[rows, 512:768] = acc[2, rows].astype(BF)
-        return carry
-
-    lax.fori_loop(0, 9, pack, 0)
+    def tiles_back(low_tile, high_tile):
+        def pair(i, carry):
+            tile_step(low_tile + 2 * i, 0)
+            tile_step(low_tile + 2 * i + 1, 0)
+            return carry
+
+        pairs = (high_tile - low_tile) // 2
+        lax.fori_loop(0, pairs, pair, 0)
+        if high_tile - low_tile > 2 * pairs:
+            lax.fori_loop(high_tile - 1, high_tile, tile_step, 0)
+
+    def pack():
+        def step(i, carry):
+            rows = pl.ds(pl.multiple_of(i * 128, 128), 128)
+            dqkv[rows, 256:512] = acc[1, rows].astype(BF)
+            products = (
+                dqkv[rows, 0:256].astype(F32) * q_s[rows].astype(F32) * HD**0.5
+                + dqkv[rows, 256:512].astype(F32) * k_s[rows].astype(F32)
+                + dqkv[rows, 512:768].astype(F32) * v_s[rows].astype(F32)
+            )
+            mean = jnp.sum(products, axis=1, keepdims=True) * (1.0 / 2048)
+            means[rows] = jnp.broadcast_to(mean, (128, 128))
+            return carry
+
+        lax.fori_loop(0, 9, step, 0)
+
+    w_hop(1, 0, 0)
+    w_hop(1, 1, 0)
+    from_near(0)
+    second()
+    w_hop(2, 1, 0)
+    w_hop(2, 0, 0)
+    spread(1)
+    w_hop(1, 0, 1)
+    x_hop(0, 0)
+    w_hop(1, 1, 1)
+    halo_on()
+    from_near(1)
+    c_send(1)
+    e2_got(1, 0)
+    w_hop(3, 0, 0)
+    x_hop(1, 1)
+    w_hop(3, 1, 0)
+    spread(2)
+    w_hop(2, 0, 1)
+    from_far(0)
+    c_send(0)
+    c_send(3)
+    e2_got(1, 1)
+    c_send(2)
+    x_hop(1, 0)
+    w_hop(4, 0, 0)
+    w_hop(2, 1, 1)
+    from_twin(0)
+    project(0, 0)
+    x_hop(2, 1)
+    from_far(1)
+    e2_got(2, 0)
+    c_on(1)
+    w_hop(3, 0, 1)
+    w_hop(4, 1, 0)
+    from_near(2)
+    project(1, 0)
+    x_hop(2, 0)
+    w_hop(3, 1, 1)
+    e2_got(2, 1)
+    project(2, 0)
+    c_on(0)
+    from_twin(1)
+    e2_got(3, 0)
+    w_hop(4, 0, 1)
+    x_hop(3, 1)
+    project(0, 1)
+    project(1, 1)
+    project(2, 1)
+    w_hop(4, 1, 1)
+    c_got(1)
+    from_far(2)
+    e2_got(3, 1)
+    x_hop(3, 0)
+    c_on(3)
+    project(3, 0)
+    project(3, 1)
+    c_got(0)
+    from_twin(2)
+    x_hop(4, 1)
+    e2_got(4, 1)
+    x_hop(4, 0)
+    project(4, 1)
+    project(0, 2)
+    c_on(2)
+    project(4, 0)
+    project(1, 2)
+    project(3, 2)
+    c_got(3)
+    project(4, 2)
+    project(2, 2)
+    extract()
+    own_c.wait()
+    grad_block(odd)
+    tiles_front(0, 2)
+    tiles_front(2, 4)
+    c_got(2)
+    grad_block(1 - odd)
+    tiles_front(4, 6)
+    tiles_value()
+    front_sends = wires.started
+    wires.started = []
 
     a_slot, b_slot = ([slots(4) for _ in range(2)] for _ in range(2))
     b_e2 = slots(8)
@@ -531,18 +545,29 @@
     def to_layer(way, left):
         return (z + left) % 8 if way == 0 else (z + 8 - left) % 8
 
-    def weight_grads(left, count):
+    def layers(left, body):
         def step(way, carry):
             layer = (z + left + way * (8 - 2 * left)) % 8
-            lanes = pl.ds(pl.multiple_of(layer * 256, 256), 256)
-            triple = lax.dot_general(nv[:, lanes], dqkv[...], TN, preferred_element_type=F32)
-            for s in range(3):
-                grads[s, layer] = triple[:, s * 256 : (s + 1) * 256].astype(BF).reshape(4, 64, 256)
-            last = lax.dot_general(cv[:, lanes], attn[...], TN, preferred_element_type=F32)
-            grads[3, layer] = last.astype(BF).reshape(4, 64, 256)
+            body(layer, pl.ds(pl.multiple_of(layer * 256, 256), 256))
             return carry
 
-        lax.fori_loop(0, count, step, 0)
+        lax.fori_loop(0, 1 if left in (0, 4) else 2, step, 0)
+
+    def store(s, layer, value):
+        grads[s, layer] = value.astype(BF).reshape(4, 64, 256)
+
+    def qk_grads(layer, lanes):
+        pair = lax.dot_general(nv[:, lanes], dqkv[:, 0:512], TN, preferred_element_type=F32)
+        store(Q, layer, pair[:, 0:256])
+        store(K, layer, pair[:, 256:512])
+
+    def vo_grads(layer, lanes):
+        store(
+            V,
+            layer,
+            lax.dot_general(nv[:, lanes], dqkv[:, 512:768], TN, preferred_element_type=F32),
+        )
+        store(O, layer, lax.dot_general(cv[:, lanes], attn[...], TN, preferred_element_type=F32))
 
     def cross(k, way, left):
         wires.put(
@@ -552,51 +577,58 @@
             info["e2"],
         )
 
-    def w4():
-        weight_grads(4, 1)
-        for way in range(2):
-            wires.put(
-                a_slot[way][0],
-                grads.at[pl.ds(way, 1), to_layer(way, 4)],
-                a_got.at[way, 0, pl.ds(way, 1)],
-                info[ways[way]],
-            )
-        cross(0, 0, 4)
-
-    def w_part(left):
-        weight_grads(left, 2 if left else 1)
+    def a_part(left):
+        layers(left, vo_grads)
+        if left == 4:
+            for way in range(2):
+                wires.put(
+                    a_slot[way][0],
+                    grads.at[pl.ds(way, 1), to_layer(way, 4)],
+                    a_got.at[way, 0, pl.ds(way, 1)],
+                    info[ways[way]],
+                )
+
+    def b_part(left):
+        layers(left, qk_grads)
+        if left == 4:
+            cross(0, 0, 4)
+            return
         for way in range(2 if left else 1):
             cross(7 - 2 * left + way, way, left)
+
+    hidden_slots = {h_e1, h_halo, *h_near, *h_far, *h_opp}.union(*h_twin)
+
+    def settle(sends):
+        for slot, src in sends:
+            pltpu.make_async_copy(src, src, send.at[slot]).wait()
+
+    def hsettle():
+        settle([each for each in front_sends if each[0] in hidden_slots])
+
+    def wsettle():
+        settle([each for each in front_sends if each[0] not in hidden_slots])
 
     def state_grads(r):
         block = blocks[r]
         start = pl.multiple_of(block * 384, 384)
         factor = inv[block, :, 0:1]
 
-        def first(c, carry):
+        mean = means[pl.ds(start, 384), 0:1]
+        once = jnp.where(mp == 0, 1.0, 0.0)
+
+        def final(c, carry):
             lanes = pl.ds(pl.multiple_of(c * 256, 256), 256)
             total = None
             for s in range(1 if r == 0 else 0, 3):
                 term = lax.dot_general(
                     dqkv[pl.ds(start, 384), s * 256 : (s + 1) * 256],
-                    wv[s, c].reshape(256, 256),
+                    wv[(Q, K, V)[s], c].reshape(256, 256),
                     NT,
                     preferred_element_type=F32,
                 )
                 total = term if total is None else total + term
-            total = total * gain[:, lanes].astype(F32)
-            acc[c // 3, pl.ds(pl.multiple_of((c % 3) * 384, 384), 384)] = total
             units = hv[block, :, lanes].astype(F32) * factor
-            return carry + jnp.sum(total * units, axis=1, keepdims=True)
-
-        mean = lax.fori_loop(0, 8, first, jnp.zeros((384, 1), F32)) * (1.0 / 2048)
-        once = jnp.where(mp == 0, 1.0, 0.0)
-
-        def final(c, carry):
-            lanes = pl.ds(pl.multiple_of(c * 256, 256), 256)
-            units = hv[block, :, lanes].astype(F32) * factor
-            scaled = acc[c // 3, pl.ds(pl.multiple_of((c % 3) * 384, 384), 384)]
-            result = factor * (scaled - units * mean)
+            result = factor * (total * gain[:, lanes].astype(F32) - units * mean)
             if r == 2:
                 result = result + cv[own_rows, lanes].astype(F32) * once
             hv[block, :, lanes] = result.astype(BF)
@@ -729,14 +761,19 @@
         )
         w_res[q, pl.ds(0, 2)] = w_pair[pl.ds(0, 2), odd]
 
+    def part_settle():
+        done = wires.started[:-8]
+        wires.started = wires.started[-8:]
+        settle(done)
+
     def w_end():
         for part in range(2):
             wires.got(r_e1[part], w_res.at[1 - q, pl.ds(2 * part, 2)])
         for half in range(2):
             lanes = slice(half * 256, half * 256 + 256)
             for s in range(3):
-                qkv_res[0, s, :, lanes] = w_res[half, s]
-            wo_res[0, :, lanes] = w_res[half, 3]
+                qkv_res[0, s, :, lanes] = w_res[half, (Q, K, V)[s]]
+            wo_res[0, :, lanes] = w_res[half, O]
 
     def t_end():
         wires.got(s_e1, t_e1)
@@ -752,43 +789,55 @@
             t_res[...] = add(t_fin[2], t_e1[...], t_halo[...])
             pltpu.make_async_copy(t_halo, t_halo, send.at[s_half]).wait()
 
-    w4()
-    w_part(3)
-    state_grads(0)
+    a_part(4)
+    tiles_back(0, 4)
+    a_part(3)
+    tiles_back(4, 5)
     a_step(1, 1)
     a_step(0, 1)
+    tiles_back(5, 6)
+    pack()
+    b_part(4)
+    hsettle()
+    b_part(3)
+    state_grads(0)
+    a_part(2)
     b_begin()
-    w_part(2)
+    a_step(1, 2)
+    a_step(0, 2)
+    state_grads(1)
     fold_twin(0)
-    w_part(1)
-    state_grads(1)
-    a_step(0, 2)
-    a_step(1, 2)
+    b_part(2)
+    a_part(1)
+    b_step(0, 1)
     b_step(1, 1)
-    b_step(0, 1)
-    fold_near(0)
-    fold_far(0)
-    state_grads(2)
     fold_twin(1)
-    fold_second(0)
-    w_part(0)
+    b_part(1)
     a_step(0, 3)
     a_step(1, 3)
+    a_part(0)
+    fold_far(0)
+    fold_near(0)
+    state_grads(2)
+    b_step(1, 2)
+    b_step(0, 2)
+    fold_far(1)
+    fold_near(1)
+    b_part(0)
+    fold_second(0)
     fold_twin(2)
-    b_step(0, 2)
-    b_step(1, 2)
-    fold_near(1)
-    halo_pass()
-    fold_far(1)
-    fold_near(2)
-    fold_far(2)
     a_finish()
     fold_second(1)
+    wsettle()
+    b_step(1, 3)
     b_step(0, 3)
-    b_step(1, 3)
+    halo_pass()
+    fold_far(2)
+    fold_near(2)
+    a_end()
+    part_settle()
+    b_finish()
     fold_second(2)
-    a_end()
-    b_finish()
     t_end()
     w_end()
     wires.finish()
@@ -832,7 +881,7 @@
         scratch_shapes=vmem(first, BF)
         + vmem(wide, F32)
         + vmem(heads, BF)
-        + vmem([(1152, 128)], F32)
+        + vmem([(1152, 128), (1152, 128), (6, 512, 512)], F32)
         + vmem(later, BF)
         + [
             pltpu.SemaphoreType.DMA((SLOTS,)),

time: 119 us -> 110 us (0.924)
  Pallas kernels: 118 us -> 109 us
    pallas_call x1, Pallas kernels: 117 us -> 107 us  [per_device(): pl.pallas_call(kernel, out_shape=(jax.ShapeDtypeStruct((384, 256), BF), j...]
where the time goes in v4:
time: 110 us
  Pallas kernels  109 us (99%)
    pallas_call x1, Pallas kernels, per_device(): pl.pallas_call(kernel, out_shape=(jax.ShapeDtypeStruct((384, 256), BF), j...  107 us

profile of v4, /device:TPU:4, one launch (start us, length us, event | category | flops | bytes accessed | tf_op | source)
XLA Modules:
  0.0 109.6 jit_solution(5909013489324067176)
XLA Ops:
  0.6 107.2 %whole.1 = (bf16[384,256]{1,0:T(8,128)(2,1)}, bf16[1,3,64,512]{3,2,1,0:T(8,128)(2,1)}, bf16[1,64,512]{2,1,0:T(8,128)(2,1)}) custom-call(bf16[384,256]{1,0:T(8,128)(2,1)} %hid.1, bf16[1,3,64,512]{3,2,1,0:T(8,128)(2,1)} %bitcast.3, bf16[1,64,512]{2,1,0:T(8,128)(2,1)} %wo.1, bf16[1,384,2048]{2,1,0:T(8,128)(2,1)} %cot.1, bf16[1,2048]{1,0:T(2,128)(2,1)} %gain.1, ...), custom_call_target="tpu_custom_call" | custom-call | tf_op jit(solution)/shard_map/whole/pallas_call | solution.py:872
  107.8 1.8 %hand_over.1 = (bf16[384,256]{1,0:T(8,128)(2,1)}, bf16[1,3,64,512]{3,2,1,0:T(8,128)(2,1)}, bf16[1,64,512]{2,1,0:T(8,128)(2,1)}) custom-call(bf16[384,256]{1,0:T(8,128)(2,1)} %get-tuple-element.9.a_ref, bf16[1,3,64,512]{3,2,1,0:T(8,128)(2,1)} %get-tuple-element.10.b_ref, bf16[1,64,512]{2,1,0:T(8,128)(2,1)} %get-tuple-element.11.c_ref), custom_call_target="tpu_custom_call" | custom-call | tf_op jit(solution)/shard_map/hand_over/pallas_call | solution.py:903

commit v5 on v4

--- a/solution.py
+++ b/solution.py
@@ -1,4 +1,4 @@
-import functools
+import math
 
 import jax
 import jax.numpy as jnp
@@ -50,41 +50,46 @@
     pl.semaphore_wait(barrier, len(names))
 
 
+GROUPS = ("hidden", "weights", "cotangent", "grads", "trunk")
+
+
 class Wires:
     def __init__(self, send, recv):
         self.send, self.recv, self.count = send, recv, 0
-        self.started = []
+        self.sent = dict.fromkeys(GROUPS, 0)
 
     def slot(self):
         self.count += 1
         return self.count - 1
 
-    def put(self, slot, src, dst, device):
-        copy = pltpu.make_async_remote_copy(
+    def put(self, group, slot, src, dst, device):
+        pltpu.make_async_remote_copy(
             src_ref=src,
             dst_ref=dst,
-            send_sem=self.send.at[slot],
+            send_sem=self.send.at[GROUPS.index(group)],
             recv_sem=self.recv.at[slot],
             device_id=device,
             device_id_type=MESH,
-        )
-        copy.start()
-        self.started.append((slot, src))
+        ).start()
+        self.sent[group] += math.prod(src.shape)
 
     def got(self, slot, dst):
         pltpu.make_async_copy(dst, dst, self.recv.at[slot]).wait()
 
-    def finish(self):
-        for slot, src in self.started:
-            pltpu.make_async_copy(src, src, self.send.at[slot]).wait()
+    def settle(self, group, like):
+        rows, rest = divmod(self.sent[group], like.shape[1])
+        assert rest == 0 and rows <= like.shape[0]
+        ref = like.at[0:rows]
+        pltpu.make_async_copy(ref, ref, self.send.at[GROUPS.index(group)]).wait()
 
 
 NT = (((1,), (1,)), ((), ()))
 TN = (((0,), (0,)), ((), ()))
-COT_PARTS = 4
+COT_PARTS = 6
 COT_ROWS = 192 // COT_PARTS
-SLOTS = 160
-Q, K, V, O = 2, 3, 0, 1
+SLOTS = 200
+V, Q, K, O = range(4)
+CROSSING = (O, K)
 
 
 def add(*terms):
@@ -133,7 +138,7 @@
     def slots(count):
         return [wires.slot() for _ in range(count)]
 
-    (w_e1,) = slots(1)
+    w_e1, o_e1 = slots(2)
     h_e1, h_halo = slots(2)
     h_near, h_far, h_opp = slots(3), slots(3), slots(3)
     h_twin = [slots(2) for _ in range(3)]
@@ -141,6 +146,8 @@
     x_z = [slots(4) for _ in range(2)]
     first_e2 = slots(2)
     b_e2in = [slots(5) for _ in range(2)]
+    o_z = [slots(4) for _ in range(2)]
+    o_e2in = [slots(5) for _ in range(2)]
     c_e1, c_near = slots(COT_PARTS), slots(COT_PARTS)
 
     def one(first, count, layer, place):
@@ -153,27 +160,29 @@
         return wv.at[pl.ds(first, count), layer, pl.ds(2 * p, 2)]
 
     def span(way, hop, count):
-        return (0, count) if hop < 4 else (way * count // 2, count // 2)
+        if hop < 4:
+            return 0, count
+        return ((0, 2), (2, 1))[way] if count == 3 else (way, 1)
 
     def layer_from(way, hop):
         return (z + 8 - hop) % 8 if way == 0 else (z + hop) % 8
 
     mine = cols(b, hi, core, mp)
     halo_own = cols(0, hi, core, mp)
-    wires.put(w_e1, ws.at[1 - q], wv.at[:, z, x], info["e1"])
-    wires.put(h_e1, hid, mine, info["e1"])
-    own_rows_w = ws.at[q]
-    own_place = wv.at[:, z, x]
+    wires.put("weights", w_e1, ws.at[1 - q, 0:3], wv.at[0:3, z, x], info["e1"])
+    wires.put("hidden", h_e1, hid, mine, info["e1"])
+    own_rows_w = ws.at[q, 0:3]
+    own_place = wv.at[0:3, z, x]
     for way in range(2):
-        wires.put(w_z[0][way][0], own_rows_w, own_place, info[ways[way]])
-    wires.put(first_e2[0], own_rows_w, own_place, info["e2"])
+        wires.put("weights", w_z[0][way][0], own_rows_w, own_place, info[ways[way]])
+    wires.put("weights", first_e2[0], own_rows_w, own_place, info["e2"])
 
     @pl.when(odd == 1)
     def _():
         pltpu.make_async_remote_copy(
             src_ref=hid,
             dst_ref=halo_own,
-            send_sem=send.at[h_halo],
+            send_sem=send.at[GROUPS.index("hidden")],
             recv_sem=recv.at[h_halo],
             device_id=info["halo"],
             device_id_type=MESH,
@@ -184,10 +193,11 @@
         if r == 1:
             wires.got(h_e1, dst)
         src = hid if r == 0 else dst
-        wires.put(h_near[r], src, dst, info["near"])
-        wires.put(h_far[r], src, dst, info["far"])
+        wires.put("hidden", h_near[r], src, dst, info["near"])
+        wires.put("hidden", h_far[r], src, dst, info["far"])
 
     spread(0)
+    wires.put("weights", o_e1, ws.at[1 - q, O], wv.at[O, z, x], info["e1"])
 
     def half_cols(block, head_hi, head_core):
         start = pl.multiple_of((head_hi * 2 + head_core) * 512, 512)
@@ -201,28 +211,28 @@
             pltpu.make_async_remote_copy(
                 src_ref=halo_own,
                 dst_ref=halo_own,
-                send_sem=send.at[h_halo],
+                send_sem=send.at[GROUPS.index("hidden")],
                 recv_sem=recv.at[h_halo],
                 device_id=info["e1"],
                 device_id_type=MESH,
             ).start()
 
-        wires.started.append((h_halo, hid))
+        wires.sent["hidden"] += 384 * 256
 
     def from_near(r):
         got = cols(order[r], hi, core, 1 - mp)
         wires.got(h_near[r], got)
-        wires.put(h_opp[r], got, got, info["far"])
+        wires.put("hidden", h_opp[r], got, got, info["far"])
         if r == 0:
             own_h.wait()
         both = half_cols(order[r], hi, core)
-        wires.put(h_twin[r][0], both, both, info["twin"])
+        wires.put("hidden", h_twin[r][0], both, both, info["twin"])
 
     def from_far(r):
         wires.got(h_far[r], cols(order[r], 1 - hi, core, 1 - mp))
         wires.got(h_opp[r], cols(order[r], 1 - hi, core, mp))
         both = half_cols(order[r], 1 - hi, core)
-        wires.put(h_twin[r][1], both, both, info["twin"])
+        wires.put("hidden", h_twin[r][1], both, both, info["twin"])
 
     def from_twin(r):
         wires.got(h_twin[r][0], half_cols(order[r], hi, 1 - core))
@@ -246,43 +256,62 @@
 
     def c_send(k):
         start = pl.multiple_of(mp * 192 + k * COT_ROWS, COT_ROWS)
-        wires.put(c_e1[k], cot.at[0, pl.ds(start, COT_ROWS)], c_rows(odd, mp, k), info["e1"])
+        wires.put("cotangent", c_e1[k], cot.at[0, pl.ds(start, COT_ROWS)], c_rows(odd, mp, k), info["e1"])
+
+    c_send(0)
 
     def c_on(k):
         ref = c_rows(1 - odd, mp, k)
         wires.got(c_e1[k], ref)
-        wires.put(c_near[k], ref, ref, info["near"])
+        wires.put("cotangent", c_near[k], ref, ref, info["near"])
 
     def c_got(k):
         wires.got(c_near[k], c_rows(1 - odd, 1 - mp, k))
 
     def second():
-        ref = wv.at[:, z, mate]
+        ref = wv.at[0:3, z, mate]
         wires.got(w_e1, ref)
-        wires.put(first_e2[1], ref, ref, info["e2"])
+        wires.put("weights", first_e2[1], ref, ref, info["e2"])
         for way in range(2):
-            wires.put(w_z[1][way][0], ref, ref, info[ways[way]])
+            wires.put("weights", w_z[1][way][0], ref, ref, info[ways[way]])
 
     def w_hop(hop, way, member):
         place = (x, mate)[member]
         layer = layer_from(way, hop)
-        lo, count = span(way, hop, 4)
+        lo, count = span(way, hop, 3)
         wires.got(w_z[member][way][hop - 1], one(lo, count, layer, place))
         if hop < 4:
-            lo, count = span(way, hop + 1, 4)
+            lo, count = span(way, hop + 1, 3)
             on = one(lo, count, layer, place)
-            wires.put(w_z[member][way][hop], on, on, info[ways[way]])
+            wires.put("weights", w_z[member][way][hop], on, on, info[ways[way]])
         if member == 1 and (hop < 4 or way == 1):
-            ref = own_pair(2, 2, layer)
-            wires.put(b_e2in[way][hop], ref, ref, info["e2"])
+            ref = own_pair(K, 1, layer)
+            wires.put("weights", b_e2in[way][hop], ref, ref, info["e2"])
+
+    def o_second():
+        wires.got(o_e1, wv.at[O, z, mate])
+        ref = own_pair(O, 1, z)
+        for way in range(2):
+            wires.put("weights", o_z[way][0], ref, ref, info[ways[way]])
+        wires.put("weights", o_e2in[0][0], ref, ref, info["e2"])
+
+    def o_hop(hop, way):
+        ref = own_pair(O, 1, layer_from(way, hop))
+        wires.got(o_z[way][hop - 1], ref)
+        if hop < 3 or (hop == 3 and way == 1):
+            wires.put("weights", o_z[way][hop], ref, ref, info[ways[way]])
+        wires.put("weights", o_e2in[way][hop], ref, ref, info["e2"])
+
+    def o_got(hop, way):
+        wires.got(o_e2in[way][hop], other_pair(O, 1, layer_from(way, hop)))
 
     def x_hop(hop, way):
         if hop == 0:
-            wires.got(first_e2[0], wv.at[:, z, 3 - x])
-            wires.got(first_e2[1], wv.at[:, z, 3 - mate])
+            wires.got(first_e2[0], wv.at[0:3, z, 3 - x])
+            wires.got(first_e2[1], wv.at[0:3, z, 3 - mate])
             ref = other_pair(0, 2, z)
             for each in range(2):
-                wires.put(x_z[each][0], ref, ref, info[ways[each]])
+                wires.put("weights", x_z[each][0], ref, ref, info[ways[each]])
             return
         lo, count = span(way, hop, 2)
         layer = layer_from(way, hop)
@@ -290,10 +319,10 @@
         if hop < 4:
             lo, count = span(way, hop + 1, 2)
             on = other_pair(lo, count, layer)
-            wires.put(x_z[way][hop], on, on, info[ways[way]])
+            wires.put("weights", x_z[way][hop], on, on, info[ways[way]])
 
     def e2_got(hop, way):
-        wires.got(b_e2in[way][hop], other_pair(2, 2, layer_from(way, hop)))
+        wires.got(b_e2in[way][hop], other_pair(K, 1, layer_from(way, hop)))
 
     def project(hop, r):
         here = pl.ds(pl.multiple_of(order[r] * 384, 384), 384)
@@ -351,10 +380,17 @@
             [jnp.where(lane_head == h, rows, jnp.zeros_like(rows)) for h in range(4)], axis=0
         )
 
-    def fold(wide):
-        return jnp.concatenate(
-            [wide[h * HD : (h + 1) * HD, h * 128 : (h + 1) * 128] for h in range(4)], axis=0
-        ).T
+    def gather_heads(rows, weights):
+        parts = []
+        for pair in range(2):
+            wide = lax.dot_general(
+                rows[:, pair * 128 : (pair + 1) * 128],
+                weights[:, pair * 256 : (pair + 1) * 256],
+                TN,
+                preferred_element_type=F32,
+            )
+            parts += [wide[0:HD, 0:128], wide[HD : 2 * HD, 128:256]]
+        return jnp.concatenate(parts, axis=0).T
 
     key_at = lax.broadcasted_iota(jnp.int32, (512, 128), 0)
     query_at = lax.broadcasted_iota(jnp.int32, (512, 128), 1) + 384
@@ -377,30 +413,31 @@
         scores = jnp.where(allowed, scores, MASKED)
         expo = jnp.exp(scores - jnp.max(scores, axis=0, keepdims=True))
         rows = expo * (1.0 / jnp.sum(expo, axis=0, keepdims=True))
-        probs[t] = rows
         prob_rows = rows.astype(BF)
-        attn[here, :] = fold(
-            lax.dot_general(values, prob_rows, TN, preferred_element_type=F32)
-        ).astype(BF)
+        probs[t] = prob_rows
+        attn[here, :] = gather_heads(values, prob_rows).astype(BF)
         return carry
 
+    def unrolled(step, low_tile, high_tile):
+        def all_of_them(i, carry):
+            for t in range(low_tile, high_tile):
+                step(i + t, carry)
+            return carry
+
+        lax.fori_loop(0, 1, all_of_them, 0)
+
     def tiles_front(low_tile, high_tile):
-        def pair(i, carry):
-            tile_front(low_tile + 2 * i, 0)
-            tile_front(low_tile + 2 * i + 1, 0)
-            return carry
-
-        lax.fori_loop(0, (high_tile - low_tile) // 2, pair, 0)
+        unrolled(tile_front, low_tile, high_tile)
 
     def tiles_value():
         def value_step(t, carry):
             here, window, there = tile_rows(t)
             acc[2, window] += jnp.dot(
-                probs[t].astype(BF), by_head(g_s[here, :]), preferred_element_type=F32
+                probs[t], by_head(g_s[here, :]), preferred_element_type=F32
             )
             return carry
 
-        lax.fori_loop(0, 6, value_step, 0)
+        unrolled(value_step, 0, 6)
 
         def pack_values(i, carry):
             rows = pl.ds(pl.multiple_of(i * 128, 128), 128)
@@ -413,26 +450,16 @@
         here, window, there = tile_rows(t)
         queries, out_grads = by_head(q_s[there, :]), by_head(g_s[here, :])
         keys, values = k_s[window, :], v_s[window, :]
-        rows = probs[t]
+        rows = probs[t].astype(F32)
         prob_grad = lax.dot_general(values, out_grads, NT, preferred_element_type=F32)
         delta = jnp.sum(rows * prob_grad, axis=0, keepdims=True)
         score_grad = (rows * (prob_grad - delta)).astype(BF)
         acc[1, window] += jnp.dot(score_grad, queries, preferred_element_type=F32)
-        dqkv[there, 0:256] = (
-            fold(lax.dot_general(keys, score_grad, TN, preferred_element_type=F32)) * HD**-0.5
-        ).astype(BF)
+        dqkv[there, 0:256] = (gather_heads(keys, score_grad) * HD**-0.5).astype(BF)
         return carry
 
     def tiles_back(low_tile, high_tile):
-        def pair(i, carry):
-            tile_step(low_tile + 2 * i, 0)
-            tile_step(low_tile + 2 * i + 1, 0)
-            return carry
-
-        pairs = (high_tile - low_tile) // 2
-        lax.fori_loop(0, pairs, pair, 0)
-        if high_tile - low_tile > 2 * pairs:
-            lax.fori_loop(high_tile - 1, high_tile, tile_step, 0)
+        unrolled(tile_step, low_tile, high_tile)
 
     def pack():
         def step(i, carry):
@@ -449,93 +476,112 @@
 
         lax.fori_loop(0, 9, step, 0)
 
+    w_hop(1, 1, 0)
     w_hop(1, 0, 0)
-    w_hop(1, 1, 0)
+    second()
     from_near(0)
-    second()
     w_hop(2, 1, 0)
     w_hop(2, 0, 0)
+    x_hop(0, 0)
     spread(1)
+    w_hop(1, 1, 1)
+    o_second()
+    w_hop(3, 1, 0)
+    w_hop(3, 0, 0)
+    from_far(0)
     w_hop(1, 0, 1)
-    x_hop(0, 0)
-    w_hop(1, 1, 1)
     halo_on()
     from_near(1)
-    c_send(1)
+    w_hop(2, 1, 1)
+    c_send(2)
     e2_got(1, 0)
-    w_hop(3, 0, 0)
-    x_hop(1, 1)
-    w_hop(3, 1, 0)
-    spread(2)
-    w_hop(2, 0, 1)
-    from_far(0)
-    c_send(0)
+    o_got(0, 0)
+    e2_got(1, 1)
     c_send(3)
-    e2_got(1, 1)
-    c_send(2)
     x_hop(1, 0)
     w_hop(4, 0, 0)
-    w_hop(2, 1, 1)
+    spread(2)
+    o_hop(1, 1)
+    o_hop(1, 0)
+    w_hop(2, 0, 1)
+    w_hop(4, 1, 0)
+    c_send(5)
     from_twin(0)
+    x_hop(1, 1)
     project(0, 0)
+    c_send(4)
+    e2_got(2, 1)
+    c_send(1)
+    w_hop(3, 1, 1)
+    c_on(2)
+    o_hop(2, 1)
+    from_far(1)
+    project(1, 0)
+    o_got(1, 1)
+    x_hop(2, 0)
+    o_hop(2, 0)
+    from_near(2)
+    c_on(3)
+    o_got(1, 0)
+    c_on(0)
+    e2_got(2, 0)
     x_hop(2, 1)
-    from_far(1)
-    e2_got(2, 0)
+    w_hop(3, 0, 1)
+    project(2, 0)
+    w_hop(4, 1, 1)
+    e2_got(3, 1)
+    from_twin(1)
+    project(0, 1)
+    o_got(2, 1)
+    x_hop(3, 0)
+    o_hop(3, 1)
+    c_on(5)
+    project(2, 1)
+    project(1, 1)
+    c_got(3)
+    o_hop(3, 0)
+    e2_got(3, 0)
+    x_hop(3, 1)
+    c_on(4)
+    o_got(2, 0)
+    project(3, 1)
+    from_far(2)
+    project(3, 0)
+    w_hop(4, 0, 1)
+    e2_got(4, 1)
+    c_got(0)
+    o_got(3, 1)
     c_on(1)
-    w_hop(3, 0, 1)
-    w_hop(4, 1, 0)
-    from_near(2)
-    project(1, 0)
-    x_hop(2, 0)
-    w_hop(3, 1, 1)
-    e2_got(2, 1)
-    project(2, 0)
-    c_on(0)
-    from_twin(1)
-    e2_got(3, 0)
-    w_hop(4, 0, 1)
-    x_hop(3, 1)
-    project(0, 1)
-    project(1, 1)
-    project(2, 1)
-    w_hop(4, 1, 1)
-    c_got(1)
-    from_far(2)
-    e2_got(3, 1)
-    x_hop(3, 0)
-    c_on(3)
-    project(3, 0)
-    project(3, 1)
-    c_got(0)
+    o_hop(4, 1)
+    x_hop(4, 0)
+    x_hop(4, 1)
+    project(4, 1)
     from_twin(2)
-    x_hop(4, 1)
-    e2_got(4, 1)
-    x_hop(4, 0)
-    project(4, 1)
+    project(4, 0)
     project(0, 2)
-    c_on(2)
-    project(4, 0)
+    c_got(5)
+    o_got(4, 1)
+    o_got(3, 0)
     project(1, 2)
     project(3, 2)
-    c_got(3)
+    project(2, 2)
     project(4, 2)
-    project(2, 2)
+    c_got(4)
     extract()
     own_c.wait()
     grad_block(odd)
     tiles_front(0, 2)
+    c_got(1)
+    c_got(2)
     tiles_front(2, 4)
-    c_got(2)
+    tiles_front(4, 6)
     grad_block(1 - odd)
-    tiles_front(4, 6)
     tiles_value()
-    front_sends = wires.started
-    wires.started = []
-
-    a_slot, b_slot = ([slots(4) for _ in range(2)] for _ in range(2))
-    b_e2 = slots(8)
-    (a_e2,) = slots(1)
-    r_e1 = slots(2)
+
+    a_slot, b_slot = ([[slots(4) for _ in range(2)] for _ in range(2)] for _ in range(2))
+    b_e2 = [slots(2) for _ in range(8)]
+    a_e2 = slots(2)
+    r_e1 = [slots(2) for _ in range(2)]
     s_twin = [slots(2) for _ in range(3)]
     s_far1, s_far2, s_near1, s_near2, s_near3 = (slots(3) for _ in range(5))
     s_e1, s_half, s_halo = slots(3)
@@ -569,44 +615,36 @@
         )
         store(O, layer, lax.dot_general(cv[:, lanes], attn[...], TN, preferred_element_type=F32))
 
-    def cross(k, way, left):
-        wires.put(
-            b_e2[k],
-            grads.at[pl.ds(2, 2), to_layer(way, left), pl.ds(2 - 2 * p, 2)],
-            b_e2got.at[k],
-            info["e2"],
-        )
-
-    def a_part(left):
-        layers(left, vo_grads)
+    def part(m, left):
+        layers(left, (vo_grads, qk_grads)[m])
         if left == 4:
-            for way in range(2):
-                wires.put(
-                    a_slot[way][0],
-                    grads.at[pl.ds(way, 1), to_layer(way, 4)],
-                    a_got.at[way, 0, pl.ds(way, 1)],
-                    info[ways[way]],
-                )
-
-    def b_part(left):
-        layers(left, qk_grads)
-        if left == 4:
-            cross(0, 0, 4)
-            return
-        for way in range(2 if left else 1):
-            cross(7 - 2 * left + way, way, left)
-
-    hidden_slots = {h_e1, h_halo, *h_near, *h_far, *h_opp}.union(*h_twin)
-
-    def settle(sends):
-        for slot, src in sends:
-            pltpu.make_async_copy(src, src, send.at[slot]).wait()
+            wires.put("grads",
+                a_slot[m][m][0],
+                grads.at[m, to_layer(m, 4)],
+                a_got.at[m, 0, m],
+                info[ways[m]],
+            )
+        for way in range(1 if left in (0, 4) else 2):
+            k = 0 if left == 4 else 7 - 2 * left + way
+            wires.put("grads",
+                b_e2[k][m],
+                grads.at[CROSSING[m], to_layer(way, left), pl.ds(2 - 2 * p, 2)],
+                b_e2got.at[k, m],
+                info["e2"],
+            )
+
+    def early_part(left):
+        part(0, left)
+
+    def late_part(left):
+        part(1, left)
 
     def hsettle():
-        settle([each for each in front_sends if each[0] in hidden_slots])
+        wires.settle("hidden", nv)
 
     def wsettle():
-        settle([each for each in front_sends if each[0] not in hidden_slots])
+        wires.settle("weights", nv)
+        wires.settle("cotangent", nv)
 
     def state_grads(r):
         block = blocks[r]
@@ -637,31 +675,31 @@
         lax.fori_loop(0, 8, final, 0)
         for side in range(2):
             lanes = pl.ds(pl.multiple_of(side * 1024 + (1 - core) * 512, 512), 512)
-            wires.put(s_twin[r][side], hv.at[block, :, lanes], t_twin.at[r, side], info["twin"])
+            wires.put("trunk", s_twin[r][side], hv.at[block, :, lanes], t_twin.at[r, side], info["twin"])
 
     def fold_twin(r):
         for side in (0, 1):
             lanes = pl.ds(pl.multiple_of(side * 1024 + core * 512, 512), 512)
             wires.got(s_twin[r][side], t_twin.at[r, side])
             t_twin[r, side] = add(t_twin[r, side], hv[blocks[r], :, lanes])
-        wires.put(s_far1[r], t_twin.at[r, 1 - hi, top], t_far1.at[r], info["far"])
+        wires.put("trunk", s_far1[r], t_twin.at[r, 1 - hi, top], t_far1.at[r], info["far"])
         there = pl.ds(pl.multiple_of((1 - mp) * 256, 256), 256)
-        wires.put(s_near1[r], t_twin.at[r, hi, low, there], t_near1.at[r, 0], info["near"])
+        wires.put("trunk", s_near1[r], t_twin.at[r, hi, low, there], t_near1.at[r, 0], info["near"])
         there = pl.ds(pl.multiple_of(mp * 256, 256), 256)
-        wires.put(s_near3[r], t_twin.at[r, 1 - hi, low, there], t_near1.at[r, 1], info["near"])
+        wires.put("trunk", s_near3[r], t_twin.at[r, 1 - hi, low, there], t_near1.at[r, 1], info["near"])
 
     def fold_far(r):
         wires.got(s_far1[r], t_far1.at[r])
         for part in range(2):
             lanes = slice(part * 256, part * 256 + 256)
             t_mid1[r, part] = add(t_twin[r, hi, 0:192, lanes], t_far1[r, :, lanes])
-        wires.put(s_near2[r], t_mid1.at[r, 1 - mp], t_near2.at[r], info["near"])
+        wires.put("trunk", s_near2[r], t_mid1.at[r, 1 - mp], t_near2.at[r], info["near"])
 
     def fold_near(r):
         wires.got(s_near3[r], t_near1.at[r, 1])
         there = pl.ds(pl.multiple_of((1 - mp) * 256, 256), 256)
         t_mid2[r, 1] = add(t_twin[r, 1 - hi, 192:384, there], t_near1[r, 1])
-        wires.put(s_far2[r], t_mid2.at[r, 1], t_far2.at[r], info["far"])
+        wires.put("trunk", s_far2[r], t_mid2.at[r, 1], t_far2.at[r], info["far"])
         wires.got(s_near1[r], t_near1.at[r, 0])
         there = pl.ds(pl.multiple_of(mp * 256, 256), 256)
         t_mid2[r, 0] = add(t_twin[r, hi, 192:384, there], t_near1[r, 0])
@@ -677,14 +715,14 @@
                 pltpu.make_async_remote_copy(
                     src_ref=t_fin.at[0],
                     dst_ref=t_halo,
-                    send_sem=send.at[s_half],
+                    send_sem=send.at[len(GROUPS)],
                     recv_sem=recv.at[s_half],
                     device_id=info["e1"],
                     device_id_type=MESH,
                 ).start()
 
         if r == 1:
-            wires.put(s_e1, t_fin.at[1], t_e1, info["e1"])
+            wires.put("trunk", s_e1, t_fin.at[1], t_e1, info["e1"])
 
     def halo_pass():
         @pl.when(odd == 0)
@@ -694,81 +732,68 @@
             pltpu.make_async_remote_copy(
                 src_ref=t_pass,
                 dst_ref=t_halo,
-                send_sem=send.at[s_halo],
+                send_sem=send.at[len(GROUPS)],
                 recv_sem=recv.at[s_halo],
                 device_id=info["halo"],
                 device_id_type=MESH,
             ).start()
 
-    def a_step(way, step):
+    def a_step(way, step, m):
         layer = to_layer(way, 4 - step)
-        if step == 1:
-            wires.got(a_slot[way][0], a_got.at[way, 0, pl.ds(way, 1)])
-            a_got[way, 0, way] = add(grads[way, layer], a_got[way, 0, way])
-            a_got[way, 0, 1 - way] = grads[1 - way, layer]
+        on = a_got.at[way, step, m]
+        if step == 1 and m != way:
+            wires.put("grads", a_slot[m][way][1], grads.at[m, layer], on, info[ways[way]])
+            return
+        here = a_got.at[way, step - 1, m]
+        wires.got(a_slot[m][way][step - 1], here)
+        here[...] = add(grads[m, layer], here[...])
+        wires.put("grads", a_slot[m][way][step], here, on, info[ways[way]])
+
+    def b_start(way, left, k, m):
+        wires.got(b_e2[k][m], b_e2got.at[k, m])
+        return add(grads[CROSSING[m], to_layer(way, left), pl.ds(2 * p, 2)], b_e2got[k, m])
+
+    def b_begin(m):
+        b_e2got[0, m] = b_start(m, 4, 0, m)
+        wires.put("grads", b_slot[m][m][0], b_e2got.at[0, m], b_got.at[m, 0, m], info[ways[m]])
+
+    def b_step(way, step, m):
+        k = 2 * step - 1 + way
+        added = b_start(way, 4 - step, k, m)
+        here = b_got.at[way, step - 1, m]
+        if step == 1 and m != way:
+            here[...] = added
         else:
-            wires.got(a_slot[way][step - 1], a_got.at[way, step - 1])
-            a_got[way, step - 1] = add(grads[pl.ds(0, 2), layer], a_got[way, step - 1])
-        wires.put(a_slot[way][step], a_got.at[way, step - 1], a_got.at[way, step], info[ways[way]])
-
-    def b_start(way, left, k):
-        wires.got(b_e2[k], b_e2got.at[k])
-        layer = to_layer(way, left)
-        return add(grads[pl.ds(2, 2), layer, pl.ds(2 * p, 2)], b_e2got[k])
-
-    def b_begin():
-        b_e2got[0] = b_start(0, 4, 0)
+            wires.got(b_slot[m][way][step - 1], here)
+            here[...] = add(added, here[...])
+        wires.put("grads", b_slot[m][way][step], here, b_got.at[way, step, m], info[ways[way]])
+
+    def a_finish(m):
         for way in range(2):
-            wires.put(
-                b_slot[way][0],
-                b_e2got.at[0, pl.ds(way, 1)],
-                b_got.at[way, 0, pl.ds(way, 1)],
-                info[ways[way]],
-            )
-
-    def b_step(way, step):
-        added = b_start(way, 4 - step, 2 * step - 1 + way)
-        if step == 1:
-            wires.got(b_slot[way][0], b_got.at[way, 0, pl.ds(way, 1)])
-            b_got[way, 0, way] = add(added[way], b_got[way, 0, way])
-            b_got[way, 0, 1 - way] = added[1 - way]
-        else:
-            wires.got(b_slot[way][step - 1], b_got.at[way, step - 1])
-            b_got[way, step - 1] = add(added, b_got[way, step - 1])
-        wires.put(b_slot[way][step], b_got.at[way, step - 1], b_got.at[way, step], info[ways[way]])
-
-    def a_finish():
+            wires.got(a_slot[m][way][3], a_got.at[way, 3, m])
+        a_fin[m] = add(grads[m, z], a_got[0, 3, m], a_got[1, 3, m])
+        wires.put("grads", a_e2[m], a_fin.at[m, pl.ds(2 - 2 * p, 2)], a_e2got.at[m], info["e2"])
+
+    def swap(s, m, kind):
+        wires.put("grads", r_e1[kind][m], w_pair.at[s, 1 - odd], w_res.at[q, s], info["e1"])
+        w_res[q, s] = w_pair[s, odd]
+
+    def b_finish(m):
+        last = b_start(0, 0, 7, m)
         for way in range(2):
-            wires.got(a_slot[way][3], a_got.at[way, 3])
-        a_fin[...] = add(grads[pl.ds(0, 2), z], a_got[0, 3], a_got[1, 3])
-        wires.put(a_e2, a_fin.at[:, pl.ds(2 - 2 * p, 2)], a_e2got, info["e2"])
-
-    def b_finish():
-        last = b_start(0, 0, 7)
-        for way in range(2):
-            wires.got(b_slot[way][3], b_got.at[way, 3])
-        w_pair[pl.ds(2, 2)] = add(last, b_got[0, 3], b_got[1, 3])
-        wires.put(
-            r_e1[1], w_pair.at[pl.ds(2, 2), 1 - odd], w_res.at[q, pl.ds(2, 2)], info["e1"]
-        )
-        w_res[q, pl.ds(2, 2)] = w_pair[pl.ds(2, 2), odd]
-
-    def a_end():
-        wires.got(a_e2, a_e2got)
-        w_pair[pl.ds(0, 2)] = add(a_fin[:, pl.ds(2 * p, 2)], a_e2got[...])
-        wires.put(
-            r_e1[0], w_pair.at[pl.ds(0, 2), 1 - odd], w_res.at[q, pl.ds(0, 2)], info["e1"]
-        )
-        w_res[q, pl.ds(0, 2)] = w_pair[pl.ds(0, 2), odd]
-
-    def part_settle():
-        done = wires.started[:-8]
-        wires.started = wires.started[-8:]
-        settle(done)
+            wires.got(b_slot[m][way][3], b_got.at[way, 3, m])
+        w_pair[CROSSING[m]] = add(last, b_got[0, 3, m], b_got[1, 3, m])
+        swap(CROSSING[m], m, 1)
+
+    def a_end(m):
+        wires.got(a_e2[m], a_e2got.at[m])
+        w_pair[m] = add(a_fin[m, pl.ds(2 * p, 2)], a_e2got[m])
+        swap(m, m, 0)
 
     def w_end():
-        for part in range(2):
-            wires.got(r_e1[part], w_res.at[1 - q, pl.ds(2 * part, 2)])
+        for kind in range(2):
+            for m in range(2):
+                wires.got(r_e1[kind][m], w_res.at[1 - q, (m, CROSSING[m])[kind]])
         for half in range(2):
             lanes = slice(half * 256, half * 256 + 256)
             for s in range(3):
@@ -781,66 +806,81 @@
         @pl.when(odd == 0)
         def _():
             t_res[...] = add(t_fin[2], t_e1[...])
-            pltpu.make_async_copy(t_pass, t_pass, send.at[s_halo]).wait()
+            pltpu.make_async_copy(t_pass, t_pass, send.at[len(GROUPS)]).wait()
 
         @pl.when(odd == 1)
         def _():
             wires.got(s_halo, t_halo)
             t_res[...] = add(t_fin[2], t_e1[...], t_halo[...])
-            pltpu.make_async_copy(t_halo, t_halo, send.at[s_half]).wait()
-
-    a_part(4)
+            pltpu.make_async_copy(t_halo, t_halo, send.at[len(GROUPS)]).wait()
+
+    early_part(4)
+    early_part(3)
+    a_step(1, 1, 0)
     tiles_back(0, 4)
-    a_part(3)
-    tiles_back(4, 5)
-    a_step(1, 1)
-    a_step(0, 1)
-    tiles_back(5, 6)
+    a_step(0, 1, 0)
+    tiles_back(4, 6)
     pack()
-    b_part(4)
     hsettle()
-    b_part(3)
+    late_part(4)
+    b_step(1, 1, 0)
+    late_part(3)
     state_grads(0)
-    a_part(2)
-    b_begin()
-    a_step(1, 2)
-    a_step(0, 2)
+    b_begin(0)
+    a_step(0, 1, 1)
+    early_part(2)
+    a_step(1, 1, 1)
     state_grads(1)
     fold_twin(0)
-    b_part(2)
-    a_part(1)
-    b_step(0, 1)
-    b_step(1, 1)
+    a_step(0, 2, 0)
+    a_step(1, 2, 0)
+    late_part(2)
+    b_step(0, 1, 0)
+    b_begin(1)
+    b_step(0, 1, 1)
+    a_step(0, 2, 1)
     fold_twin(1)
-    b_part(1)
-    a_step(0, 3)
-    a_step(1, 3)
-    a_part(0)
+    a_step(1, 2, 1)
+    early_part(1)
+    a_step(0, 3, 0)
+    a_step(1, 3, 0)
+    late_part(1)
     fold_far(0)
+    b_step(0, 2, 0)
+    b_step(1, 1, 1)
     fold_near(0)
     state_grads(2)
-    b_step(1, 2)
-    b_step(0, 2)
+    a_step(1, 3, 1)
+    a_step(0, 3, 1)
+    b_step(0, 2, 1)
+    wsettle()
+    fold_near(1)
     fold_far(1)
-    fold_near(1)
-    b_part(0)
+    b_step(1, 2, 0)
     fold_second(0)
+    early_part(0)
     fold_twin(2)
-    a_finish()
+    late_part(0)
+    b_step(1, 2, 1)
+    a_finish(0)
+    b_step(0, 3, 0)
     fold_second(1)
-    wsettle()
-    b_step(1, 3)
-    b_step(0, 3)
+    a_finish(1)
+    b_step(1, 3, 0)
     halo_pass()
+    b_step(0, 3, 1)
+    b_step(1, 3, 1)
     fold_far(2)
     fold_near(2)
-    a_end()
-    part_settle()
-    b_finish()
+    a_end(0)
+    b_finish(0)
+    a_end(1)
+    b_finish(1)
     fold_second(2)
     t_end()
     w_end()
-    wires.finish()
+    wires.settle("grads", nv)
+    wires.settle("trunk", nv)
 
 
 def hand_over(a_ref, b_ref, c_ref, a_out, b_out, c_out):
@@ -881,10 +921,10 @@
         scratch_shapes=vmem(first, BF)
         + vmem(wide, F32)
         + vmem(heads, BF)
-        + vmem([(1152, 128), (1152, 128), (6, 512, 512)], F32)
-        + vmem(later, BF)
+        + vmem([(1152, 128), (1152, 128)], F32)
+        + vmem([(6, 512, 512)] + later, BF)
         + [
-            pltpu.SemaphoreType.DMA((SLOTS,)),
+            pltpu.SemaphoreType.DMA((len(GROUPS) + 1,)),
             pltpu.SemaphoreType.DMA((SLOTS,)),
             pltpu.SemaphoreType.DMA((2,)),
         ],

time: 110 us -> 110 us (level)
  no operation moved by 1% of the time
where the time goes in v5:
time: 110 us
  Pallas kernels  109 us (99%)
    pallas_call x1, Pallas kernels, per_device(): pl.pallas_call(kernel, out_shape=(jax.ShapeDtypeStruct((384, 256), BF), j...  107 us

profile of v5, /device:TPU:4, one launch (start us, length us, event | category | flops | bytes accessed | tf_op | source)
XLA Modules:
  0.0 109.6 jit_solution(15486742587343701397)
XLA Ops:
  0.6 107.2 %whole.1 = (bf16[384,256]{1,0:T(8,128)(2,1)}, bf16[1,3,64,512]{3,2,1,0:T(8,128)(2,1)}, bf16[1,64,512]{2,1,0:T(8,128)(2,1)}) custom-call(bf16[384,256]{1,0:T(8,128)(2,1)} %hid.1, bf16[1,3,64,512]{3,2,1,0:T(8,128)(2,1)} %bitcast.3, bf16[1,64,512]{2,1,0:T(8,128)(2,1)} %wo.1, bf16[1,384,2048]{2,1,0:T(8,128)(2,1)} %cot.1, bf16[1,2048]{1,0:T(2,128)(2,1)} %gain.1, ...), custom_call_target="tpu_custom_call" | custom-call | tf_op jit(solution)/shard_map/whole/pallas_call | solution.py:912
  107.8 1.8 %hand_over.1 = (bf16[384,256]{1,0:T(8,128)(2,1)}, bf16[1,3,64,512]{3,2,1,0:T(8,128)(2,1)}, bf16[1,64,512]{2,1,0:T(8,128)(2,1)}) custom-call(bf16[384,256]{1,0:T(8,128)(2,1)} %get-tuple-element.9.a_ref, bf16[1,3,64,512]{3,2,1,0:T(8,128)(2,1)} %get-tuple-element.10.b_ref, bf16[1,64,512]{2,1,0:T(8,128)(2,1)} %get-tuple-element.11.c_ref), custom_call_target="tpu_custom_call" | custom-call | tf_op jit(solution)/shard_map/hand_over/pallas_call | solution.py:943

commit v6 on v5

--- a/solution.py
+++ b/solution.py
@@ -87,9 +87,8 @@
 TN = (((0,), (0,)), ((), ()))
 COT_PARTS = 6
 COT_ROWS = 192 // COT_PARTS
-SLOTS = 200
-V, Q, K, O = range(4)
-CROSSING = (O, K)
+SLOTS = 180
+Q, K, V, O = 1, 3, 0, 2
 
 
 def add(*terms):
@@ -138,7 +137,7 @@
     def slots(count):
         return [wires.slot() for _ in range(count)]
 
-    w_e1, o_e1 = slots(2)
+    (w_e1,) = slots(1)
     h_e1, h_halo = slots(2)
     h_near, h_far, h_opp = slots(3), slots(3), slots(3)
     h_twin = [slots(2) for _ in range(3)]
@@ -146,8 +145,6 @@
     x_z = [slots(4) for _ in range(2)]
     first_e2 = slots(2)
     b_e2in = [slots(5) for _ in range(2)]
-    o_z = [slots(4) for _ in range(2)]
-    o_e2in = [slots(5) for _ in range(2)]
     c_e1, c_near = slots(COT_PARTS), slots(COT_PARTS)
 
     def one(first, count, layer, place):
@@ -160,19 +157,17 @@
         return wv.at[pl.ds(first, count), layer, pl.ds(2 * p, 2)]
 
     def span(way, hop, count):
-        if hop < 4:
-            return 0, count
-        return ((0, 2), (2, 1))[way] if count == 3 else (way, 1)
+        return (0, count) if hop < 4 else (way * count // 2, count // 2)
 
     def layer_from(way, hop):
         return (z + 8 - hop) % 8 if way == 0 else (z + hop) % 8
 
     mine = cols(b, hi, core, mp)
     halo_own = cols(0, hi, core, mp)
-    wires.put("weights", w_e1, ws.at[1 - q, 0:3], wv.at[0:3, z, x], info["e1"])
+    wires.put("weights", w_e1, ws.at[1 - q], wv.at[:, z, x], info["e1"])
     wires.put("hidden", h_e1, hid, mine, info["e1"])
-    own_rows_w = ws.at[q, 0:3]
-    own_place = wv.at[0:3, z, x]
+    own_rows_w = ws.at[q]
+    own_place = wv.at[:, z, x]
     for way in range(2):
         wires.put("weights", w_z[0][way][0], own_rows_w, own_place, info[ways[way]])
     wires.put("weights", first_e2[0], own_rows_w, own_place, info["e2"])
@@ -197,7 +192,6 @@
         wires.put("hidden", h_far[r], src, dst, info["far"])
 
     spread(0)
-    wires.put("weights", o_e1, ws.at[1 - q, O], wv.at[O, z, x], info["e1"])
 
     def half_cols(block, head_hi, head_core):
         start = pl.multiple_of((head_hi * 2 + head_core) * 512, 512)
@@ -269,7 +263,7 @@
         wires.got(c_near[k], c_rows(1 - odd, 1 - mp, k))
 
     def second():
-        ref = wv.at[0:3, z, mate]
+        ref = wv.at[:, z, mate]
         wires.got(w_e1, ref)
         wires.put("weights", first_e2[1], ref, ref, info["e2"])
         for way in range(2):
@@ -278,37 +272,20 @@
     def w_hop(hop, way, member):
         place = (x, mate)[member]
         layer = layer_from(way, hop)
-        lo, count = span(way, hop, 3)
+        lo, count = span(way, hop, 4)
         wires.got(w_z[member][way][hop - 1], one(lo, count, layer, place))
         if hop < 4:
-            lo, count = span(way, hop + 1, 3)
+            lo, count = span(way, hop + 1, 4)
             on = one(lo, count, layer, place)
             wires.put("weights", w_z[member][way][hop], on, on, info[ways[way]])
         if member == 1 and (hop < 4 or way == 1):
-            ref = own_pair(K, 1, layer)
+            ref = own_pair(2, 2, layer)
             wires.put("weights", b_e2in[way][hop], ref, ref, info["e2"])
-
-    def o_second():
-        wires.got(o_e1, wv.at[O, z, mate])
-        ref = own_pair(O, 1, z)
-        for way in range(2):
-            wires.put("weights", o_z[way][0], ref, ref, info[ways[way]])
-        wires.put("weights", o_e2in[0][0], ref, ref, info["e2"])
-
-    def o_hop(hop, way):
-        ref = own_pair(O, 1, layer_from(way, hop))
-        wires.got(o_z[way][hop - 1], ref)
-        if hop < 3 or (hop == 3 and way == 1):
-            wires.put("weights", o_z[way][hop], ref, ref, info[ways[way]])
-        wires.put("weights", o_e2in[way][hop], ref, ref, info["e2"])
-
-    def o_got(hop, way):
-        wires.got(o_e2in[way][hop], other_pair(O, 1, layer_from(way, hop)))
 
     def x_hop(hop, way):
         if hop == 0:
-            wires.got(first_e2[0], wv.at[0:3, z, 3 - x])
-            wires.got(first_e2[1], wv.at[0:3, z, 3 - mate])
+            wires.got(first_e2[0], wv.at[:, z, 3 - x])
+            wires.got(first_e2[1], wv.at[:, z, 3 - mate])
             ref = other_pair(0, 2, z)
             for each in range(2):
                 wires.put("weights", x_z[each][0], ref, ref, info[ways[each]])
@@ -322,7 +299,7 @@
             wires.put("weights", x_z[way][hop], on, on, info[ways[way]])
 
     def e2_got(hop, way):
-        wires.got(b_e2in[way][hop], other_pair(K, 1, layer_from(way, hop)))
+        wires.got(b_e2in[way][hop], other_pair(2, 2, layer_from(way, hop)))
 
     def project(hop, r):
         here = pl.ds(pl.multiple_of(order[r] * 384, 384), 384)
@@ -380,17 +357,10 @@
             [jnp.where(lane_head == h, rows, jnp.zeros_like(rows)) for h in range(4)], axis=0
         )
 
-    def gather_heads(rows, weights):
-        parts = []
-        for pair in range(2):
-            wide = lax.dot_general(
-                rows[:, pair * 128 : (pair + 1) * 128],
-                weights[:, pair * 256 : (pair + 1) * 256],
-                TN,
-                preferred_element_type=F32,
-            )
-            parts += [wide[0:HD, 0:128], wide[HD : 2 * HD, 128:256]]
-        return jnp.concatenate(parts, axis=0).T
+    def fold(wide):
+        return jnp.concatenate(
+            [wide[h * HD : (h + 1) * HD, h * 128 : (h + 1) * 128] for h in range(4)], axis=0
+        ).T
 
     key_at = lax.broadcasted_iota(jnp.int32, (512, 128), 0)
     query_at = lax.broadcasted_iota(jnp.int32, (512, 128), 1) + 384
@@ -415,19 +385,18 @@
         rows = expo * (1.0 / jnp.sum(expo, axis=0, keepdims=True))
         prob_rows = rows.astype(BF)
         probs[t] = prob_rows
-        attn[here, :] = gather_heads(values, prob_rows).astype(BF)
+        attn[here, :] = fold(
+            lax.dot_general(values, prob_rows, TN, preferred_element_type=F32)
+        ).astype(BF)
         return carry
 
-    def unrolled(step, low_tile, high_tile):
-        def all_of_them(i, carry):
-            for t in range(low_tile, high_tile):
-                step(i + t, carry)
+    def tiles_front(low_tile, high_tile):
+        def pair(i, carry):
+            tile_front(low_tile + 2 * i, 0)
+            tile_front(low_tile + 2 * i + 1, 0)
             return carry
 
-        lax.fori_loop(0, 1, all_of_them, 0)
-
-    def tiles_front(low_tile, high_tile):
-        unrolled(tile_front, low_tile, high_tile)
+        lax.fori_loop(0, (high_tile - low_tile) // 2, pair, 0)
 
     def tiles_value():
         def value_step(t, carry):
@@ -437,7 +406,7 @@
             )
             return carry
 
-        unrolled(value_step, 0, 6)
+        lax.fori_loop(0, 6, value_step, 0)
 
         def pack_values(i, carry):
             rows = pl.ds(pl.multiple_of(i * 128, 128), 128)
@@ -455,11 +424,21 @@
         delta = jnp.sum(rows * prob_grad, axis=0, keepdims=True)
         score_grad = (rows * (prob_grad - delta)).astype(BF)
         acc[1, window] += jnp.dot(score_grad, queries, preferred_element_type=F32)
-        dqkv[there, 0:256] = (gather_heads(keys, score_grad) * HD**-0.5).astype(BF)
+        dqkv[there, 0:256] = (
+            fold(lax.dot_general(keys, score_grad, TN, preferred_element_type=F32)) * HD**-0.5
+        ).astype(BF)
         return carry
 
     def tiles_back(low_tile, high_tile):
-        unrolled(tile_step, low_tile, high_tile)
+        def pair(i, carry):
+            tile_step(low_tile + 2 * i, 0)
+            tile_step(low_tile + 2 * i + 1, 0)
+            return carry
+
+        pairs = (high_tile - low_tile) // 2
+        lax.fori_loop(0, pairs, pair, 0)
+        if high_tile - low_tile > 2 * pairs:
+            lax.fori_loop(high_tile - 1, high_tile, tile_step, 0)
 
     def pack():
         def step(i, carry):
@@ -480,102 +459,86 @@
     w_hop(1, 0, 0)
     second()
     from_near(0)
+    w_hop(2, 0, 0)
     w_hop(2, 1, 0)
-    w_hop(2, 0, 0)
+    spread(1)
+    w_hop(1, 0, 1)
+    w_hop(1, 1, 1)
     x_hop(0, 0)
-    spread(1)
-    w_hop(1, 1, 1)
-    o_second()
-    w_hop(3, 1, 0)
-    w_hop(3, 0, 0)
-    from_far(0)
-    w_hop(1, 0, 1)
     halo_on()
     from_near(1)
+    e2_got(1, 0)
+    c_send(5)
+    w_hop(2, 0, 1)
+    w_hop(3, 1, 0)
+    from_far(0)
+    c_send(1)
+    spread(2)
+    c_send(3)
+    c_send(2)
+    c_on(0)
     w_hop(2, 1, 1)
-    c_send(2)
-    e2_got(1, 0)
-    o_got(0, 0)
     e2_got(1, 1)
-    c_send(3)
+    c_send(4)
     x_hop(1, 0)
+    w_hop(3, 0, 0)
+    x_hop(1, 1)
+    from_twin(0)
+    c_on(5)
+    w_hop(3, 0, 1)
+    e2_got(2, 0)
+    w_hop(4, 1, 0)
+    project(0, 0)
+    from_far(1)
+    w_hop(3, 1, 1)
+    project(1, 0)
+    x_hop(2, 0)
+    e2_got(2, 1)
+    from_near(2)
+    from_twin(1)
+    x_hop(2, 1)
     w_hop(4, 0, 0)
-    spread(2)
-    o_hop(1, 1)
-    o_hop(1, 0)
-    w_hop(2, 0, 1)
-    w_hop(4, 1, 0)
-    c_send(5)
-    from_twin(0)
-    x_hop(1, 1)
-    project(0, 0)
-    c_send(4)
-    e2_got(2, 1)
-    c_send(1)
-    w_hop(3, 1, 1)
+    project(0, 1)
+    c_got(0)
+    c_on(3)
+    c_on(1)
+    w_hop(4, 1, 1)
+    project(2, 1)
+    e2_got(3, 0)
+    w_hop(4, 0, 1)
+    project(2, 0)
+    project(1, 1)
+    c_got(5)
     c_on(2)
-    o_hop(2, 1)
-    from_far(1)
-    project(1, 0)
-    o_got(1, 1)
-    x_hop(2, 0)
-    o_hop(2, 0)
-    from_near(2)
-    c_on(3)
-    o_got(1, 0)
-    c_on(0)
-    e2_got(2, 0)
-    x_hop(2, 1)
-    w_hop(3, 0, 1)
-    project(2, 0)
-    w_hop(4, 1, 1)
+    x_hop(3, 0)
+    from_far(2)
     e2_got(3, 1)
-    from_twin(1)
-    project(0, 1)
-    o_got(2, 1)
-    x_hop(3, 0)
-    o_hop(3, 1)
-    c_on(5)
-    project(2, 1)
-    project(1, 1)
+    x_hop(3, 1)
+    project(3, 0)
+    project(3, 1)
+    e2_got(4, 1)
     c_got(3)
-    o_hop(3, 0)
-    e2_got(3, 0)
-    x_hop(3, 1)
     c_on(4)
-    o_got(2, 0)
-    project(3, 1)
-    from_far(2)
-    project(3, 0)
-    w_hop(4, 0, 1)
-    e2_got(4, 1)
-    c_got(0)
-    o_got(3, 1)
-    c_on(1)
-    o_hop(4, 1)
+    from_twin(2)
     x_hop(4, 0)
     x_hop(4, 1)
+    c_got(1)
+    project(4, 0)
     project(4, 1)
-    from_twin(2)
-    project(4, 0)
     project(0, 2)
-    c_got(5)
-    o_got(4, 1)
-    o_got(3, 0)
-    project(1, 2)
-    project(3, 2)
     project(2, 2)
     project(4, 2)
-    c_got(4)
+    project(3, 2)
+    c_got(2)
+    project(1, 2)
     extract()
     own_c.wait()
     grad_block(odd)
     tiles_front(0, 2)
-    c_got(1)
-    c_got(2)
+    c_got(4)
+    grad_block(1 - odd)
     tiles_front(2, 4)
     tiles_front(4, 6)
-    grad_block(1 - odd)
     tiles_value()
 
     a_slot, b_slot = ([[slots(4) for _ in range(2)] for _ in range(2)] for _ in range(2))
@@ -628,7 +591,7 @@
             k = 0 if left == 4 else 7 - 2 * left + way
             wires.put("grads",
                 b_e2[k][m],
-                grads.at[CROSSING[m], to_layer(way, left), pl.ds(2 - 2 * p, 2)],
+                grads.at[2 + m, to_layer(way, left), pl.ds(2 - 2 * p, 2)],
                 b_e2got.at[k, m],
                 info["e2"],
             )
@@ -751,7 +714,7 @@
 
     def b_start(way, left, k, m):
         wires.got(b_e2[k][m], b_e2got.at[k, m])
-        return add(grads[CROSSING[m], to_layer(way, left), pl.ds(2 * p, 2)], b_e2got[k, m])
+        return add(grads[2 + m, to_layer(way, left), pl.ds(2 * p, 2)], b_e2got[k, m])
 
     def b_begin(m):
         b_e2got[0, m] = b_start(m, 4, 0, m)
@@ -782,8 +745,8 @@
         last = b_start(0, 0, 7, m)
         for way in range(2):
             wires.got(b_slot[m][way][3], b_got.at[way, 3, m])
-        w_pair[CROSSING[m]] = add(last, b_got[0, 3, m], b_got[1, 3, m])
-        swap(CROSSING[m], m, 1)
+        w_pair[2 + m] = add(last, b_got[0, 3, m], b_got[1, 3, m])
+        swap(2 + m, m, 1)
 
     def a_end(m):
         wires.got(a_e2[m], a_e2got.at[m])
@@ -793,7 +756,7 @@
     def w_end():
         for kind in range(2):
             for m in range(2):
-                wires.got(r_e1[kind][m], w_res.at[1 - q, (m, CROSSING[m])[kind]])
+                wires.got(r_e1[kind][m], w_res.at[1 - q, 2 * kind + m])
         for half in range(2):
             lanes = slice(half * 256, half * 256 + 256)
             for s in range(3):
@@ -815,70 +778,71 @@
             pltpu.make_async_copy(t_halo, t_halo, send.at[len(GROUPS)]).wait()
 
     early_part(4)
+    tiles_back(0, 1)
     early_part(3)
     a_step(1, 1, 0)
-    tiles_back(0, 4)
+    tiles_back(1, 4)
+    b_begin(0)
+    tiles_back(4, 6)
+    b_step(1, 1, 0)
     a_step(0, 1, 0)
-    tiles_back(4, 6)
     pack()
+    late_part(4)
+    b_step(0, 1, 0)
     hsettle()
-    late_part(4)
-    b_step(1, 1, 0)
+    state_grads(0)
+    b_begin(1)
     late_part(3)
-    state_grads(0)
-    b_begin(0)
     a_step(0, 1, 1)
+    state_grads(1)
+    a_step(1, 1, 1)
+    fold_twin(0)
+    b_step(0, 1, 1)
     early_part(2)
-    a_step(1, 1, 1)
-    state_grads(1)
-    fold_twin(0)
     a_step(0, 2, 0)
     a_step(1, 2, 0)
+    fold_twin(1)
     late_part(2)
-    b_step(0, 1, 0)
-    b_begin(1)
-    b_step(0, 1, 1)
     a_step(0, 2, 1)
-    fold_twin(1)
     a_step(1, 2, 1)
+    state_grads(2)
+    fold_far(0)
+    b_step(1, 2, 0)
+    fold_near(0)
     early_part(1)
+    a_step(1, 3, 0)
+    b_step(0, 2, 1)
     a_step(0, 3, 0)
-    a_step(1, 3, 0)
+    b_step(1, 1, 1)
+    fold_far(1)
     late_part(1)
-    fold_far(0)
+    fold_near(1)
+    a_step(1, 3, 1)
+    fold_second(0)
+    a_step(0, 3, 1)
     b_step(0, 2, 0)
-    b_step(1, 1, 1)
-    fold_near(0)
-    state_grads(2)
-    a_step(1, 3, 1)
-    a_step(0, 3, 1)
-    b_step(0, 2, 1)
-    wsettle()
-    fold_near(1)
-    fold_far(1)
-    b_step(1, 2, 0)
-    fold_second(0)
+    late_part(0)
+    fold_twin(2)
+    b_step(1, 2, 1)
     early_part(0)
-    fold_twin(2)
-    late_part(0)
-    b_step(1, 2, 1)
+    b_step(0, 3, 1)
+    b_step(1, 3, 0)
+    fold_second(1)
     a_finish(0)
+    a_finish(1)
+    b_step(1, 3, 1)
     b_step(0, 3, 0)
-    fold_second(1)
-    a_finish(1)
-    b_step(1, 3, 0)
     halo_pass()
-    b_step(0, 3, 1)
-    b_step(1, 3, 1)
+    a_end(0)
+    fold_near(2)
     fold_far(2)
-    fold_near(2)
-    a_end(0)
-    b_finish(0)
     a_end(1)
     b_finish(1)
+    b_finish(0)
+    wsettle()
     fold_second(2)
+    w_end()
     t_end()
-    w_end()
     wires.settle("grads", nv)
     wires.settle("trunk", nv)
 

time: 110 us -> 108 us (0.982)
  Pallas kernels: 109 us -> 106 us
    pallas_call x1, Pallas kernels: 107 us -> 105 us  [per_device(): pl.pallas_call(kernel, out_shape=(jax.ShapeDtypeStruct((384, 256), BF), j...]
where the time goes in v6:
time: 108 us; the launch traced here: 107 us
  Pallas kernels  106 us (98%)
    pallas_call x1, Pallas kernels, per_device(): pl.pallas_call(kernel, out_shape=(jax.ShapeDtypeStruct((384, 256), BF), j...  105 us

profile of v6, /device:TPU:4, one launch (start us, length us, event | category | flops | bytes accessed | tf_op | source)
XLA Modules:
  0.0 107.0 jit_solution(12326143618138301689)
XLA Ops:
  0.6 104.6 %whole.1 = (bf16[384,256]{1,0:T(8,128)(2,1)}, bf16[1,3,64,512]{3,2,1,0:T(8,128)(2,1)}, bf16[1,64,512]{2,1,0:T(8,128)(2,1)}) custom-call(bf16[384,256]{1,0:T(8,128)(2,1)} %hid.1, bf16[1,3,64,512]{3,2,1,0:T(8,128)(2,1)} %bitcast.3, bf16[1,64,512]{2,1,0:T(8,128)(2,1)} %wo.1, bf16[1,384,2048]{2,1,0:T(8,128)(2,1)} %cot.1, bf16[1,2048]{1,0:T(2,128)(2,1)} %gain.1, ...), custom_call_target="tpu_custom_call" | custom-call | tf_op jit(solution)/shard_map/whole/pallas_call | solution.py:876
  105.2 1.8 %hand_over.1 = (bf16[384,256]{1,0:T(8,128)(2,1)}, bf16[1,3,64,512]{3,2,1,0:T(8,128)(2,1)}, bf16[1,64,512]{2,1,0:T(8,128)(2,1)}) custom-call(bf16[384,256]{1,0:T(8,128)(2,1)} %get-tuple-element.9.a_ref, bf16[1,3,64,512]{3,2,1,0:T(8,128)(2,1)} %get-tuple-element.10.b_ref, bf16[1,64,512]{2,1,0:T(8,128)(2,1)} %get-tuple-element.11.c_ref), custom_call_target="tpu_custom_call" | custom-call | tf_op jit(solution)/shard_map/hand_over/pallas_call | solution.py:907

commit v7 on v6

--- a/solution.py
+++ b/solution.py
@@ -357,10 +357,17 @@
             [jnp.where(lane_head == h, rows, jnp.zeros_like(rows)) for h in range(4)], axis=0
         )
 
-    def fold(wide):
-        return jnp.concatenate(
-            [wide[h * HD : (h + 1) * HD, h * 128 : (h + 1) * 128] for h in range(4)], axis=0
-        ).T
+    def gather_heads(rows, weights):
+        parts = []
+        for pair in range(2):
+            wide = lax.dot_general(
+                rows[:, pair * 128 : (pair + 1) * 128],
+                weights[:, pair * 256 : (pair + 1) * 256],
+                TN,
+                preferred_element_type=F32,
+            )
+            parts += [wide[0:HD, 0:128], wide[HD : 2 * HD, 128:256]]
+        return jnp.concatenate(parts, axis=0).T
 
     key_at = lax.broadcasted_iota(jnp.int32, (512, 128), 0)
     query_at = lax.broadcasted_iota(jnp.int32, (512, 128), 1) + 384
@@ -385,9 +392,7 @@
         rows = expo * (1.0 / jnp.sum(expo, axis=0, keepdims=True))
         prob_rows = rows.astype(BF)
         probs[t] = prob_rows
-        attn[here, :] = fold(
-            lax.dot_general(values, prob_rows, TN, preferred_element_type=F32)
-        ).astype(BF)
+        attn[here, :] = gather_heads(values, prob_rows).astype(BF)
         return carry
 
     def tiles_front(low_tile, high_tile):
@@ -406,7 +411,12 @@
             )
             return carry
 
-        lax.fori_loop(0, 6, value_step, 0)
+        def values_three(i, carry):
+            for t in range(3):
+                value_step(3 * i + t, carry)
+            return carry
+
+        lax.fori_loop(0, 2, values_three, 0)
 
         def pack_values(i, carry):
             rows = pl.ds(pl.multiple_of(i * 128, 128), 128)
@@ -424,9 +434,7 @@
         delta = jnp.sum(rows * prob_grad, axis=0, keepdims=True)
         score_grad = (rows * (prob_grad - delta)).astype(BF)
         acc[1, window] += jnp.dot(score_grad, queries, preferred_element_type=F32)
-        dqkv[there, 0:256] = (
-            fold(lax.dot_general(keys, score_grad, TN, preferred_element_type=F32)) * HD**-0.5
-        ).astype(BF)
+        dqkv[there, 0:256] = (gather_heads(keys, score_grad) * HD**-0.5).astype(BF)
         return carry
 
     def tiles_back(low_tile, high_tile):

time: 108 us -> 107 us (level)
  no operation moved by 1% of the time
where the time goes in v7:
time: 107 us; the launch traced here: 106 us
  Pallas kernels  105 us (98%)
    pallas_call x1, Pallas kernels, per_device(): pl.pallas_call(kernel, out_shape=(jax.ShapeDtypeStruct((384, 256), BF), j...  104 us

profile of v7, /device:TPU:4, one launch (start us, length us, event | category | flops | bytes accessed | tf_op | source)
XLA Modules:
  0.0 106.1 jit_solution(4399733264210399517)
XLA Ops:
  0.6 103.7 %whole.1 = (bf16[384,256]{1,0:T(8,128)(2,1)}, bf16[1,3,64,512]{3,2,1,0:T(8,128)(2,1)}, bf16[1,64,512]{2,1,0:T(8,128)(2,1)}) custom-call(bf16[384,256]{1,0:T(8,128)(2,1)} %hid.1, bf16[1,3,64,512]{3,2,1,0:T(8,128)(2,1)} %bitcast.3, bf16[1,64,512]{2,1,0:T(8,128)(2,1)} %wo.1, bf16[1,384,2048]{2,1,0:T(8,128)(2,1)} %cot.1, bf16[1,2048]{1,0:T(2,128)(2,1)} %gain.1, ...), custom_call_target="tpu_custom_call" | custom-call | tf_op jit(solution)/shard_map/whole/pallas_call | solution.py:884
  104.3 1.8 %hand_over.1 = (bf16[384,256]{1,0:T(8,128)(2,1)}, bf16[1,3,64,512]{3,2,1,0:T(8,128)(2,1)}, bf16[1,64,512]{2,1,0:T(8,128)(2,1)}) custom-call(bf16[384,256]{1,0:T(8,128)(2,1)} %get-tuple-element.9.a_ref, bf16[1,3,64,512]{3,2,1,0:T(8,128)(2,1)} %get-tuple-element.10.b_ref, bf16[1,64,512]{2,1,0:T(8,128)(2,1)} %get-tuple-element.11.c_ref), custom_call_target="tpu_custom_call" | custom-call | tf_op jit(solution)/shard_map/hand_over/pallas_call | solution.py:915
